TPU v7x, 128 devices: a whole 4x4x4 slice. The times are simulated.
128 devices in a mesh: member: 4 (over z_hi, core), space: 32 (over y, x, z_lo).
Axes of the slice: x: 4, y: 4, z: 4 (z_hi: 2, z_lo: 2; z = z_hi * 2 + z_lo), core: 2. Of those that a mesh axis runs over, the one named last changes fastest.
Arguments:
- trajectory_outcomes: float32 [8, 96, 131072], P('member', None, 'space'), may hold values from -8 to 8
- verifying_analysis: float32 [96, 131072], P(None, 'space'), may hold values from -8 to 8
- latitude_surface_factor: float32 [131072], P('space'), may hold values from 0.5 to 6, as said below
- variable_penalty_factor: float32 [96], replicated, may hold values from 0.25 to 4
Outputs:
- derivative_by_trajectory: float32 [8, 96, 131072], P('member', None, 'space')
- field_loss: float32 [96], replicated
Inputs may be any that keep to these rules, and one draw needn't show every extreme that they name: `latitude_surface_factor`: positive area weights.
All inputs are finite; a program needn't handle non-finite values.
Results may differ from a plain program's by a relative error of at most 0.0003.
Values sent between devices are 32-bit elements; how exact they have to be, the bound alone decides.
No kernel may reach another device: no remote copies, remote signals or barrier semaphores. Data moves between devices by JAX's collectives and lax.ppermute only.
A program may use at most 128 MiB of HBM per device.

v0:
```python
import jax
import jax.numpy as jnp
from jax import lax
from jax.sharding import PartitionSpec as P


def shards(
    trajectory_outcomes, verifying_analysis, latitude_surface_factor, variable_penalty_factor
):
    trajectory_samples = trajectory_outcomes.shape[0] * lax.axis_size("member")
    total_points = latitude_surface_factor.shape[0] * lax.axis_size("space")
    pairwise_multiplier = (1.0 - 0.05 / trajectory_samples) / (
        trajectory_samples * (trajectory_samples - 1)
    )
    shard_contribution = lax.all_gather(trajectory_outcomes, "member", axis=0, tiled=True)
    running_sign_sum = jnp.zeros(trajectory_outcomes.shape, jnp.float32)
    dispersion_term = jnp.zeros(verifying_analysis.shape, jnp.float32)
    for realization_entries in range(shard_contribution.shape[0]):
        realization_gap = trajectory_outcomes - shard_contribution[realization_entries][None]
        running_sign_sum = running_sign_sum + jnp.sign(realization_gap)
        dispersion_term = dispersion_term + jnp.sum(jnp.abs(realization_gap), axis=0)
    running_sign_sum, dispersion_term = (running_sign_sum, dispersion_term)
    error_versus_truth = trajectory_outcomes - verifying_analysis[None]
    scaling_coefficient = (
        variable_penalty_factor[None, :, None] * latitude_surface_factor[None, None, :]
    )
    derivative_by_trajectory = scaling_coefficient * (
        jnp.sign(error_versus_truth) / trajectory_samples - pairwise_multiplier * running_sign_sum
    )
    per_node_score = (
        jnp.sum(jnp.abs(error_versus_truth), axis=0) / trajectory_samples
        - 0.5 * pairwise_multiplier * dispersion_term
    )
    partial_value = jnp.sum(per_node_score * latitude_surface_factor[None], axis=1)
    summed = lax.psum(partial_value, ("member", "space"))
    field_loss = variable_penalty_factor * summed / total_points
    return (derivative_by_trajectory, field_loss)


def solution(mesh):
    return jax.shard_map(
        shards,
        mesh=mesh,
        in_specs=(P("member", None, "space"), P(None, "space"), P("space"), P()),
        out_specs=(P("member", None, "space"), P()),
        check_vma=False,
    )
```

profile of v0, /device:TPU:1, one launch (start us, length us, event | category | flops | bytes accessed | tf_op | source)
XLA Modules:
  0.0 197.4 jit_solution(13747145537314920842)
XLA Ops:
  7.2 0.0 copy-start.2
  7.2 0.0 copy-start.1
  7.2 0.0 all-gather.2.cloned.1.call-start
  7.2 0.7 all-gather.2.cloned.1.call-update
  7.9 0.0 copy-done.2
  7.9 0.0 copy-done.1
  7.9 1.4 broadcast_multiply_fusion
  9.3 90.3 %all-gather.2.cloned.1.call-done = f32[8,96,4096]{2,1,0:T(8,128)} async-done(((f32[2,96,4096]{2,1,0:T(8,128)}), f32[8,96,4096]{2,1,0:T(8,128)}) %all-gather.2.cloned.1.call-update) | async-done | bytes 12582928 | tf_op jit(solution)/shard_map/all_gather | solution.py:15
  99.7 0.0 copy-start
  99.7 8.6 %slice_bitcast_fusion.7 = (f32[96,4096]{1,0:T(8,128)S(1)}, f32[96,4096]{1,0:T(8,128)S(1)}, f32[96,4096]{1,0:T(8,128)}, f32[96,4096]{1,0:T(8,128)}, f32[96,4096]{...) fusion(f32[8,96,4096]{2,1,0:T(8,128)} %all-gather.2.cloned.1.call-done), kind=kLoop, calls=%fused_computation.17 | loop fusion | bytes 25165824 | tf_op jit(solution)/shard_map/sub | solution.py:19
  108.3 0.0 copy-done
  108.3 15.7 %abs_reduce_fusion.8 = (f32[96,4096]{1,0:T(8,128)S(1)}, f32[96,4096]{1,0:T(8,128)S(1)}, f32[96,4096]{1,0:T(8,128)S(1)}, f32[96,4096]{1,0:T(8,128)S(1)}, f32[96,4...) fusion(f32[2,96,4096]{2,1,0:T(8,128)S(1)} %copy-done, ...), kind=kLoop, calls=%fused_computation.8 | loop fusion | flops 33423360 | bytes 36175872 | tf_op jit(solution)/shard_map/reduce_sum | solution.py:31
  124.0 1.4 multiply_reduce_fusion
  125.4 64.6 %psum.7 = f32[96]{0:T(128)S(1)} all-reduce(f32[96]{0:T(128)S(1)} %multiply_reduce_fusion), channel_id=1, replica_groups=mesh['member'=4,'space'=32] {'member','space'}, use_global_device_ids=true, to_apply=%region_10.0 | all-reduce | flops 96 | bytes 768 | tf_op jit(solution)/shard_map/psum | solution.py:35
  190.0 0.5 multiply_multiply_fusion
Async XLA Ops:
  7.2 0.8 copy-start.2
  7.2 0.8 copy-start.1
  7.2 92.5 %all-gather.2.cloned.1.call-start = ((), (), s32[]{:S(2)}) async-start(), calls=%async_computation | async-start | bytes 15728640 | tf_op jit(solution)/shard_map/all_gather | solution.py:15
  99.7 8.6 %copy-start = (f32[2,96,4096]{2,1,0:T(8,128)S(1)}, f32[2,96,4096]{2,1,0:T(8,128)}, u32[]{:S(2)}) copy-start(f32[2,96,4096]{2,1,0:T(8,128)} %param.4) | copy-start | bytes 9437188
Sparse Core Ops, SparseCore 0:
  9.7 89.9 all-gather.1
where the time goes:
time: 198 us; the launch traced here: 197 us
  waiting for transfers between devices  91 us (46%)
  blocking collectives  64.6 us (33%)
  other arithmetic  19.1 us (10%)
  between operations  14.1 us (7%)
  local copies, waits for them, and re-layouts  8.65 us (4%)
    all_gather x1, waiting for transfers between devices, shards(): lax.all_gather(trajectory_outcomes, 'member', axis=0, tiled=True)  90.3 us
    psum x1, blocking collectives, shards(): summed = lax.psum(partial_value, ('member', 'space'))  64.6 us
    reduce_sum x1, other arithmetic, shards(): jnp.sum(jnp.abs(error_versus_truth), axis=0) / trajectory_samples  15.7 us
    sub x1, local copies, waits for them, and re-layouts, shards(): trajectory_outcomes - shard_contribution[realization_entries][None]  8.64 us
  transfers between devices with their start and end apart: 1, of which 1 were waited for; matrix products, arithmetic and copies ran while one was open for 1% of the time, Pallas kernels for 0%

commit v1 on v0

v1 whole, which is shorter than its diff:
```python
import functools

import jax
import jax.numpy as jnp
from jax import lax
from jax.experimental import pallas as pl
from jax.experimental.pallas import tpu as pltpu
from jax.sharding import PartitionSpec as P

AXES = ("member", "space")
CHUNKS = 2
LANES = 128
SUBLANES = 8


def exchange(block, flip):
    members, spaces = lax.axis_size("member"), lax.axis_size("space")
    pairs = [
        (m * spaces + s, (m ^ flip) * spaces + s) for m in range(members) for s in range(spaces)
    ]
    return lax.ppermute(block, AXES, pairs)


def score_kernel(scale, weight, own, near, far, cross, truth, lat, pen, d_own, d_near, d_far, d_cross, loss):
    rows, cols = truth.shape
    sources = (own, near, far, cross)
    targets = (d_own, d_near, d_far, d_cross)
    for row in range(0, rows, SUBLANES):
        r = pl.ds(row, SUBLANES)
        penalty = pen[r, :]

        def step(i, total):
            c = pl.ds(pl.multiple_of(i * LANES, LANES), LANES)
            x = [ref[k, r, c] for ref in sources for k in range(2)]
            n = len(x)
            y = truth[r, c]
            area = jnp.broadcast_to(lat[:, c], (SUBLANES, LANES))
            signs = [None] * n
            for a in range(n):
                for b in range(a + 1, n):
                    s = jnp.where(x[a] > x[b], 1.0, jnp.where(x[a] < x[b], -1.0, 0.0))
                    signs[a] = s if signs[a] is None else signs[a] + s
                    signs[b] = -s if signs[b] is None else signs[b] - s
            factor = penalty * area
            score = jnp.zeros_like(y)
            for j in range(n):
                e = x[j] - y
                g = jnp.where(e > 0.0, weight, jnp.where(e < 0.0, -weight, 0.0)) - scale * signs[j]
                score = score + e * g
                targets[j // 2][j % 2, r, c] = factor * g
            return total + area * score

        total = lax.fori_loop(0, cols // LANES, step, jnp.zeros((SUBLANES, LANES), jnp.float32), unroll=2)
        loss[r, :] = total


def shards(x, y, lat, pen):
    members = lax.axis_size("member")
    spaces = lax.axis_size("space")
    samples = x.shape[0] * members
    fields, points = y.shape
    scale = (1.0 - 0.05 / samples) / (samples * (samples - 1))
    quarter = fields // members
    width = points // CHUNKS
    me = lax.axis_index("member")

    def part(array, flip, chunk):
        start = ((me ^ flip) * quarter, chunk * width)
        size = (quarter, width)
        if array.ndim == 3:
            start, size = (0,) + start, (array.shape[0],) + size
        return lax.dynamic_slice(array, start, size)

    got = [{f: exchange(part(x, f, c), f) for f in (2, 3, 1)} for c in range(CHUNKS)]
    pen_own = lax.dynamic_slice(pen, (me * quarter,), (quarter,))
    pen_own = jnp.broadcast_to(pen_own[:, None], (quarter, LANES))
    block = jax.ShapeDtypeStruct((x.shape[0], quarter, width), jnp.float32)
    vmem = pl.BlockSpec(memory_space=pltpu.VMEM)
    call = pl.pallas_call(
        functools.partial(score_kernel, scale, 1.0 / samples),
        out_shape=[block] * 4 + [jax.ShapeDtypeStruct((quarter, LANES), jnp.float32)],
        in_specs=[vmem] * 7,
        out_specs=[vmem] * 5,
        compiler_params=pltpu.CompilerParams(vmem_limit_bytes=32 * 1024 * 1024),
        cost_estimate=pl.CostEstimate(
            flops=300 * quarter * width, bytes_accessed=20 * quarter * width * 4, transcendentals=0
        ),
    )
    pieces = []
    loss = 0.0
    for c in range(CHUNKS):
        d_own, d_near, d_far, d_cross, part_loss = call(
            part(x, 0, c), got[c][1], got[c][2], got[c][3], part(y, 0, c),
            lat[None, c * width:(c + 1) * width], pen_own,
        )
        loss = loss + part_loss
        pieces.append({0: d_own, 2: exchange(d_far, 2), 3: exchange(d_cross, 3), 1: exchange(d_near, 1)})
    sums = jnp.sum(loss, axis=1)[None, :]
    devices = members * spaces
    everyone = lax.all_to_all(jnp.broadcast_to(sums[None], (devices,) + sums.shape), AXES, 0, 0)
    total = jnp.sum(everyone.reshape(members, spaces, quarter), axis=1).reshape(fields)
    field_loss = pen * total / (points * spaces)
    out = jnp.zeros(x.shape, jnp.float32)
    for c in range(CHUNKS):
        for f in (0, 1, 2, 3):
            out = lax.dynamic_update_slice(out, pieces[c][f], (0, (me ^ f) * quarter, c * width))
    return out, field_loss


def solution(mesh):
    return jax.shard_map(
        shards,
        mesh=mesh,
        in_specs=(P("member", None, "space"), P(None, "space"), P("space"), P()),
        out_specs=(P("member", None, "space"), P()),
        check_vma=False,
    )
```

time: 198 us -> 81.1 us (0.41)
  blocking collectives: 64.6 us -> 0 us
  waiting for transfers between devices: 91 us -> 26.4 us
  starting transfers between devices: 0.04 us -> 32.4 us
  other arithmetic: 19.1 us -> 1.49 us
  between operations: 14.1 us -> 0.73 us
  local copies, waits for them, and re-layouts: 8.65 us -> 16.2 us
  Pallas kernels: 0 us -> 3.5 us
    all_gather x1 -> x0, waiting for transfers between devices: 90.3 us -> none  [shards(): lax.all_gather(trajectory_outcomes, 'member', axis=0, tiled=True)]
    psum x1 -> x0, blocking collectives: 64.6 us -> none  [shards(): summed = lax.psum(partial_value, ('member', 'space'))]
    ppermute x0 -> x12, waiting for transfers between devices: none -> 23.2 us  [exchange(): return lax.ppermute(block, AXES, pairs)]
    ppermute x0 -> x12, starting transfers between devices: none -> 21.4 us  [exchange(): return lax.ppermute(block, AXES, pairs)]
    reduce_sum x2, other arithmetic: 17.1 us -> 0.97 us  [the longest x1 0.86 us: shards(): jnp.sum(everyone.reshape(members, spaces, quarter), axis=1).reshape(fields)]
    all_to_all x0 -> x1, starting transfers between devices: none -> 11 us  [shards(): lax.all_to_all(jnp.broadcast_to(sums[None], (devices,) + sums.shape), AXE...]
    dynamic_update_slice x0 -> x8, local copies, waits for them, and re-layouts: none -> 10.1 us  [shards(): lax.dynamic_update_slice(out, pieces[c][f], (0, (me ^ f) * quarter, c * w...]
    sub x1 -> x0, local copies, waits for them, and re-layouts: 8.64 us -> none  [shards(): trajectory_outcomes - shard_contribution[realization_entries][None]]
  transfers between devices with their start and end apart: 1 -> 13, of which waited for: 1 -> 5; matrix products, arithmetic and copies ran while one was open for 1% -> 18% of each run, Pallas kernels for 0% -> 4%
where the time goes in v1:
time: 81.1 us; the launch traced here: 80.7 us
  starting transfers between devices  32.4 us (40%)
  waiting for transfers between devices  26.4 us (33%)
  local copies, waits for them, and re-layouts  16.2 us (20%)
  Pallas kernels  3.5 us (4%)
  other arithmetic  1.49 us (2%)
    ppermute x12, waiting for transfers between devices, exchange(): return lax.ppermute(block, AXES, pairs)  23.2 us
    ppermute x12, starting transfers between devices, exchange(): return lax.ppermute(block, AXES, pairs)  21.4 us
    all_to_all x1, starting transfers between devices, shards(): lax.all_to_all(jnp.broadcast_to(sums[None], (devices,) + sums.shape), AXE...  11 us
    dynamic_update_slice x8, local copies, waits for them, and re-layouts, shards(): lax.dynamic_update_slice(out, pieces[c][f], (0, (me ^ f) * quarter, c * w...  10.1 us
    pallas_call x2, Pallas kernels, shards(): call(part(x, 0, c), got[c][1], got[c][2], got[c][3], part(y, 0, c), lat[N...  3.5 us
    all_to_all x1, waiting for transfers between devices, shards(): lax.all_to_all(jnp.broadcast_to(sums[None], (devices,) + sums.shape), AXE...  3.22 us
    dynamic_slice x2, local copies, waits for them, and re-layouts, part(): return lax.dynamic_slice(array, start, size)  3.16 us
    broadcast_in_dim x1, local copies, waits for them, and re-layouts, shards(): out = jnp.zeros(x.shape, jnp.float32)  2.02 us
  transfers between devices with their start and end apart: 13, of which 5 were waited for; matrix products, arithmetic and copies ran while one was open for 18% of the time, Pallas kernels for 4%

profile of v1, /device:TPU:1, one launch (start us, length us, event | category | flops | bytes accessed | tf_op | source)
XLA Modules:
  0.0 80.7 jit_solution(5587362897935100835)
XLA Ops:
  0.7 0.0 copy-start.1
  0.7 0.0 copy-start
  0.7 2.1 %constant_dynamic-slice_fusion = (f32[2,24,2048]{2,1,0:T(8,128)S(1)}, f32[2,24,2048]{2,1,0:T(8,128)S(1)}, f32[2,24,2048]{2,1,0:T(8,128)S(1)}, f32[2,24,2048]{2,1...) fusion(f32[2,96,4096]{2,1,0:T(8,128)} %param.4, ...), kind=kLoop, calls=%fused_computation.6 | loop fusion | bytes 6291472 | tf_op jit(solution)/shard_map/dynamic_slice | solution.py:72
  2.8 5.1 %collective-permute-start.2 = (f32[2,24,2048]{2,1,0:T(8,128)S(1)}, f32[2,24,2048]{2,1,0:T(8,128)S(1)}, u32[]{:S(2)}, u32[]{:S(2)}) collective-permute-start(f32[2,24,2048]{2,1,0:T(8,128)S(1)} %get-tuple-element.25), channel_id=1, source_target_pairs={{0,96},{1,97},{2,98},{3,99},{4,100},{5,101},{6,102},{7,103},{8,104... | collective-permute-start | bytes 1179656 | tf_op jit(solution)/shard_map/ppermute | solution.py:21
  7.9 0.1 collective-permute-start.8
  7.9 0.0 collective-permute-start.6
  8.0 3.3 %collective-permute-start.1 = (f32[2,24,2048]{2,1,0:T(8,128)S(1)}, f32[2,24,2048]{2,1,0:T(8,128)S(1)}, u32[]{:S(2)}, u32[]{:S(2)}) collective-permute-start(f32[2,24,2048]{2,1,0:T(8,128)S(1)} %get-tuple-element.26), channel_id=1, source_target_pairs={{0,64},{1,65},{2,66},{3,67},{4,68},{5,69},{6,70},{7,71},{8,72},{9,... | collective-permute-start | bytes 1179656 | tf_op jit(solution)/shard_map/ppermute | solution.py:21
  11.2 0.3 collective-permute-start
  11.5 0.0 copy-done.1
  11.5 0.1 dynamic_slice.38
  11.6 6.2 %collective-permute-done.2.cross = f32[2,24,2048]{2,1,0:T(8,128)S(1)} collective-permute-done((f32[2,24,2048]{2,1,0:T(8,128)S(1)}, f32[2,24,2048]{2,1,0:T(8,128)S(1)}, u32[]{:S(2)}, u32[]{:S(2)}) %collective-permute-start.2) | collective-permute-done | bytes 393248 | tf_op jit(solution)/shard_map/ppermute | solution.py:21
  17.8 2.7 %collective-permute-start.7 = (f32[2,24,2048]{2,1,0:T(8,128)S(1)}, f32[2,24,2048]{2,1,0:T(8,128)S(1)}, u32[]{:S(2)}, u32[]{:S(2)}) collective-permute-start(f32[2,24,2048]{2,1,0:T(8,128)S(1)} %get-tuple-element.29), channel_id=1, source_target_pairs={{0,64},{1,65},{2,66},{3,67},{4,68},{5,69},{6,70},{7,71},{8,72},{9,... | collective-permute-start | bytes 1179656 | tf_op jit(solution)/shard_map/ppermute | solution.py:21
  20.5 0.0 copy-done
  20.5 1.0 %constant_dynamic-slice_fusion.9 = (f32[24,2048]{1,0:T(8,128)S(1)}, f32[24,2048]{1,0:T(8,128)S(1)}) fusion(f32[96,4096]{1,0:T(8,128)} %param.5, s32[]{:T(128)S(6)} %select_n.8), kind=kLoop, calls=%fused_computation.19 | loop fusion | bytes 786436 | tf_op jit(solution)/shard_map/dynamic_slice | solution.py:72
  21.6 12.1 %collective-permute-done.1.far = f32[2,24,2048]{2,1,0:T(8,128)S(1)} collective-permute-done((f32[2,24,2048]{2,1,0:T(8,128)S(1)}, f32[2,24,2048]{2,1,0:T(8,128)S(1)}, u32[]{:S(2)}, u32[]{:S(2)}) %collective-permute-start.1) | collective-permute-done | bytes 393248 | tf_op jit(solution)/shard_map/ppermute | solution.py:21
  33.6 0.0 collective-permute-done.near
  33.6 0.1 broadcast_in_dim.22.pen
  33.7 1.8 %shard_map.59 = (f32[2,24,2048]{2,1,0:T(8,128)S(1)}, f32[2,24,2048]{2,1,0:T(8,128)S(1)}, f32[2,24,2048]{2,1,0:T(8,128)S(1)}, f32[2,24,2048]{2,1,0:T(8,128)S(1)}, f32[24,128]{1,0:T(8,128)S(1)}) custom-call(f32[2,24,2048]{2,1,0:T(8,128)S(1)} %get-tuple-element.28.own, f32[2,24,2048]{2,1,0:T(8,128)S(1)} %collective-permute-done.near, ...), custom_call_target="tpu_custom_call" | custom-call | flops 14745600 | bytes 3932160 | tf_op jit(solution)/shard_map/pallas_call | solution.py:92
  35.5 1.5 %collective-permute-start.3 = (f32[2,24,2048]{2,1,0:T(8,128)S(1)}, f32[2,24,2048]{2,1,0:T(8,128)}, u32[]{:S(2)}, u32[]{:S(2)}) collective-permute-start(f32[2,24,2048]{2,1,0:T(8,128)S(1)} %get-tuple-element.13), channel_id=1, source_target_pairs={{0,32},{1,33},{2,34},{3,35},{4,36},{5,37},{6,38},{7,39},{8,40},{9,... | collective-permute-start | bytes 1179656 | tf_op jit(solution)/shard_map/ppermute | solution.py:21
  37.0 2.7 %collective-permute-start.4 = (f32[2,24,2048]{2,1,0:T(8,128)S(1)}, f32[2,24,2048]{2,1,0:T(8,128)S(1)}, u32[]{:S(2)}, u32[]{:S(2)}) collective-permute-start(f32[2,24,2048]{2,1,0:T(8,128)S(1)} %get-tuple-element.14), channel_id=1, source_target_pairs={{0,64},{1,65},{2,66},{3,67},{4,68},{5,69},{6,70},{7,71},{8,72},{9,... | collective-permute-start | bytes 1179656 | tf_op jit(solution)/shard_map/ppermute | solution.py:21
  39.7 0.0 collective-permute-done.8.cross
  39.7 0.5 collective-permute-start.5
  40.2 0.0 collective-permute-done.6.near
  40.2 1.9 %collective-permute-done.7.far = f32[2,24,2048]{2,1,0:T(8,128)S(1)} collective-permute-done((f32[2,24,2048]{2,1,0:T(8,128)S(1)}, f32[2,24,2048]{2,1,0:T(8,128)S(1)}, u32[]{:S(2)}, u32[]{:S(2)}) %collective-permute-start.7) | collective-permute-done | bytes 393248 | tf_op jit(solution)/shard_map/ppermute | solution.py:21
  42.1 1.7 %shard_map.60 = (f32[2,24,2048]{2,1,0:T(8,128)S(1)}, f32[2,24,2048]{2,1,0:T(8,128)S(1)}, f32[2,24,2048]{2,1,0:T(8,128)S(1)}, f32[2,24,2048]{2,1,0:T(8,128)S(1)}, f32[24,128]{1,0:T(8,128)S(1)}) custom-call(f32[2,24,2048]{2,1,0:T(8,128)S(1)} %get-tuple-element.24.own, f32[2,24,2048]{2,1,0:T(8,128)S(1)} %collective-permute-done.6.near, ...), custom_call_target="tpu_custom_call" | custom-call | flops 14745600 | bytes 3932160 | tf_op jit(solution)/shard_map/pallas_call | solution.py:92
  43.8 0.1 add_reduce_fusion
  43.9 0.7 broadcast_in_dim.24
  44.6 11.0 %all-to-all-start = ((f32[128,1,24]{2,1,0:T(1,128)}), f32[128,1,24]{2,1,0:T(1,128)}, u32[]{:S(2)}, u32[]{:S(2)}) async-start(f32[128,1,24]{2,1,0:T(1,128)} %broadcast_in_dim.24), calls=%async_computation | async-start | bytes 131072 | tf_op jit(solution)/shard_map/all_to_all | solution.py:100
  55.6 1.2 %collective-permute-start.9 = (f32[2,24,2048]{2,1,0:T(8,128)S(1)}, f32[2,24,2048]{2,1,0:T(8,128)}, u32[]{:S(2)}, u32[]{:S(2)}) collective-permute-start(f32[2,24,2048]{2,1,0:T(8,128)S(1)} %get-tuple-element.17), channel_id=1, source_target_pairs={{0,32},{1,33},{2,34},{3,35},{4,36},{5,37},{6,38},{7,39},{8,40},{9,... | collective-permute-start | bytes 1179656 | tf_op jit(solution)/shard_map/ppermute | solution.py:21
  56.8 2.5 %collective-permute-start.10 = (f32[2,24,2048]{2,1,0:T(8,128)S(1)}, f32[2,24,2048]{2,1,0:T(8,128)}, u32[]{:S(2)}, u32[]{:S(2)}) collective-permute-start(f32[2,24,2048]{2,1,0:T(8,128)S(1)} %get-tuple-element.18), channel_id=1, source_target_pairs={{0,64},{1,65},{2,66},{3,67},{4,68},{5,69},{6,70},{7,71},{8,72},{9,... | collective-permute-start | bytes 1179656 | tf_op jit(solution)/shard_map/ppermute | solution.py:21
  59.3 2.0 %broadcast_in_dim.20 = f32[2,96,4096]{2,1,0:T(8,128)} broadcast(f32[]{:T(128)} %constant.11.clone.1), dimensions={} | broadcast | bytes 3145732 | tf_op jit(solution)/shard_map/broadcast_in_dim | solution.py:103
  61.3 0.8 constant_dynamic-update-slice_fusion.7
  62.1 3.2 %all-to-all-done = f32[128,1,24]{2,1,0:T(1,128)} async-done(((f32[128,1,24]{2,1,0:T(1,128)}), f32[128,1,24]{2,1,0:T(1,128)}, u32[]{:S(2)}, u32[]{:S(2)}) %all-to-all-start) | async-done | bytes 12320 | tf_op jit(solution)/shard_map/all_to_all | solution.py:100
  65.3 0.9 %bitcast_reduce_fusion = f32[4,24]{1,0:T(4,128)S(1)} fusion(f32[4,32,24]{2,1,0:T(8,128)} %bitcast.4), kind=kLoop, calls=%fused_computation | loop fusion | flops 2976 | bytes 12672 | tf_op jit(solution)/shard_map/reduce_sum | solution.py:101
  66.2 0.1 reshape.15
  66.3 0.5 multiply_multiply_fusion
  66.8 0.0 collective-permute-done.3
  66.8 1.5 %collective-permute-start.11 = (f32[2,24,2048]{2,1,0:T(8,128)S(1)}, f32[2,24,2048]{2,1,0:T(8,128)S(1)}, u32[]{:S(2)}, u32[]{:S(2)}) collective-permute-start(f32[2,24,2048]{2,1,0:T(8,128)S(1)} %get-tuple-element.19), channel_id=1, source_target_pairs={{0,96},{1,97},{2,98},{3,99},{4,100},{5,101},{6,102},{7,103},{8,104... | collective-permute-start | bytes 1179656 | tf_op jit(solution)/shard_map/ppermute | solution.py:21
  68.3 1.8 %constant_dynamic-update-slice_fusion.6 = f32[2,96,4096]{2,1,0:T(8,128)} fusion(f32[2,96,4096]{2,1,0:T(8,128)} %constant_dynamic-update-slice_fusion.7, f32[2,24,2048]{2,1,0:T(8,128)} %collective-permute-done.3, s32[]{:T(128)S(6)} %select_n.9), kind=kLoop, calls=%fused_computation.12 | loop fusion | bytes 786436 | tf_op jit(solution)/shard_map/dynamic_update_slice | solution.py:106
  70.1 0.0 collective-permute-done.4
  70.1 0.8 constant_dynamic-update-slice_fusion.5
  70.8 0.0 collective-permute-done.5
  70.8 1.8 %constant_dynamic-update-slice_fusion.4 = f32[2,96,4096]{2,1,0:T(8,128)} fusion(f32[2,96,4096]{2,1,0:T(8,128)} %constant_dynamic-update-slice_fusion.5, f32[2,24,2048]{2,1,0:T(8,128)} %collective-permute-done.5, s32[]{:T(128)S(6)} %select_n.11), kind=kLoop, calls=%fused_computation.10 | loop fusion | bytes 786436 | tf_op jit(solution)/shard_map/dynamic_update_slice | solution.py:106
  72.6 0.8 constant_dynamic-update-slice_fusion.3
  73.4 0.0 collective-permute-done.9
  73.4 1.8 %constant_dynamic-update-slice_fusion.2 = f32[2,96,4096]{2,1,0:T(8,128)} fusion(f32[2,96,4096]{2,1,0:T(8,128)} %constant_dynamic-update-slice_fusion.3, f32[2,24,2048]{2,1,0:T(8,128)} %collective-permute-done.9, s32[]{:T(128)S(6)} %select_n.9), kind=kLoop, calls=%fused_computation.4 | loop fusion | bytes 786436 | tf_op jit(solution)/shard_map/dynamic_update_slice | solution.py:106
  75.2 0.0 collective-permute-done.10
  75.2 1.8 %constant_dynamic-update-slice_fusion.1 = f32[2,96,4096]{2,1,0:T(8,128)} fusion(f32[2,96,4096]{2,1,0:T(8,128)} %constant_dynamic-update-slice_fusion.2, f32[2,24,2048]{2,1,0:T(8,128)} %collective-permute-done.10, s32[]{:T(128)S(6)} %select_n.10), kind=kLoop, calls=%fused_computation.3 | loop fusion | bytes 786436 | tf_op jit(solution)/shard_map/dynamic_update_slice | solution.py:106
  76.9 3.0 %collective-permute-done.11 = f32[2,24,2048]{2,1,0:T(8,128)S(1)} collective-permute-done((f32[2,24,2048]{2,1,0:T(8,128)S(1)}, f32[2,24,2048]{2,1,0:T(8,128)S(1)}, u32[]{:S(2)}, u32[]{:S(2)}) %collective-permute-start.11) | collective-permute-done | bytes 393248 | tf_op jit(solution)/shard_map/ppermute | solution.py:21
  79.9 0.8 constant_dynamic-update-slice_fusion
  (1 shorter events, 0.0 us)
Async XLA Ops:
  0.7 10.9 %copy-start.1 = (f32[96]{0:T(128)S(1)}, f32[96]{0:T(128)}, u32[]{:S(2)}) copy-start(f32[96]{0:T(128)} %param.7) | copy-start | bytes 1156
  0.7 19.8 %copy-start = (f32[4096]{0:T(1024)S(1)}, f32[4096]{0:T(1024)}, u32[]{:S(2)}) copy-start(f32[4096]{0:T(1024)} %param.6) | copy-start | bytes 49156
  2.8 15.0 %collective-permute-start.2 = (f32[2,24,2048]{2,1,0:T(8,128)S(1)}, f32[2,24,2048]{2,1,0:T(8,128)S(1)}, u32[]{:S(2)}, u32[]{:S(2)}) collective-permute-start(f32[2,24,2048]{2,1,0:T(8,128)S(1)} %get-tuple-element.25), channel_id=1, source_target_pairs={{0,96},{1,97},{2,98},{3,99},{4,100},{5,101},{6,102},{7,103},{8,104... | collective-permute-start | bytes 1179656 | tf_op jit(solution)/shard_map/ppermute | solution.py:21
  7.9 31.8 %collective-permute-start.8 = (f32[2,24,2048]{2,1,0:T(8,128)S(1)}, f32[2,24,2048]{2,1,0:T(8,128)S(1)}, u32[]{:S(2)}, u32[]{:S(2)}) collective-permute-start(f32[2,24,2048]{2,1,0:T(8,128)S(1)} %get-tuple-element.22), channel_id=1, source_target_pairs={{0,96},{1,97},{2,98},{3,99},{4,100},{5,101},{6,102},{7,103},{8,104... | collective-permute-start | bytes 1179656 | tf_op jit(solution)/shard_map/ppermute | solution.py:21
  7.9 32.2 %collective-permute-start.6 = (f32[2,24,2048]{2,1,0:T(8,128)S(1)}, f32[2,24,2048]{2,1,0:T(8,128)S(1)}, u32[]{:S(2)}, u32[]{:S(2)}) collective-permute-start(f32[2,24,2048]{2,1,0:T(8,128)S(1)} %get-tuple-element.23), channel_id=1, source_target_pairs={{0,32},{1,33},{2,34},{3,35},{4,36},{5,37},{6,38},{7,39},{8,40},{9,... | collective-permute-start | bytes 1179656 | tf_op jit(solution)/shard_map/ppermute | solution.py:21
  8.0 25.7 %collective-permute-start.1 = (f32[2,24,2048]{2,1,0:T(8,128)S(1)}, f32[2,24,2048]{2,1,0:T(8,128)S(1)}, u32[]{:S(2)}, u32[]{:S(2)}) collective-permute-start(f32[2,24,2048]{2,1,0:T(8,128)S(1)} %get-tuple-element.26), channel_id=1, source_target_pairs={{0,64},{1,65},{2,66},{3,67},{4,68},{5,69},{6,70},{7,71},{8,72},{9,... | collective-permute-start | bytes 1179656 | tf_op jit(solution)/shard_map/ppermute | solution.py:21
  11.2 22.4 %collective-permute-start = (f32[2,24,2048]{2,1,0:T(8,128)S(1)}, f32[2,24,2048]{2,1,0:T(8,128)S(1)}, u32[]{:S(2)}, u32[]{:S(2)}) collective-permute-start(f32[2,24,2048]{2,1,0:T(8,128)S(1)} %get-tuple-element.27), channel_id=1, source_target_pairs={{0,32},{1,33},{2,34},{3,35},{4,36},{5,37},{6,38},{7,39},{8,40},{9,... | collective-permute-start | bytes 1179656 | tf_op jit(solution)/shard_map/ppermute | solution.py:21
  17.8 24.3 %collective-permute-start.7 = (f32[2,24,2048]{2,1,0:T(8,128)S(1)}, f32[2,24,2048]{2,1,0:T(8,128)S(1)}, u32[]{:S(2)}, u32[]{:S(2)}) collective-permute-start(f32[2,24,2048]{2,1,0:T(8,128)S(1)} %get-tuple-element.29), channel_id=1, source_target_pairs={{0,64},{1,65},{2,66},{3,67},{4,68},{5,69},{6,70},{7,71},{8,72},{9,... | collective-permute-start | bytes 1179656 | tf_op jit(solution)/shard_map/ppermute | solution.py:21
  35.5 31.3 %collective-permute-start.3 = (f32[2,24,2048]{2,1,0:T(8,128)S(1)}, f32[2,24,2048]{2,1,0:T(8,128)}, u32[]{:S(2)}, u32[]{:S(2)}) collective-permute-start(f32[2,24,2048]{2,1,0:T(8,128)S(1)} %get-tuple-element.13), channel_id=1, source_target_pairs={{0,32},{1,33},{2,34},{3,35},{4,36},{5,37},{6,38},{7,39},{8,40},{9,... | collective-permute-start | bytes 1179656 | tf_op jit(solution)/shard_map/ppermute | solution.py:21
  37.0 33.1 %collective-permute-start.4 = (f32[2,24,2048]{2,1,0:T(8,128)S(1)}, f32[2,24,2048]{2,1,0:T(8,128)S(1)}, u32[]{:S(2)}, u32[]{:S(2)}) collective-permute-start(f32[2,24,2048]{2,1,0:T(8,128)S(1)} %get-tuple-element.14), channel_id=1, source_target_pairs={{0,64},{1,65},{2,66},{3,67},{4,68},{5,69},{6,70},{7,71},{8,72},{9,... | collective-permute-start | bytes 1179656 | tf_op jit(solution)/shard_map/ppermute | solution.py:21
  39.7 31.2 %collective-permute-start.5 = (f32[2,24,2048]{2,1,0:T(8,128)S(1)}, f32[2,24,2048]{2,1,0:T(8,128)}, u32[]{:S(2)}, u32[]{:S(2)}) collective-permute-start(f32[2,24,2048]{2,1,0:T(8,128)S(1)} %get-tuple-element.15), channel_id=1, source_target_pairs={{0,96},{1,97},{2,98},{3,99},{4,100},{5,101},{6,102},{7,103},{8,104... | collective-permute-start | bytes 1179656 | tf_op jit(solution)/shard_map/ppermute | solution.py:21
  44.6 20.7 %all-to-all-start = ((f32[128,1,24]{2,1,0:T(1,128)}), f32[128,1,24]{2,1,0:T(1,128)}, u32[]{:S(2)}, u32[]{:S(2)}) async-start(f32[128,1,24]{2,1,0:T(1,128)} %broadcast_in_dim.24), calls=%async_computation | async-start | bytes 131072 | tf_op jit(solution)/shard_map/all_to_all | solution.py:100
  55.6 17.8 %collective-permute-start.9 = (f32[2,24,2048]{2,1,0:T(8,128)S(1)}, f32[2,24,2048]{2,1,0:T(8,128)}, u32[]{:S(2)}, u32[]{:S(2)}) collective-permute-start(f32[2,24,2048]{2,1,0:T(8,128)S(1)} %get-tuple-element.17), channel_id=1, source_target_pairs={{0,32},{1,33},{2,34},{3,35},{4,36},{5,37},{6,38},{7,39},{8,40},{9,... | collective-permute-start | bytes 1179656 | tf_op jit(solution)/shard_map/ppermute | solution.py:21
  56.8 18.4 %collective-permute-start.10 = (f32[2,24,2048]{2,1,0:T(8,128)S(1)}, f32[2,24,2048]{2,1,0:T(8,128)}, u32[]{:S(2)}, u32[]{:S(2)}) collective-permute-start(f32[2,24,2048]{2,1,0:T(8,128)S(1)} %get-tuple-element.18), channel_id=1, source_target_pairs={{0,64},{1,65},{2,66},{3,67},{4,68},{5,69},{6,70},{7,71},{8,72},{9,... | collective-permute-start | bytes 1179656 | tf_op jit(solution)/shard_map/ppermute | solution.py:21
  66.8 13.2 %collective-permute-start.11 = (f32[2,24,2048]{2,1,0:T(8,128)S(1)}, f32[2,24,2048]{2,1,0:T(8,128)S(1)}, u32[]{:S(2)}, u32[]{:S(2)}) collective-permute-start(f32[2,24,2048]{2,1,0:T(8,128)S(1)} %get-tuple-element.19), channel_id=1, source_target_pairs={{0,96},{1,97},{2,98},{3,99},{4,100},{5,101},{6,102},{7,103},{8,104... | collective-permute-start | bytes 1179656 | tf_op jit(solution)/shard_map/ppermute | solution.py:21

commit v2 on v1

v2 whole, which is shorter than its diff:
```python
import functools
import math

import jax
import jax.numpy as jnp
from jax import lax
from jax.experimental import pallas as pl
from jax.experimental.pallas import tpu as pltpu
from jax.sharding import PartitionSpec as P

AXES = ("member", "space")
SPLIT = 0.625
LANES = 128
SUBLANES = 8
NEAR, FAR, CROSS = 1, 2, 3
SMALL, LARGE = 4 * 2**20, 16 * 2**20
WORK, PLACING = 400_000, 40 * 10**9
VMEM = pl.BlockSpec(memory_space=pltpu.VMEM)
HBM = pl.BlockSpec(memory_space=pltpu.HBM)
ANY = pl.BlockSpec(memory_space=pl.ANY)


def exchange(block, flip):
    members, spaces = lax.axis_size("member"), lax.axis_size("space")
    pairs = [
        (m * spaces + s, (m ^ flip) * spaces + s) for m in range(members) for s in range(spaces)
    ]
    return lax.ppermute(block, AXES, pairs)


def window(ref, flip, quarter, start, width):
    row = pl.multiple_of((lax.axis_index("member") ^ flip) * quarter, SUBLANES)
    index = (pl.ds(row, quarter), pl.ds(start, width))
    return ref.at[(slice(None),) + index if len(ref.shape) == 3 else index]


def moved(shapes, flops=0):
    size = sum(4 * math.prod(s) for s in shapes)
    return pl.CostEstimate(flops=flops, bytes_accessed=2 * size, transcendentals=0)


def take_kernel(specs, quarter, n_arrays, n_deps, *refs):
    arrays, outs, sems = refs[:n_arrays], refs[n_arrays + n_deps:-1], refs[-1]
    copies = []
    for i, (which, flip, start, width) in enumerate(specs):
        source = window(arrays[which], flip, quarter, start, width)
        copies.append(pltpu.make_async_copy(source, outs[i], sems.at[i]))
    for copy in copies:
        copy.start()
    for copy in copies:
        copy.wait()


def take(specs, quarter, arrays, deps=()):
    shapes = [arrays[w].shape[:-2] + (quarter, width) for w, _, _, width in specs]
    return pl.pallas_call(
        functools.partial(take_kernel, specs, quarter, len(arrays), len(deps)),
        out_shape=[jax.ShapeDtypeStruct(s, jnp.float32) for s in shapes],
        in_specs=[HBM] * len(arrays) + [ANY] * len(deps),
        out_specs=[VMEM] * len(specs),
        scratch_shapes=[pltpu.SemaphoreType.DMA((len(specs),))],
        compiler_params=pltpu.CompilerParams(vmem_limit_bytes=SMALL),
        cost_estimate=moved(shapes),
    )(*[pltpu.with_memory_space_constraint(a, pltpu.HBM) for a in arrays], *deps)


def place_kernel(specs, quarter, job, n_more, *refs):
    pieces, more, outs, sems = refs[:len(specs)], refs[len(specs) + 1:][:n_more], refs[len(specs) + 1 + n_more:-1], refs[-1]
    copies = []
    for i, (flip, start, width) in enumerate(specs):
        copies.append(pltpu.make_async_copy(pieces[i], window(outs[0], flip, quarter, start, width), sems.at[i]))
    for copy in copies:
        copy.start()
    if job is not None:
        small = outs[2]
        job(*more, small)
        copies.append(pltpu.make_async_copy(small, outs[1], sems.at[len(specs)]))
        copies[-1].start()
    for copy in copies:
        copy.wait()


def place(specs, quarter, pieces, out, flops=0, job=None, more=(), shape=None):
    shapes = [out.shape] + ([shape] if job else [])
    return pl.pallas_call(
        functools.partial(place_kernel, specs, quarter, job, len(more)),
        out_shape=[jax.ShapeDtypeStruct(s, jnp.float32) for s in shapes],
        in_specs=[VMEM] * len(pieces) + [HBM] + [VMEM] * len(more),
        out_specs=[HBM] * len(shapes),
        scratch_shapes=[pltpu.VMEM(s, jnp.float32) for s in shapes[1:]] + [pltpu.SemaphoreType.DMA((len(specs) + 1,))],
        input_output_aliases={len(pieces): 0},
        compiler_params=pltpu.CompilerParams(vmem_limit_bytes=SMALL),
        cost_estimate=moved([p.shape for p in pieces], flops),
    )(*pieces, out, *more)


def add_rows(rows, total):
    total[...] = jnp.sum(rows[:, 0, :], axis=0, keepdims=True)


def weigh(count, pen, own, far, cross, near, loss):
    total = own[...] + far[...] + cross[...] + near[...]
    loss[...] = pen[...] * total[:, :pen.shape[1]] / count


def score_kernel(scale, weight, start, last, n_before, own, near, far, cross, truth, lat, pen, *refs):
    before, refs = refs[:n_before], refs[n_before:]
    far_out, cross_out, d_near, loss, out, row_sums, d_own, d_far, d_cross, sems = refs
    rows, cols = d_far.shape[1:]
    sources = ((own, start), (near, start), (far, 0), (cross, 0))
    targets = ((d_own, 0), (d_near, start), (d_far, 0), (d_cross, 0))
    homes = ((d_own, window(out, 0, rows, start, cols)), (d_far, far_out), (d_cross, cross_out))
    copies = []
    for row in range(0, rows, SUBLANES):
        r = pl.ds(row, SUBLANES)
        penalty = pen[pl.ds(pl.multiple_of(lax.axis_index("member") * rows + row, SUBLANES), SUBLANES), :]

        def step(i, total):
            def at(shift):
                return pl.ds(pl.multiple_of(i * LANES + shift, LANES), LANES)

            x = [ref[k, r, at(shift)] for ref, shift in sources for k in range(2)]
            n = len(x)
            y = truth[r, at(start)]
            area = jnp.broadcast_to(lat[:, at(start)], (SUBLANES, LANES))
            signs = [None] * n
            for a in range(n):
                for b in range(a + 1, n):
                    s = jnp.where(x[a] > x[b], 1.0, jnp.where(x[a] < x[b], -1.0, 0.0))
                    signs[a] = s if signs[a] is None else signs[a] + s
                    signs[b] = -s if signs[b] is None else signs[b] - s
            factor = penalty * area
            score = jnp.zeros_like(y)
            for j in range(n):
                e = x[j] - y
                g = jnp.where(e > 0.0, weight, jnp.where(e < 0.0, -weight, 0.0)) - scale * signs[j]
                score = score + e * g
                target, shift = targets[j // 2]
                target[j % 2, r, at(shift)] = factor * g
            return total + area * score

        total = before[1][r, :] if before else jnp.zeros((SUBLANES, LANES), jnp.float32)
        total = lax.fori_loop(0, cols // LANES, step, total, unroll=2)
        loss[r, :] = total
        for i, (source, home) in enumerate(homes):
            copies.append(pltpu.make_async_copy(source.at[:, r], home.at[:, r], sems.at[i, row // SUBLANES]))
            copies[-1].start()
    if last:
        sums = jnp.sum(loss[...], axis=1, keepdims=True)
        field = lax.axis_index("member") * rows + lax.broadcasted_iota(jnp.int32, loss.shape, 0)
        here = lax.broadcasted_iota(jnp.int32, loss.shape, 1) == field
        row_sums[...] = jnp.sum(jnp.where(here, sums, 0.0), axis=0, keepdims=True)
    for copy in copies:
        copy.wait()


def score(scale, weight, start, width, shape, last, own, near, far, cross, truth, lat, pen, *before):
    members, quarter = own.shape[:2]
    block = (members, quarter, width)
    shapes = (block, block, own.shape, (quarter, LANES), shape, (1, LANES))
    return pl.pallas_call(
        functools.partial(score_kernel, scale, weight, start, last, len(before)),
        out_shape=[jax.ShapeDtypeStruct(s, jnp.float32) for s in shapes],
        in_specs=[VMEM] * 7 + [VMEM, VMEM, HBM][:len(before)],
        out_specs=[HBM, HBM, VMEM, VMEM, HBM, VMEM],
        scratch_shapes=[pltpu.VMEM(block, jnp.float32)] * 3 + [pltpu.SemaphoreType.DMA((3, quarter // SUBLANES))],
        input_output_aliases={7: 2, 8: 3, 9: 4} if before else {},
        compiler_params=pltpu.CompilerParams(vmem_limit_bytes=LARGE),
        cost_estimate=pl.CostEstimate(
            flops=WORK * quarter * width, bytes_accessed=20 * quarter * width * 4, transcendentals=0
        ),
    )(own, near, far, cross, truth, lat, pen, *before)


def shards(x, y, lat, pen):
    members = lax.axis_size("member")
    spaces = lax.axis_size("space")
    samples = x.shape[0] * members
    fields, points = y.shape
    scale = (1.0 - 0.05 / samples) / (samples * (samples - 1))
    quarter = fields // members
    first = int(points * SPLIT)
    chunks = ((0, first), (first, points - first))

    far_cross = [[(0, FAR, start, width), (0, CROSS, start, width)] for start, width in chunks]
    to_near, *first_sent = take([(0, NEAR, 0, points)] + far_cross[0], quarter, [x])
    second_sent = take(far_cross[1], quarter, [x], first_sent)
    own, truth = take([(0, 0, 0, points), (1, 0, 0, points)], quarter, [x, y], second_sent)
    sent = (first_sent, second_sent)
    far = [exchange(pair[0], FAR) for pair in sent]
    cross = [exchange(pair[1], CROSS) for pair in sent]
    near = exchange(to_near, NEAR)
    pen_lanes = jnp.broadcast_to(pen[:, None], (fields, LANES))
    back, before = [], ()
    for c, (start, width) in enumerate(chunks):
        d_far, d_cross, *before, sums = score(
            scale, 1.0 / samples, start, width, x.shape, c == len(chunks) - 1, own, near, far[c], cross[c], truth, lat[None, :], pen_lanes, *before
        )
        back.append([(FAR, start, width, exchange(d_far, FAR)), (CROSS, start, width, exchange(d_cross, CROSS))])
    d_near, loss, out = before
    back.insert(1, [(NEAR, 0, points, exchange(d_near, NEAR))])
    everyone = lax.all_to_all(jnp.broadcast_to(sums[None], (spaces,) + sums.shape), "space", 0, 0)

    def put(group, *job):
        return place([g[:3] for g in group], quarter, [g[3] for g in group], out, *job)

    out, sums = put(back[0], PLACING, add_rows, (everyone,), sums.shape)
    rows = [exchange(sums, f) for f in (FAR, CROSS, NEAR)]
    out, = put(back[1])
    pen_row = pen[None, :]
    out, field_loss = put(
        back[2], 0, functools.partial(weigh, points * spaces), (pen_row, sums, *rows), pen_row.shape
    )
    return out, field_loss[0]


def solution(mesh):
    return jax.shard_map(
        shards,
        mesh=mesh,
        in_specs=(P("member", None, "space"), P(None, "space"), P("space"), P()),
        out_specs=(P("member", None, "space"), P()),
        check_vma=False,
    )
```

time: 81.1 us -> 77 us (0.949)
  local copies, waits for them, and re-layouts: 16.2 us -> 0.7 us
  Pallas kernels: 3.5 us -> 13.4 us
  waiting for transfers between devices: 26.4 us -> 33.3 us
  starting transfers between devices: 32.4 us -> 28.6 us
  other arithmetic: 1.49 us -> 0 us
    dynamic_update_slice x8 -> x0, local copies, waits for them, and re-layouts: 10.1 us -> none  [shards(): lax.dynamic_update_slice(out, pieces[c][f], (0, (me ^ f) * quarter, c * w...]
    pallas_call x2 -> x8, Pallas kernels: 3.5 us -> 13.4 us  [the longest x2 5.91 us: score(): pl.pallas_call(functools.partial(score_kernel, scale, weight, start, last...]
    ppermute x12 -> x13, waiting for transfers between devices: 23.2 us -> 26.7 us  [exchange(): return lax.ppermute(block, AXES, pairs)]
    all_to_all x1, waiting for transfers between devices: 3.22 us -> 6.56 us  [shards(): lax.all_to_all(jnp.broadcast_to(sums[None], (spaces,) + sums.shape), 'spa...]
    dynamic_slice x3 -> x0, local copies, waits for them, and re-layouts: 3.23 us -> none  [the longest x2 3.16 us: part(): return lax.dynamic_slice(array, start, size)]
    all_to_all x1, starting transfers between devices: 11 us -> 7.97 us  [shards(): lax.all_to_all(jnp.broadcast_to(sums[None], (spaces,) + sums.shape), 'spa...]
    broadcast_in_dim x3 -> x2, local copies, waits for them, and re-layouts: 2.75 us -> 0.68 us  [the longest x1 0.61 us: shards(): jnp.broadcast_to(sums[None], (spaces,) + sums.shape)]
    reduce_sum x2 -> x0, other arithmetic: 0.97 us -> none  [the longest x1 0.86 us: shards(): jnp.sum(everyone.reshape(members, spaces, quarter), axis=1).reshape(fields)]
  transfers between devices with their start and end apart: 13 -> 14, of which waited for: 5 -> 7; matrix products, arithmetic and copies ran while one was open for 18% -> 1% of each run, Pallas kernels for 4% -> 14%
where the time goes in v2:
time: 77 us; the launch traced here: 76.7 us
  waiting for transfers between devices  33.3 us (43%)
  starting transfers between devices  28.6 us (37%)
  Pallas kernels  13.4 us (17%)
    ppermute x13, waiting for transfers between devices, exchange(): return lax.ppermute(block, AXES, pairs)  26.7 us
    ppermute x13, starting transfers between devices, exchange(): return lax.ppermute(block, AXES, pairs)  20.6 us
    all_to_all x1, starting transfers between devices, shards(): lax.all_to_all(jnp.broadcast_to(sums[None], (spaces,) + sums.shape), 'spa...  7.97 us
    all_to_all x1, waiting for transfers between devices, shards(): lax.all_to_all(jnp.broadcast_to(sums[None], (spaces,) + sums.shape), 'spa...  6.56 us
    pallas_call x2, Pallas kernels, score(): pl.pallas_call(functools.partial(score_kernel, scale, weight, start, last...  5.91 us
    pallas_call x3, Pallas kernels, take(): pl.pallas_call(functools.partial(take_kernel, specs, quarter, len(arrays)...  3.77 us
    pallas_call x3, Pallas kernels, place(): pl.pallas_call(functools.partial(place_kernel, specs, quarter, job, len(m...  3.73 us
  transfers between devices with their start and end apart: 14, of which 7 were waited for; matrix products, arithmetic and copies ran while one was open for 1% of the time, Pallas kernels for 14%

profile of v2, /device:TPU:1, one launch (start us, length us, event | category | flops | bytes accessed | tf_op | source)
XLA Modules:
  0.0 76.7 jit_solution(3574502706598150886)
XLA Ops:
  0.6 1.5 %shard_map.59 = (f32[2,24,4096]{2,1,0:T(8,128)S(1)}, f32[2,24,2560]{2,1,0:T(8,128)S(1)}, f32[2,24,2560]{2,1,0:T(8,128)S(1)}) custom-call(f32[2,96,4096]{2,1,0:T(8,128)} %refs_0_.5), custom_call_target="tpu_custom_call" | custom-call | bytes 3538944 | tf_op jit(solution)/shard_map/pallas_call | solution.py:56
  2.1 1.5 %collective-permute-start = (f32[2,24,4096]{2,1,0:T(8,128)S(1)}, f32[2,24,4096]{2,1,0:T(8,128)S(1)}, u32[]{:S(2)}, u32[]{:S(2)}) collective-permute-start(f32[2,24,4096]{2,1,0:T(8,128)S(1)} %get-tuple-element.28), channel_id=1, source_target_pairs={{0,32},{1,33},{2,34},{3,35},{4,36},{5,37},{6,38},{7,39},{8,40},{9,... | collective-permute-start | bytes 2359304 | tf_op jit(solution)/shard_map/ppermute | solution.py:28
  3.6 3.7 %collective-permute-start.3 = (f32[2,24,2560]{2,1,0:T(8,128)S(1)}, f32[2,24,2560]{2,1,0:T(8,128)S(1)}, u32[]{:S(2)}, u32[]{:S(2)}) collective-permute-start(f32[2,24,2560]{2,1,0:T(8,128)S(1)} %get-tuple-element.23.refs_1_), channel_id=1, source_target_pairs={{0,64},{1,65},{2,66},{3,67},{4,68},{5,69},{6,70},{7,71},{8,72},{9,... | collective-permute-start | bytes 1474568 | tf_op jit(solution)/shard_map/ppermute | solution.py:28
  7.3 0.1 collective-permute-start.4
  7.3 1.1 %shard_map.60 = (f32[2,24,1536]{2,1,0:T(8,128)S(1)}, f32[2,24,1536]{2,1,0:T(8,128)S(1)}) custom-call(f32[2,96,4096]{2,1,0:T(8,128)} %refs_0_.5, f32[2,24,2560]{2,1,0:T(8,128)S(1)} %get-tuple-element.23.refs_1_, f32[2,24,2560]{2,1,0:T(8,128)S(1)} %get-tuple-element.24.refs_2_), custom_call_target="tpu_custom_call" | custom-call | bytes 1179648 | tf_op jit(solution)/shard_map/pallas_call | solution.py:56
  8.4 0.0 copy-start
  8.4 0.0 copy-start.1
  8.4 3.2 %collective-permute-start.1 = (f32[2,24,1536]{2,1,0:T(8,128)S(1)}, f32[2,24,1536]{2,1,0:T(8,128)S(1)}, u32[]{:S(2)}, u32[]{:S(2)}) collective-permute-start(f32[2,24,1536]{2,1,0:T(8,128)S(1)} %get-tuple-element.25.refs_2_), channel_id=1, source_target_pairs={{0,64},{1,65},{2,66},{3,67},{4,68},{5,69},{6,70},{7,71},{8,72},{9,... | collective-permute-start | bytes 884744 | tf_op jit(solution)/shard_map/ppermute | solution.py:28
  11.7 0.3 collective-permute-start.2
  12.0 1.2 %shard_map.61 = (f32[2,24,4096]{2,1,0:T(8,128)S(1)}, f32[24,4096]{1,0:T(8,128)S(1)}) custom-call(f32[2,96,4096]{2,1,0:T(8,128)} %refs_0_.5, f32[96,4096]{1,0:T(8,128)} %refs_1_.1, f32[2,24,1536]{2,1,0:T(8,128)S(1)} %get-tuple-element.25.refs_2_, f32[2,24,1536]{2,1,0:T(8,128)S(1)} %get-tuple-element.26.refs_3_), custom_call_target="tpu_custom_call" | custom-call | bytes 2359296 | tf_op jit(solution)/shard_map/pallas_call | solution.py:56
  13.3 5.5 %collective-permute-done.3.far = f32[2,24,2560]{2,1,0:T(8,128)S(1)} collective-permute-done((f32[2,24,2560]{2,1,0:T(8,128)S(1)}, f32[2,24,2560]{2,1,0:T(8,128)S(1)}, u32[]{:S(2)}, u32[]{:S(2)}) %collective-permute-start.3) | collective-permute-done | bytes 491552 | tf_op jit(solution)/shard_map/ppermute | solution.py:28
  18.8 10.8 %collective-permute-done.4.cross = f32[2,24,2560]{2,1,0:T(8,128)S(1)} collective-permute-done((f32[2,24,2560]{2,1,0:T(8,128)S(1)}, f32[2,24,2560]{2,1,0:T(8,128)S(1)}, u32[]{:S(2)}, u32[]{:S(2)}) %collective-permute-start.4) | collective-permute-done | bytes 491552 | tf_op jit(solution)/shard_map/ppermute | solution.py:28
  29.6 0.0 collective-permute-done.near
  29.6 0.0 copy-done
  29.6 0.1 broadcast_in_dim.22.pen
  29.6 0.0 copy-done.1
  29.6 3.7 %shard_map.62 = (f32[2,24,2560]{2,1,0:T(8,128)}, f32[2,24,2560]{2,1,0:T(8,128)S(1)}, f32[2,24,4096]{2,1,0:T(8,128)S(1)}, f32[24,128]{1,0:T(8,128)S(1)}, f32[2,96,4096]{2,1,0:T(8,128)}, /*index=5*/f32[1,128]{1,0:T(1,128)}) custom-call(f32[2,24,4096]{2,1,0:T(8,128)S(1)} %get-tuple-element.27.own, f32[2,24,4096]{2,1,0:T(8,128)S(1)} %collective-permute-done.near, ...), custom_call_target="tpu_custom_call" | custom-call | flops 24576000000 | bytes 4915200 | tf_op jit(solution)/shard_map/pallas_call | solution.py:161
  33.4 3.3 %collective-permute-start.8 = (f32[2,24,2560]{2,1,0:T(8,128)}, f32[2,24,2560]{2,1,0:T(8,128)S(1)}, u32[]{:S(2)}, u32[]{:S(2)}) collective-permute-start(f32[2,24,2560]{2,1,0:T(8,128)} %get-tuple-element.36), channel_id=1, source_target_pairs={{0,64},{1,65},{2,66},{3,67},{4,68},{5,69},{6,70},{7,71},{8,72},{9,... | collective-permute-start | bytes 1474568 | tf_op jit(solution)/shard_map/ppermute | solution.py:28
  36.6 0.1 collective-permute-start.9
  36.8 0.0 collective-permute-done.1.far
  36.8 5.4 %collective-permute-done.2.cross = f32[2,24,1536]{2,1,0:T(8,128)S(1)} collective-permute-done((f32[2,24,1536]{2,1,0:T(8,128)S(1)}, f32[2,24,1536]{2,1,0:T(8,128)S(1)}, u32[]{:S(2)}, u32[]{:S(2)}) %collective-permute-start.2) | collective-permute-done | bytes 294944 | tf_op jit(solution)/shard_map/ppermute | solution.py:28
  42.2 2.2 %shard_map.63 = (f32[2,24,1536]{2,1,0:T(8,128)}, f32[2,24,1536]{2,1,0:T(8,128)S(1)}, f32[2,24,4096]{2,1,0:T(8,128)S(1)}, f32[24,128]{1,0:T(8,128)S(1)}, f32[2,96,4096]{2,1,0:T(8,128)}, /*index=5*/f32[1,128]{1,0:T(1,128)S(1)}) custom-call(f32[2,24,4096]{2,1,0:T(8,128)S(1)} %get-tuple-element.27.own, ...), custom_call_target="tpu_custom_call", output_to_operand_aliasing={{2}: (7, {}), {3}: (8, {}), {4}: (9, {})} | custom-call | flops 14745600000 | bytes 2949120 | tf_op jit(solution)/shard_map/pallas_call | solution.py:161
  44.4 0.6 broadcast_in_dim.24
  45.0 8.0 %all-to-all-start = ((f32[32,1,128]{2,1,0:T(1,128)}), f32[32,1,128]{2,1,0:T(1,128)S(1)}, u32[]{:S(2)}, u32[]{:S(2)}) async-start(f32[32,1,128]{2,1,0:T(1,128)} %broadcast_in_dim.24), calls=%async_computation | async-start | bytes 32768 | tf_op jit(solution)/shard_map/all_to_all | solution.py:202
  53.0 3.4 %collective-permute-start.5 = (f32[2,24,1536]{2,1,0:T(8,128)}, f32[2,24,1536]{2,1,0:T(8,128)S(1)}, u32[]{:S(2)}, u32[]{:S(2)}) collective-permute-start(f32[2,24,1536]{2,1,0:T(8,128)} %get-tuple-element.33), channel_id=1, source_target_pairs={{0,64},{1,65},{2,66},{3,67},{4,68},{5,69},{6,70},{7,71},{8,72},{9,... | collective-permute-start | bytes 884744 | tf_op jit(solution)/shard_map/ppermute | solution.py:28
  56.4 0.0 collective-permute-start.6
  56.4 0.5 collective-permute-start.7
  56.9 6.6 %all-to-all-done.refs_3_ = f32[32,1,128]{2,1,0:T(1,128)S(1)} async-done(((f32[32,1,128]{2,1,0:T(1,128)}), f32[32,1,128]{2,1,0:T(1,128)S(1)}, u32[]{:S(2)}, u32[]{:S(2)}) %all-to-all-start) | async-done | bytes 16416 | tf_op jit(solution)/shard_map/all_to_all | solution.py:202
  63.4 0.0 collective-permute-done.8.refs_0_
  63.4 0.1 collective-permute-done.9.refs_1_
  63.5 2.0 %shard_map.64 = (f32[2,96,4096]{2,1,0:T(8,128)}, f32[1,128]{1,0:T(1,128)S(1)}) custom-call(f32[2,24,2560]{2,1,0:T(8,128)S(1)} %collective-permute-done.8.refs_0_, f32[2,24,2560]{2,1,0:T(8,128)} %collective-permute-done.9.refs_1_, f32[2,96,4096]{2,1,0:T(8,128)} %get-tuple-element.38.refs_2_, ...), custom_call_target="tpu_custom_call", output_to_operand_aliasing={{0}: (2, {})} | custom-call | flops 40000000000 | bytes 1966080 | tf_op jit(solution)/shard_map/pallas_call | solution.py:85
  65.5 1.6 %collective-permute-start.12 = (f32[1,128]{1,0:T(1,128)S(1)}, f32[1,128]{1,0:T(1,128)S(1)}, u32[]{:S(2)}, u32[]{:S(2)}) collective-permute-start(f32[1,128]{1,0:T(1,128)S(1)} %get-tuple-element.41.refs_4_), channel_id=1, source_target_pairs={{0,32},{1,33},{2,34},{3,35},{4,36},{5,37},{6,38},{7,39},{8,40},{9,... | collective-permute-start | bytes 1544 | tf_op jit(solution)/shard_map/ppermute | solution.py:28
  67.1 2.1 %collective-permute-start.11 = (f32[1,128]{1,0:T(1,128)S(1)}, f32[1,128]{1,0:T(1,128)S(1)}, u32[]{:S(2)}, u32[]{:S(2)}) collective-permute-start(f32[1,128]{1,0:T(1,128)S(1)} %get-tuple-element.41.refs_4_), channel_id=1, source_target_pairs={{0,96},{1,97},{2,98},{3,99},{4,100},{5,101},{6,102},{7,103},{8,104... | collective-permute-start | bytes 1544 | tf_op jit(solution)/shard_map/ppermute | solution.py:28
  69.2 0.0 collective-permute-done.7.refs_0_
  69.2 0.9 %collective-permute-start.10 = (f32[1,128]{1,0:T(1,128)S(1)}, f32[1,128]{1,0:T(1,128)S(1)}, u32[]{:S(2)}, u32[]{:S(2)}) collective-permute-start(f32[1,128]{1,0:T(1,128)S(1)} %get-tuple-element.41.refs_4_), channel_id=1, source_target_pairs={{0,64},{1,65},{2,66},{3,67},{4,68},{5,69},{6,70},{7,71},{8,72},{9,... | collective-permute-start | bytes 1544 | tf_op jit(solution)/shard_map/ppermute | solution.py:28
  70.1 0.9 %shard_map.65.refs_2_ = f32[2,96,4096]{2,1,0:T(8,128)} custom-call(f32[2,24,4096]{2,1,0:T(8,128)S(1)} %collective-permute-done.7.refs_0_, f32[2,96,4096]{2,1,0:T(8,128)} %get-tuple-element.40.refs_1_), custom_call_target="tpu_custom_call", output_to_operand_aliasing={{}: (1, {})} | custom-call | bytes 1572864 | tf_op jit(solution)/shard_map/pallas_call | solution.py:85
  71.0 0.0 collective-permute-done.5.refs_0_
  71.0 4.8 %collective-permute-done.6.refs_1_ = f32[2,24,1536]{2,1,0:T(8,128)S(1)} collective-permute-done((f32[2,24,1536]{2,1,0:T(8,128)S(1)}, f32[2,24,1536]{2,1,0:T(8,128)S(1)}, u32[]{:S(2)}, u32[]{:S(2)}) %collective-permute-start.6) | collective-permute-done | bytes 294944 | tf_op jit(solution)/shard_map/ppermute | solution.py:28
  75.8 0.0 collective-permute-done.12.refs_7_
  75.8 0.1 collective-permute-done.11.refs_6_
  75.9 0.0 collective-permute-done.10.refs_5_
  75.9 0.8 %shard_map.66 = (f32[2,96,4096]{2,1,0:T(8,128)}, f32[1,96]{1,0:T(1,128)}) custom-call(f32[2,24,1536]{2,1,0:T(8,128)S(1)} %collective-permute-done.5.refs_0_, f32[2,24,1536]{2,1,0:T(8,128)S(1)} %collective-permute-done.6.refs_1_, f32[2,96,4096]{2,1,0:T(8,128)} %shard_map.65.refs_2_, f32[1,96]{1,0:T(1,128)S(1)} %bitcast.4, ...), custom_call_target="tpu_custom_call", output_to_operand_aliasing={{0}: (2, {})} | custom-call | bytes 1179648 | tf_op jit(solution)/shard_map/pallas_call | solution.py:85
Async XLA Ops:
  2.1 27.5 %collective-permute-start = (f32[2,24,4096]{2,1,0:T(8,128)S(1)}, f32[2,24,4096]{2,1,0:T(8,128)S(1)}, u32[]{:S(2)}, u32[]{:S(2)}) collective-permute-start(f32[2,24,4096]{2,1,0:T(8,128)S(1)} %get-tuple-element.28), channel_id=1, source_target_pairs={{0,32},{1,33},{2,34},{3,35},{4,36},{5,37},{6,38},{7,39},{8,40},{9,... | collective-permute-start | bytes 2359304 | tf_op jit(solution)/shard_map/ppermute | solution.py:28
  3.6 15.2 %collective-permute-start.3 = (f32[2,24,2560]{2,1,0:T(8,128)S(1)}, f32[2,24,2560]{2,1,0:T(8,128)S(1)}, u32[]{:S(2)}, u32[]{:S(2)}) collective-permute-start(f32[2,24,2560]{2,1,0:T(8,128)S(1)} %get-tuple-element.23.refs_1_), channel_id=1, source_target_pairs={{0,64},{1,65},{2,66},{3,67},{4,68},{5,69},{6,70},{7,71},{8,72},{9,... | collective-permute-start | bytes 1474568 | tf_op jit(solution)/shard_map/ppermute | solution.py:28
  7.3 22.3 %collective-permute-start.4 = (f32[2,24,2560]{2,1,0:T(8,128)S(1)}, f32[2,24,2560]{2,1,0:T(8,128)S(1)}, u32[]{:S(2)}, u32[]{:S(2)}) collective-permute-start(f32[2,24,2560]{2,1,0:T(8,128)S(1)} %get-tuple-element.24.refs_2_), channel_id=1, source_target_pairs={{0,96},{1,97},{2,98},{3,99},{4,100},{5,101},{6,102},{7,103},{8,104... | collective-permute-start | bytes 1474568 | tf_op jit(solution)/shard_map/ppermute | solution.py:28
  8.4 21.1 %copy-start = (f32[96]{0:T(128)S(1)}, f32[96]{0:T(128)}, u32[]{:S(2)}) copy-start(f32[96]{0:T(128)} %param.7) | copy-start | bytes 1156
  8.4 21.2 %copy-start.1 = (f32[4096]{0:T(1024)S(1)}, f32[4096]{0:T(1024)}, u32[]{:S(2)}) copy-start(f32[4096]{0:T(1024)} %param.6) | copy-start | bytes 49156
  8.4 28.3 %collective-permute-start.1 = (f32[2,24,1536]{2,1,0:T(8,128)S(1)}, f32[2,24,1536]{2,1,0:T(8,128)S(1)}, u32[]{:S(2)}, u32[]{:S(2)}) collective-permute-start(f32[2,24,1536]{2,1,0:T(8,128)S(1)} %get-tuple-element.25.refs_2_), channel_id=1, source_target_pairs={{0,64},{1,65},{2,66},{3,67},{4,68},{5,69},{6,70},{7,71},{8,72},{9,... | collective-permute-start | bytes 884744 | tf_op jit(solution)/shard_map/ppermute | solution.py:28
  11.7 30.5 %collective-permute-start.2 = (f32[2,24,1536]{2,1,0:T(8,128)S(1)}, f32[2,24,1536]{2,1,0:T(8,128)S(1)}, u32[]{:S(2)}, u32[]{:S(2)}) collective-permute-start(f32[2,24,1536]{2,1,0:T(8,128)S(1)} %get-tuple-element.26.refs_3_), channel_id=1, source_target_pairs={{0,96},{1,97},{2,98},{3,99},{4,100},{5,101},{6,102},{7,103},{8,104... | collective-permute-start | bytes 884744 | tf_op jit(solution)/shard_map/ppermute | solution.py:28
  33.4 30.0 %collective-permute-start.8 = (f32[2,24,2560]{2,1,0:T(8,128)}, f32[2,24,2560]{2,1,0:T(8,128)S(1)}, u32[]{:S(2)}, u32[]{:S(2)}) collective-permute-start(f32[2,24,2560]{2,1,0:T(8,128)} %get-tuple-element.36), channel_id=1, source_target_pairs={{0,64},{1,65},{2,66},{3,67},{4,68},{5,69},{6,70},{7,71},{8,72},{9,... | collective-permute-start | bytes 1474568 | tf_op jit(solution)/shard_map/ppermute | solution.py:28
  36.6 26.9 %collective-permute-start.9 = (f32[2,24,2560]{2,1,0:T(8,128)S(1)}, f32[2,24,2560]{2,1,0:T(8,128)}, u32[]{:S(2)}, u32[]{:S(2)}) collective-permute-start(f32[2,24,2560]{2,1,0:T(8,128)S(1)} %get-tuple-element.37), channel_id=1, source_target_pairs={{0,96},{1,97},{2,98},{3,99},{4,100},{5,101},{6,102},{7,103},{8,104... | collective-permute-start | bytes 1474568 | tf_op jit(solution)/shard_map/ppermute | solution.py:28
  45.0 18.4 %all-to-all-start = ((f32[32,1,128]{2,1,0:T(1,128)}), f32[32,1,128]{2,1,0:T(1,128)S(1)}, u32[]{:S(2)}, u32[]{:S(2)}) async-start(f32[32,1,128]{2,1,0:T(1,128)} %broadcast_in_dim.24), calls=%async_computation | async-start | bytes 32768 | tf_op jit(solution)/shard_map/all_to_all | solution.py:202
  53.0 18.0 %collective-permute-start.5 = (f32[2,24,1536]{2,1,0:T(8,128)}, f32[2,24,1536]{2,1,0:T(8,128)S(1)}, u32[]{:S(2)}, u32[]{:S(2)}) collective-permute-start(f32[2,24,1536]{2,1,0:T(8,128)} %get-tuple-element.33), channel_id=1, source_target_pairs={{0,64},{1,65},{2,66},{3,67},{4,68},{5,69},{6,70},{7,71},{8,72},{9,... | collective-permute-start | bytes 884744 | tf_op jit(solution)/shard_map/ppermute | solution.py:28
  56.4 19.4 %collective-permute-start.6 = (f32[2,24,1536]{2,1,0:T(8,128)S(1)}, f32[2,24,1536]{2,1,0:T(8,128)S(1)}, u32[]{:S(2)}, u32[]{:S(2)}) collective-permute-start(f32[2,24,1536]{2,1,0:T(8,128)S(1)} %get-tuple-element.34), channel_id=1, source_target_pairs={{0,96},{1,97},{2,98},{3,99},{4,100},{5,101},{6,102},{7,103},{8,104... | collective-permute-start | bytes 884744 | tf_op jit(solution)/shard_map/ppermute | solution.py:28
  56.4 12.8 %collective-permute-start.7 = (f32[2,24,4096]{2,1,0:T(8,128)S(1)}, f32[2,24,4096]{2,1,0:T(8,128)S(1)}, u32[]{:S(2)}, u32[]{:S(2)}) collective-permute-start(f32[2,24,4096]{2,1,0:T(8,128)S(1)} %get-tuple-element.35), channel_id=1, source_target_pairs={{0,32},{1,33},{2,34},{3,35},{4,36},{5,37},{6,38},{7,39},{8,40},{9,... | collective-permute-start | bytes 2359304 | tf_op jit(solution)/shard_map/ppermute | solution.py:28
  65.5 10.3 %collective-permute-start.12 = (f32[1,128]{1,0:T(1,128)S(1)}, f32[1,128]{1,0:T(1,128)S(1)}, u32[]{:S(2)}, u32[]{:S(2)}) collective-permute-start(f32[1,128]{1,0:T(1,128)S(1)} %get-tuple-element.41.refs_4_), channel_id=1, source_target_pairs={{0,32},{1,33},{2,34},{3,35},{4,36},{5,37},{6,38},{7,39},{8,40},{9,... | collective-permute-start | bytes 1544 | tf_op jit(solution)/shard_map/ppermute | solution.py:28
  67.1 8.7 %collective-permute-start.11 = (f32[1,128]{1,0:T(1,128)S(1)}, f32[1,128]{1,0:T(1,128)S(1)}, u32[]{:S(2)}, u32[]{:S(2)}) collective-permute-start(f32[1,128]{1,0:T(1,128)S(1)} %get-tuple-element.41.refs_4_), channel_id=1, source_target_pairs={{0,96},{1,97},{2,98},{3,99},{4,100},{5,101},{6,102},{7,103},{8,104... | collective-permute-start | bytes 1544 | tf_op jit(solution)/shard_map/ppermute | solution.py:28
  69.2 6.7 %collective-permute-start.10 = (f32[1,128]{1,0:T(1,128)S(1)}, f32[1,128]{1,0:T(1,128)S(1)}, u32[]{:S(2)}, u32[]{:S(2)}) collective-permute-start(f32[1,128]{1,0:T(1,128)S(1)} %get-tuple-element.41.refs_4_), channel_id=1, source_target_pairs={{0,64},{1,65},{2,66},{3,67},{4,68},{5,69},{6,70},{7,71},{8,72},{9,... | collective-permute-start | bytes 1544 | tf_op jit(solution)/shard_map/ppermute | solution.py:28

commit v3 on v2

--- a/solution.py
+++ b/solution.py
@@ -42,8 +42,10 @@
 def take_kernel(specs, quarter, n_arrays, n_deps, *refs):
     arrays, outs, sems = refs[:n_arrays], refs[n_arrays + n_deps:-1], refs[-1]
     copies = []
-    for i, (which, flip, start, width) in enumerate(specs):
+    for i, (which, flip, start, width, *member) in enumerate(specs):
         source = window(arrays[which], flip, quarter, start, width)
+        if member:
+            source = source.at[pl.ds(member[0], 1)]
         copies.append(pltpu.make_async_copy(source, outs[i], sems.at[i]))
     for copy in copies:
         copy.start()
@@ -52,7 +54,7 @@
 
 
 def take(specs, quarter, arrays, deps=()):
-    shapes = [arrays[w].shape[:-2] + (quarter, width) for w, _, _, width in specs]
+    shapes = [((1,) if member else arrays[w].shape[:-2]) + (quarter, width) for w, _, _, width, *member in specs]
     return pl.pallas_call(
         functools.partial(take_kernel, specs, quarter, len(arrays), len(deps)),
         out_shape=[jax.ShapeDtypeStruct(s, jnp.float32) for s in shapes],
@@ -103,11 +105,11 @@
     loss[...] = pen[...] * total[:, :pen.shape[1]] / count
 
 
-def score_kernel(scale, weight, start, last, n_before, own, near, far, cross, truth, lat, pen, *refs):
+def score_kernel(scale, weight, start, last, n_before, own, near_0, near_1, far, cross, truth, lat, pen, *refs):
     before, refs = refs[:n_before], refs[n_before:]
     far_out, cross_out, d_near, loss, out, row_sums, d_own, d_far, d_cross, sems = refs
     rows, cols = d_far.shape[1:]
-    sources = ((own, start), (near, start), (far, 0), (cross, 0))
+    sources = ((own, 0, start), (own, 1, start), (near_0, 0, start), (near_1, 0, start), (far, 0, 0), (far, 1, 0), (cross, 0, 0), (cross, 1, 0))
     targets = ((d_own, 0), (d_near, start), (d_far, 0), (d_cross, 0))
     homes = ((d_own, window(out, 0, rows, start, cols)), (d_far, far_out), (d_cross, cross_out))
     copies = []
@@ -119,7 +121,7 @@
             def at(shift):
                 return pl.ds(pl.multiple_of(i * LANES + shift, LANES), LANES)
 
-            x = [ref[k, r, at(shift)] for ref, shift in sources for k in range(2)]
+            x = [ref[k, r, at(shift)] for ref, k, shift in sources]
             n = len(x)
             y = truth[r, at(start)]
             area = jnp.broadcast_to(lat[:, at(start)], (SUBLANES, LANES))
@@ -161,15 +163,15 @@
     return pl.pallas_call(
         functools.partial(score_kernel, scale, weight, start, last, len(before)),
         out_shape=[jax.ShapeDtypeStruct(s, jnp.float32) for s in shapes],
-        in_specs=[VMEM] * 7 + [VMEM, VMEM, HBM][:len(before)],
+        in_specs=[VMEM] * 8 + [VMEM, VMEM, HBM][:len(before)],
         out_specs=[HBM, HBM, VMEM, VMEM, HBM, VMEM],
         scratch_shapes=[pltpu.VMEM(block, jnp.float32)] * 3 + [pltpu.SemaphoreType.DMA((3, quarter // SUBLANES))],
-        input_output_aliases={7: 2, 8: 3, 9: 4} if before else {},
+        input_output_aliases={8: 2, 9: 3, 10: 4} if before else {},
         compiler_params=pltpu.CompilerParams(vmem_limit_bytes=LARGE),
         cost_estimate=pl.CostEstimate(
             flops=WORK * quarter * width, bytes_accessed=20 * quarter * width * 4, transcendentals=0
         ),
-    )(own, near, far, cross, truth, lat, pen, *before)
+    )(own, *near, far, cross, truth, lat, pen, *before)
 
 
 def shards(x, y, lat, pen):
@@ -183,13 +185,15 @@
     chunks = ((0, first), (first, points - first))
 
     far_cross = [[(0, FAR, start, width), (0, CROSS, start, width)] for start, width in chunks]
-    to_near, *first_sent = take([(0, NEAR, 0, points)] + far_cross[0], quarter, [x])
+    first_sent = take(far_cross[0], quarter, [x])
     second_sent = take(far_cross[1], quarter, [x], first_sent)
-    own, truth = take([(0, 0, 0, points), (1, 0, 0, points)], quarter, [x, y], second_sent)
+    *to_near, own, truth = take(
+        [(0, NEAR, 0, points, 0), (0, NEAR, 0, points, 1), (0, 0, 0, points), (1, 0, 0, points)], quarter, [x, y], second_sent
+    )
     sent = (first_sent, second_sent)
     far = [exchange(pair[0], FAR) for pair in sent]
     cross = [exchange(pair[1], CROSS) for pair in sent]
-    near = exchange(to_near, NEAR)
+    near = [exchange(piece, NEAR) for piece in to_near]
     pen_lanes = jnp.broadcast_to(pen[:, None], (fields, LANES))
     back, before = [], ()
     for c, (start, width) in enumerate(chunks):

time: 77 us -> 76.1 us (0.988)
  waiting for transfers between devices: 33.3 us -> 30.7 us
  starting transfers between devices: 28.6 us -> 30.3 us
    ppermute x13 -> x14, starting transfers between devices: 20.6 us -> 22.2 us  [exchange(): return lax.ppermute(block, AXES, pairs)]
    all_to_all x1, waiting for transfers between devices: 6.56 us -> 5.18 us  [shards(): lax.all_to_all(jnp.broadcast_to(sums[None], (spaces,) + sums.shape), 'spa...]
    ppermute x13 -> x14, waiting for transfers between devices: 26.7 us -> 25.5 us  [exchange(): return lax.ppermute(block, AXES, pairs)]
  transfers between devices with their start and end apart: 14 -> 15, of which waited for: 7 -> 7; matrix products, arithmetic and copies ran while one was open for 1% -> 1% of each run, Pallas kernels for 14% -> 15%
where the time goes in v3:
time: 76.1 us; the launch traced here: 75.8 us
  waiting for transfers between devices  30.7 us (40%)
  starting transfers between devices  30.3 us (40%)
  Pallas kernels  13.5 us (18%)
    ppermute x14, waiting for transfers between devices, exchange(): return lax.ppermute(block, AXES, pairs)  25.5 us
    ppermute x14, starting transfers between devices, exchange(): return lax.ppermute(block, AXES, pairs)  22.2 us
    all_to_all x1, starting transfers between devices, shards(): lax.all_to_all(jnp.broadcast_to(sums[None], (spaces,) + sums.shape), 'spa...  8.08 us
    pallas_call x2, Pallas kernels, score(): pl.pallas_call(functools.partial(score_kernel, scale, weight, start, last...  5.94 us
    all_to_all x1, waiting for transfers between devices, shards(): lax.all_to_all(jnp.broadcast_to(sums[None], (spaces,) + sums.shape), 'spa...  5.18 us
    pallas_call x3, Pallas kernels, take(): pl.pallas_call(functools.partial(take_kernel, specs, quarter, len(arrays)...  3.8 us
    pallas_call x3, Pallas kernels, place(): pl.pallas_call(functools.partial(place_kernel, specs, quarter, job, len(m...  3.73 us
  transfers between devices with their start and end apart: 15, of which 7 were waited for; matrix products, arithmetic and copies ran while one was open for 1% of the time, Pallas kernels for 15%

profile of v3, /device:TPU:1, one launch (start us, length us, event | category | flops | bytes accessed | tf_op | source)
XLA Modules:
  0.0 75.8 jit_solution(10832052866041363833)
XLA Ops:
  0.6 1.2 %shard_map.59 = (f32[2,24,2560]{2,1,0:T(8,128)S(1)}, f32[2,24,2560]{2,1,0:T(8,128)S(1)}) custom-call(f32[2,96,4096]{2,1,0:T(8,128)} %refs_0_.5), custom_call_target="tpu_custom_call" | custom-call | bytes 1966080 | tf_op jit(solution)/shard_map/pallas_call | solution.py:58
  1.8 4.5 %collective-permute-start.4 = (f32[2,24,2560]{2,1,0:T(8,128)S(1)}, f32[2,24,2560]{2,1,0:T(8,128)S(1)}, u32[]{:S(2)}, u32[]{:S(2)}) collective-permute-start(f32[2,24,2560]{2,1,0:T(8,128)S(1)} %get-tuple-element.24.refs_1_), channel_id=1, source_target_pairs={{0,64},{1,65},{2,66},{3,67},{4,68},{5,69},{6,70},{7,71},{8,72},{9,... | collective-permute-start | bytes 1474568 | tf_op jit(solution)/shard_map/ppermute | solution.py:28
  6.4 0.7 collective-permute-start.5
  7.0 1.1 %shard_map.60 = (f32[2,24,1536]{2,1,0:T(8,128)S(1)}, f32[2,24,1536]{2,1,0:T(8,128)S(1)}) custom-call(f32[2,96,4096]{2,1,0:T(8,128)} %refs_0_.5, f32[2,24,2560]{2,1,0:T(8,128)S(1)} %get-tuple-element.24.refs_1_, f32[2,24,2560]{2,1,0:T(8,128)S(1)} %get-tuple-element.25.refs_2_), custom_call_target="tpu_custom_call" | custom-call | bytes 1179648 | tf_op jit(solution)/shard_map/pallas_call | solution.py:58
  8.1 0.0 copy-start
  8.1 0.0 copy-start.1
  8.1 1.5 %shard_map.61 = (f32[1,24,4096]{2,1,0:T(8,128)S(1)}, f32[1,24,4096]{2,1,0:T(8,128)S(1)}, f32[2,24,4096]{2,1,0:T(8,128)S(1)}, f32[24,4096]{1,0:T(8,128)S(1)}) custom-call(f32[2,96,4096]{2,1,0:T(8,128)} %refs_0_.5, f32[96,4096]{1,0:T(8,128)} %refs_1_.1, f32[2,24,1536]{2,1,0:T(8,128)S(1)} %get-tuple-element.26.refs_2_, f32[2,24,1536]{2,1,0:T(8,128)S(1)} %get-tuple-element.27.refs_3_), custom_call_target="tpu_custom_call" | custom-call | bytes 3932160 | tf_op jit(solution)/shard_map/pallas_call | solution.py:58
  9.6 0.4 collective-permute-start
  10.0 0.2 collective-permute-start.1
  10.2 3.2 %collective-permute-start.2 = (f32[2,24,1536]{2,1,0:T(8,128)S(1)}, f32[2,24,1536]{2,1,0:T(8,128)S(1)}, u32[]{:S(2)}, u32[]{:S(2)}) collective-permute-start(f32[2,24,1536]{2,1,0:T(8,128)S(1)} %get-tuple-element.26.refs_2_), channel_id=1, source_target_pairs={{0,64},{1,65},{2,66},{3,67},{4,68},{5,69},{6,70},{7,71},{8,72},{9,... | collective-permute-start | bytes 884744 | tf_op jit(solution)/shard_map/ppermute | solution.py:28
  13.4 0.0 collective-permute-done.near_0
  13.4 1.2 %collective-permute-start.3 = (f32[2,24,1536]{2,1,0:T(8,128)S(1)}, f32[2,24,1536]{2,1,0:T(8,128)S(1)}, u32[]{:S(2)}, u32[]{:S(2)}) collective-permute-start(f32[2,24,1536]{2,1,0:T(8,128)S(1)} %get-tuple-element.27.refs_3_), channel_id=1, source_target_pairs={{0,96},{1,97},{2,98},{3,99},{4,100},{5,101},{6,102},{7,103},{8,104... | collective-permute-start | bytes 884744 | tf_op jit(solution)/shard_map/ppermute | solution.py:28
  14.6 0.0 collective-permute-done.1.near_1
  14.6 2.7 %collective-permute-done.4.far = f32[2,24,2560]{2,1,0:T(8,128)S(1)} collective-permute-done((f32[2,24,2560]{2,1,0:T(8,128)S(1)}, f32[2,24,2560]{2,1,0:T(8,128)S(1)}, u32[]{:S(2)}, u32[]{:S(2)}) %collective-permute-start.4) | collective-permute-done | bytes 491552 | tf_op jit(solution)/shard_map/ppermute | solution.py:28
  17.3 11.9 %collective-permute-done.5.cross = f32[2,24,2560]{2,1,0:T(8,128)S(1)} collective-permute-done((f32[2,24,2560]{2,1,0:T(8,128)S(1)}, f32[2,24,2560]{2,1,0:T(8,128)S(1)}, u32[]{:S(2)}, u32[]{:S(2)}) %collective-permute-start.5) | collective-permute-done | bytes 491552 | tf_op jit(solution)/shard_map/ppermute | solution.py:28
  29.2 0.0 copy-done
  29.2 0.1 broadcast_in_dim.22.pen
  29.3 0.0 copy-done.1
  29.3 3.7 %shard_map.62 = (f32[2,24,2560]{2,1,0:T(8,128)}, f32[2,24,2560]{2,1,0:T(8,128)S(1)}, f32[2,24,4096]{2,1,0:T(8,128)S(1)}, f32[24,128]{1,0:T(8,128)S(1)}, f32[2,96,4096]{2,1,0:T(8,128)}, /*index=5*/f32[1,128]{1,0:T(1,128)}) custom-call(f32[2,24,4096]{2,1,0:T(8,128)S(1)} %get-tuple-element.28.own, f32[1,24,4096]{2,1,0:T(8,128)S(1)} %collective-permute-done.near_0, ...), custom_call_target="tpu_custom_call" | custom-call | flops 24576000000 | bytes 4915200 | tf_op jit(solution)/shard_map/pallas_call | solution.py:163
  33.0 3.4 %collective-permute-start.9 = (f32[2,24,2560]{2,1,0:T(8,128)}, f32[2,24,2560]{2,1,0:T(8,128)S(1)}, u32[]{:S(2)}, u32[]{:S(2)}) collective-permute-start(f32[2,24,2560]{2,1,0:T(8,128)} %get-tuple-element.38), channel_id=1, source_target_pairs={{0,64},{1,65},{2,66},{3,67},{4,68},{5,69},{6,70},{7,71},{8,72},{9,... | collective-permute-start | bytes 1474568 | tf_op jit(solution)/shard_map/ppermute | solution.py:28
  36.4 0.1 collective-permute-start.10
  36.5 0.0 collective-permute-done.2.far
  36.5 5.3 %collective-permute-done.3.cross = f32[2,24,1536]{2,1,0:T(8,128)S(1)} collective-permute-done((f32[2,24,1536]{2,1,0:T(8,128)S(1)}, f32[2,24,1536]{2,1,0:T(8,128)S(1)}, u32[]{:S(2)}, u32[]{:S(2)}) %collective-permute-start.3) | collective-permute-done | bytes 294944 | tf_op jit(solution)/shard_map/ppermute | solution.py:28
  41.8 2.2 %shard_map.63 = (f32[2,24,1536]{2,1,0:T(8,128)}, f32[2,24,1536]{2,1,0:T(8,128)S(1)}, f32[2,24,4096]{2,1,0:T(8,128)S(1)}, f32[24,128]{1,0:T(8,128)S(1)}, f32[2,96,4096]{2,1,0:T(8,128)}, /*index=5*/f32[1,128]{1,0:T(1,128)S(1)}) custom-call(f32[2,24,4096]{2,1,0:T(8,128)S(1)} %get-tuple-element.28.own, ...), custom_call_target="tpu_custom_call", output_to_operand_aliasing={{2}: (8, {}), {3}: (9, {}), {4}: (10, {})} | custom-call | flops 14745600000 | bytes 2949120 | tf_op jit(solution)/shard_map/pallas_call | solution.py:163
  44.1 0.6 broadcast_in_dim.24
  44.7 8.1 %all-to-all-start = ((f32[32,1,128]{2,1,0:T(1,128)}), f32[32,1,128]{2,1,0:T(1,128)S(1)}, u32[]{:S(2)}, u32[]{:S(2)}) async-start(f32[32,1,128]{2,1,0:T(1,128)} %broadcast_in_dim.24), calls=%async_computation | async-start | bytes 32768 | tf_op jit(solution)/shard_map/all_to_all | solution.py:206
  52.8 3.4 %collective-permute-start.6 = (f32[2,24,1536]{2,1,0:T(8,128)}, f32[2,24,1536]{2,1,0:T(8,128)S(1)}, u32[]{:S(2)}, u32[]{:S(2)}) collective-permute-start(f32[2,24,1536]{2,1,0:T(8,128)} %get-tuple-element.35), channel_id=1, source_target_pairs={{0,64},{1,65},{2,66},{3,67},{4,68},{5,69},{6,70},{7,71},{8,72},{9,... | collective-permute-start | bytes 884744 | tf_op jit(solution)/shard_map/ppermute | solution.py:28
  56.1 0.0 collective-permute-start.7
  56.1 0.5 collective-permute-start.8
  56.6 5.2 %all-to-all-done.refs_3_ = f32[32,1,128]{2,1,0:T(1,128)S(1)} async-done(((f32[32,1,128]{2,1,0:T(1,128)}), f32[32,1,128]{2,1,0:T(1,128)S(1)}, u32[]{:S(2)}, u32[]{:S(2)}) %all-to-all-start) | async-done | bytes 16416 | tf_op jit(solution)/shard_map/all_to_all | solution.py:206
  61.8 0.0 collective-permute-done.9.refs_0_
  61.8 1.4 %collective-permute-done.10.refs_1_ = f32[2,24,2560]{2,1,0:T(8,128)} collective-permute-done((f32[2,24,2560]{2,1,0:T(8,128)S(1)}, f32[2,24,2560]{2,1,0:T(8,128)}, u32[]{:S(2)}, u32[]{:S(2)}) %collective-permute-start.10) | collective-permute-done | bytes 491552 | tf_op jit(solution)/shard_map/ppermute | solution.py:28
  63.2 2.0 %shard_map.64 = (f32[2,96,4096]{2,1,0:T(8,128)}, f32[1,128]{1,0:T(1,128)S(1)}) custom-call(f32[2,24,2560]{2,1,0:T(8,128)S(1)} %collective-permute-done.9.refs_0_, f32[2,24,2560]{2,1,0:T(8,128)} %collective-permute-done.10.refs_1_, f32[2,96,4096]{2,1,0:T(8,128)} %get-tuple-element.40.refs_2_, ...), custom_call_target="tpu_custom_call", output_to_operand_aliasing={{0}: (2, {})} | custom-call | flops 40000000000 | bytes 1966080 | tf_op jit(solution)/shard_map/pallas_call | solution.py:87
  65.2 1.7 %collective-permute-start.13 = (f32[1,128]{1,0:T(1,128)S(1)}, f32[1,128]{1,0:T(1,128)S(1)}, u32[]{:S(2)}, u32[]{:S(2)}) collective-permute-start(f32[1,128]{1,0:T(1,128)S(1)} %get-tuple-element.43.refs_4_), channel_id=1, source_target_pairs={{0,32},{1,33},{2,34},{3,35},{4,36},{5,37},{6,38},{7,39},{8,40},{9,... | collective-permute-start | bytes 1544 | tf_op jit(solution)/shard_map/ppermute | solution.py:28
  66.9 2.1 %collective-permute-start.12 = (f32[1,128]{1,0:T(1,128)S(1)}, f32[1,128]{1,0:T(1,128)S(1)}, u32[]{:S(2)}, u32[]{:S(2)}) collective-permute-start(f32[1,128]{1,0:T(1,128)S(1)} %get-tuple-element.43.refs_4_), channel_id=1, source_target_pairs={{0,96},{1,97},{2,98},{3,99},{4,100},{5,101},{6,102},{7,103},{8,104... | collective-permute-start | bytes 1544 | tf_op jit(solution)/shard_map/ppermute | solution.py:28
  68.9 0.0 collective-permute-done.8.refs_0_
  68.9 0.9 %collective-permute-start.11 = (f32[1,128]{1,0:T(1,128)S(1)}, f32[1,128]{1,0:T(1,128)S(1)}, u32[]{:S(2)}, u32[]{:S(2)}) collective-permute-start(f32[1,128]{1,0:T(1,128)S(1)} %get-tuple-element.43.refs_4_), channel_id=1, source_target_pairs={{0,64},{1,65},{2,66},{3,67},{4,68},{5,69},{6,70},{7,71},{8,72},{9,... | collective-permute-start | bytes 1544 | tf_op jit(solution)/shard_map/ppermute | solution.py:28
  69.8 0.9 %shard_map.65.refs_2_ = f32[2,96,4096]{2,1,0:T(8,128)} custom-call(f32[2,24,4096]{2,1,0:T(8,128)S(1)} %collective-permute-done.8.refs_0_, f32[2,96,4096]{2,1,0:T(8,128)} %get-tuple-element.42.refs_1_), custom_call_target="tpu_custom_call", output_to_operand_aliasing={{}: (1, {})} | custom-call | bytes 1572864 | tf_op jit(solution)/shard_map/pallas_call | solution.py:87
  70.7 0.0 collective-permute-done.6.refs_0_
  70.8 4.1 %collective-permute-done.7.refs_1_ = f32[2,24,1536]{2,1,0:T(8,128)S(1)} collective-permute-done((f32[2,24,1536]{2,1,0:T(8,128)S(1)}, f32[2,24,1536]{2,1,0:T(8,128)S(1)}, u32[]{:S(2)}, u32[]{:S(2)}) %collective-permute-start.7) | collective-permute-done | bytes 294944 | tf_op jit(solution)/shard_map/ppermute | solution.py:28
  74.9 0.0 collective-permute-done.13.refs_7_
  74.9 0.1 collective-permute-done.12.refs_6_
  75.0 0.0 collective-permute-done.11.refs_5_
  75.0 0.8 %shard_map.66 = (f32[2,96,4096]{2,1,0:T(8,128)}, f32[1,96]{1,0:T(1,128)}) custom-call(f32[2,24,1536]{2,1,0:T(8,128)S(1)} %collective-permute-done.6.refs_0_, f32[2,24,1536]{2,1,0:T(8,128)S(1)} %collective-permute-done.7.refs_1_, f32[2,96,4096]{2,1,0:T(8,128)} %shard_map.65.refs_2_, f32[1,96]{1,0:T(1,128)S(1)} %bitcast.4, ...), custom_call_target="tpu_custom_call", output_to_operand_aliasing={{0}: (2, {})} | custom-call | bytes 1179648 | tf_op jit(solution)/shard_map/pallas_call | solution.py:87
Async XLA Ops:
  1.8 15.5 %collective-permute-start.4 = (f32[2,24,2560]{2,1,0:T(8,128)S(1)}, f32[2,24,2560]{2,1,0:T(8,128)S(1)}, u32[]{:S(2)}, u32[]{:S(2)}) collective-permute-start(f32[2,24,2560]{2,1,0:T(8,128)S(1)} %get-tuple-element.24.refs_1_), channel_id=1, source_target_pairs={{0,64},{1,65},{2,66},{3,67},{4,68},{5,69},{6,70},{7,71},{8,72},{9,... | collective-permute-start | bytes 1474568 | tf_op jit(solution)/shard_map/ppermute | solution.py:28
  6.4 22.8 %collective-permute-start.5 = (f32[2,24,2560]{2,1,0:T(8,128)S(1)}, f32[2,24,2560]{2,1,0:T(8,128)S(1)}, u32[]{:S(2)}, u32[]{:S(2)}) collective-permute-start(f32[2,24,2560]{2,1,0:T(8,128)S(1)} %get-tuple-element.25.refs_2_), channel_id=1, source_target_pairs={{0,96},{1,97},{2,98},{3,99},{4,100},{5,101},{6,102},{7,103},{8,104... | collective-permute-start | bytes 1474568 | tf_op jit(solution)/shard_map/ppermute | solution.py:28
  8.1 21.1 %copy-start = (f32[96]{0:T(128)S(1)}, f32[96]{0:T(128)}, u32[]{:S(2)}) copy-start(f32[96]{0:T(128)} %param.7) | copy-start | bytes 1156
  8.1 21.2 %copy-start.1 = (f32[4096]{0:T(1024)S(1)}, f32[4096]{0:T(1024)}, u32[]{:S(2)}) copy-start(f32[4096]{0:T(1024)} %param.6) | copy-start | bytes 49156
  9.6 3.8 %collective-permute-start = (f32[1,24,4096]{2,1,0:T(8,128)S(1)}, f32[1,24,4096]{2,1,0:T(8,128)S(1)}, u32[]{:S(2)}, u32[]{:S(2)}) collective-permute-start(f32[1,24,4096]{2,1,0:T(8,128)S(1)} %get-tuple-element.29), channel_id=1, source_target_pairs={{0,32},{1,33},{2,34},{3,35},{4,36},{5,37},{6,38},{7,39},{8,40},{9,... | collective-permute-start | bytes 1179656 | tf_op jit(solution)/shard_map/ppermute | solution.py:28
  10.0 4.6 %collective-permute-start.1 = (f32[1,24,4096]{2,1,0:T(8,128)S(1)}, f32[1,24,4096]{2,1,0:T(8,128)S(1)}, u32[]{:S(2)}, u32[]{:S(2)}) collective-permute-start(f32[1,24,4096]{2,1,0:T(8,128)S(1)} %get-tuple-element.30), channel_id=1, source_target_pairs={{0,32},{1,33},{2,34},{3,35},{4,36},{5,37},{6,38},{7,39},{8,40},{9,... | collective-permute-start | bytes 1179656 | tf_op jit(solution)/shard_map/ppermute | solution.py:28
  10.2 26.3 %collective-permute-start.2 = (f32[2,24,1536]{2,1,0:T(8,128)S(1)}, f32[2,24,1536]{2,1,0:T(8,128)S(1)}, u32[]{:S(2)}, u32[]{:S(2)}) collective-permute-start(f32[2,24,1536]{2,1,0:T(8,128)S(1)} %get-tuple-element.26.refs_2_), channel_id=1, source_target_pairs={{0,64},{1,65},{2,66},{3,67},{4,68},{5,69},{6,70},{7,71},{8,72},{9,... | collective-permute-start | bytes 884744 | tf_op jit(solution)/shard_map/ppermute | solution.py:28
  13.4 28.4 %collective-permute-start.3 = (f32[2,24,1536]{2,1,0:T(8,128)S(1)}, f32[2,24,1536]{2,1,0:T(8,128)S(1)}, u32[]{:S(2)}, u32[]{:S(2)}) collective-permute-start(f32[2,24,1536]{2,1,0:T(8,128)S(1)} %get-tuple-element.27.refs_3_), channel_id=1, source_target_pairs={{0,96},{1,97},{2,98},{3,99},{4,100},{5,101},{6,102},{7,103},{8,104... | collective-permute-start | bytes 884744 | tf_op jit(solution)/shard_map/ppermute | solution.py:28
  33.0 28.8 %collective-permute-start.9 = (f32[2,24,2560]{2,1,0:T(8,128)}, f32[2,24,2560]{2,1,0:T(8,128)S(1)}, u32[]{:S(2)}, u32[]{:S(2)}) collective-permute-start(f32[2,24,2560]{2,1,0:T(8,128)} %get-tuple-element.38), channel_id=1, source_target_pairs={{0,64},{1,65},{2,66},{3,67},{4,68},{5,69},{6,70},{7,71},{8,72},{9,... | collective-permute-start | bytes 1474568 | tf_op jit(solution)/shard_map/ppermute | solution.py:28
  36.4 26.8 %collective-permute-start.10 = (f32[2,24,2560]{2,1,0:T(8,128)S(1)}, f32[2,24,2560]{2,1,0:T(8,128)}, u32[]{:S(2)}, u32[]{:S(2)}) collective-permute-start(f32[2,24,2560]{2,1,0:T(8,128)S(1)} %get-tuple-element.39), channel_id=1, source_target_pairs={{0,96},{1,97},{2,98},{3,99},{4,100},{5,101},{6,102},{7,103},{8,104... | collective-permute-start | bytes 1474568 | tf_op jit(solution)/shard_map/ppermute | solution.py:28
  44.7 17.1 %all-to-all-start = ((f32[32,1,128]{2,1,0:T(1,128)}), f32[32,1,128]{2,1,0:T(1,128)S(1)}, u32[]{:S(2)}, u32[]{:S(2)}) async-start(f32[32,1,128]{2,1,0:T(1,128)} %broadcast_in_dim.24), calls=%async_computation | async-start | bytes 32768 | tf_op jit(solution)/shard_map/all_to_all | solution.py:206
  52.8 18.0 %collective-permute-start.6 = (f32[2,24,1536]{2,1,0:T(8,128)}, f32[2,24,1536]{2,1,0:T(8,128)S(1)}, u32[]{:S(2)}, u32[]{:S(2)}) collective-permute-start(f32[2,24,1536]{2,1,0:T(8,128)} %get-tuple-element.35), channel_id=1, source_target_pairs={{0,64},{1,65},{2,66},{3,67},{4,68},{5,69},{6,70},{7,71},{8,72},{9,... | collective-permute-start | bytes 884744 | tf_op jit(solution)/shard_map/ppermute | solution.py:28
  56.1 18.8 %collective-permute-start.7 = (f32[2,24,1536]{2,1,0:T(8,128)S(1)}, f32[2,24,1536]{2,1,0:T(8,128)S(1)}, u32[]{:S(2)}, u32[]{:S(2)}) collective-permute-start(f32[2,24,1536]{2,1,0:T(8,128)S(1)} %get-tuple-element.36), channel_id=1, source_target_pairs={{0,96},{1,97},{2,98},{3,99},{4,100},{5,101},{6,102},{7,103},{8,104... | collective-permute-start | bytes 884744 | tf_op jit(solution)/shard_map/ppermute | solution.py:28
  56.1 12.8 %collective-permute-start.8 = (f32[2,24,4096]{2,1,0:T(8,128)S(1)}, f32[2,24,4096]{2,1,0:T(8,128)S(1)}, u32[]{:S(2)}, u32[]{:S(2)}) collective-permute-start(f32[2,24,4096]{2,1,0:T(8,128)S(1)} %get-tuple-element.37), channel_id=1, source_target_pairs={{0,32},{1,33},{2,34},{3,35},{4,36},{5,37},{6,38},{7,39},{8,40},{9,... | collective-permute-start | bytes 2359304 | tf_op jit(solution)/shard_map/ppermute | solution.py:28
  65.2 9.7 %collective-permute-start.13 = (f32[1,128]{1,0:T(1,128)S(1)}, f32[1,128]{1,0:T(1,128)S(1)}, u32[]{:S(2)}, u32[]{:S(2)}) collective-permute-start(f32[1,128]{1,0:T(1,128)S(1)} %get-tuple-element.43.refs_4_), channel_id=1, source_target_pairs={{0,32},{1,33},{2,34},{3,35},{4,36},{5,37},{6,38},{7,39},{8,40},{9,... | collective-permute-start | bytes 1544 | tf_op jit(solution)/shard_map/ppermute | solution.py:28
  66.9 8.1 %collective-permute-start.12 = (f32[1,128]{1,0:T(1,128)S(1)}, f32[1,128]{1,0:T(1,128)S(1)}, u32[]{:S(2)}, u32[]{:S(2)}) collective-permute-start(f32[1,128]{1,0:T(1,128)S(1)} %get-tuple-element.43.refs_4_), channel_id=1, source_target_pairs={{0,96},{1,97},{2,98},{3,99},{4,100},{5,101},{6,102},{7,103},{8,104... | collective-permute-start | bytes 1544 | tf_op jit(solution)/shard_map/ppermute | solution.py:28
  68.9 6.0 %collective-permute-start.11 = (f32[1,128]{1,0:T(1,128)S(1)}, f32[1,128]{1,0:T(1,128)S(1)}, u32[]{:S(2)}, u32[]{:S(2)}) collective-permute-start(f32[1,128]{1,0:T(1,128)S(1)} %get-tuple-element.43.refs_4_), channel_id=1, source_target_pairs={{0,64},{1,65},{2,66},{3,67},{4,68},{5,69},{6,70},{7,71},{8,72},{9,... | collective-permute-start | bytes 1544 | tf_op jit(solution)/shard_map/ppermute | solution.py:28

commit v4 on v3

--- a/solution.py
+++ b/solution.py
@@ -105,13 +105,13 @@
     loss[...] = pen[...] * total[:, :pen.shape[1]] / count
 
 
-def score_kernel(scale, weight, start, last, n_before, own, near_0, near_1, far, cross, truth, lat, pen, *refs):
+def score_kernel(scale, weight, start, n_before, own, near_0, near_1, far, cross, truth, lat, pen, *refs):
     before, refs = refs[:n_before], refs[n_before:]
-    far_out, cross_out, d_near, loss, out, row_sums, d_own, d_far, d_cross, sems = refs
+    d_far, d_cross, d_near, loss, out, row_sums, d_own, sems = refs
     rows, cols = d_far.shape[1:]
     sources = ((own, 0, start), (own, 1, start), (near_0, 0, start), (near_1, 0, start), (far, 0, 0), (far, 1, 0), (cross, 0, 0), (cross, 1, 0))
     targets = ((d_own, 0), (d_near, start), (d_far, 0), (d_cross, 0))
-    homes = ((d_own, window(out, 0, rows, start, cols)), (d_far, far_out), (d_cross, cross_out))
+    homes = ((d_own, window(out, 0, rows, start, cols)),)
     copies = []
     for row in range(0, rows, SUBLANES):
         r = pl.ds(row, SUBLANES)
@@ -147,25 +147,24 @@
         for i, (source, home) in enumerate(homes):
             copies.append(pltpu.make_async_copy(source.at[:, r], home.at[:, r], sems.at[i, row // SUBLANES]))
             copies[-1].start()
-    if last:
-        sums = jnp.sum(loss[...], axis=1, keepdims=True)
-        field = lax.axis_index("member") * rows + lax.broadcasted_iota(jnp.int32, loss.shape, 0)
-        here = lax.broadcasted_iota(jnp.int32, loss.shape, 1) == field
-        row_sums[...] = jnp.sum(jnp.where(here, sums, 0.0), axis=0, keepdims=True)
+    sums = jnp.sum(loss[...], axis=1, keepdims=True)
+    field = lax.axis_index("member") * rows + lax.broadcasted_iota(jnp.int32, loss.shape, 0)
+    here = lax.broadcasted_iota(jnp.int32, loss.shape, 1) == field
+    row_sums[...] = jnp.sum(jnp.where(here, sums, 0.0), axis=0, keepdims=True)
     for copy in copies:
         copy.wait()
 
 
-def score(scale, weight, start, width, shape, last, own, near, far, cross, truth, lat, pen, *before):
+def score(scale, weight, start, width, shape, own, near, far, cross, truth, lat, pen, *before):
     members, quarter = own.shape[:2]
     block = (members, quarter, width)
-    shapes = (block, block, own.shape, (quarter, LANES), shape, (1, LANES))
+    shapes = (own.shape, (quarter, LANES), shape, (1, LANES))
     return pl.pallas_call(
-        functools.partial(score_kernel, scale, weight, start, last, len(before)),
-        out_shape=[jax.ShapeDtypeStruct(s, jnp.float32) for s in shapes],
+        functools.partial(score_kernel, scale, weight, start, len(before)),
+        out_shape=[jax.ShapeDtypeStruct(s, jnp.float32) for s in (block, block) + shapes],
         in_specs=[VMEM] * 8 + [VMEM, VMEM, HBM][:len(before)],
-        out_specs=[HBM, HBM, VMEM, VMEM, HBM, VMEM],
-        scratch_shapes=[pltpu.VMEM(block, jnp.float32)] * 3 + [pltpu.SemaphoreType.DMA((3, quarter // SUBLANES))],
+        out_specs=[VMEM, VMEM, VMEM, VMEM, HBM, VMEM],
+        scratch_shapes=[pltpu.VMEM(block, jnp.float32), pltpu.SemaphoreType.DMA((1, quarter // SUBLANES))],
         input_output_aliases={8: 2, 9: 3, 10: 4} if before else {},
         compiler_params=pltpu.CompilerParams(vmem_limit_bytes=LARGE),
         cost_estimate=pl.CostEstimate(
@@ -198,7 +197,7 @@
     back, before = [], ()
     for c, (start, width) in enumerate(chunks):
         d_far, d_cross, *before, sums = score(
-            scale, 1.0 / samples, start, width, x.shape, c == len(chunks) - 1, own, near, far[c], cross[c], truth, lat[None, :], pen_lanes, *before
+            scale, 1.0 / samples, start, width, x.shape, own, near, far[c], cross[c], truth, lat[None, :], pen_lanes, *before
         )
         back.append([(FAR, start, width, exchange(d_far, FAR)), (CROSS, start, width, exchange(d_cross, CROSS))])
     d_near, loss, out = before

time: 76.1 us -> 76.1 us (level)
  transfers between devices with their start and end apart: 15 -> 15, of which waited for: 7 -> 7; matrix products, arithmetic and copies ran while one was open for 1% -> 1% of each run, Pallas kernels for 15% -> 16%
where the time goes in v4:
time: 76.1 us; the launch traced here: 75.8 us
  starting transfers between devices  30.3 us (40%)
  waiting for transfers between devices  30.2 us (40%)
  Pallas kernels  13.9 us (18%)
    ppermute x14, waiting for transfers between devices, exchange(): return lax.ppermute(block, AXES, pairs)  25.5 us
    ppermute x14, starting transfers between devices, exchange(): return lax.ppermute(block, AXES, pairs)  22.2 us
    all_to_all x1, starting transfers between devices, shards(): lax.all_to_all(jnp.broadcast_to(sums[None], (spaces,) + sums.shape), 'spa...  8.08 us
    pallas_call x2, Pallas kernels, score(): pl.pallas_call(functools.partial(score_kernel, scale, weight, start, len(...  6.4 us
    all_to_all x1, waiting for transfers between devices, shards(): lax.all_to_all(jnp.broadcast_to(sums[None], (spaces,) + sums.shape), 'spa...  4.67 us
    pallas_call x3, Pallas kernels, take(): pl.pallas_call(functools.partial(take_kernel, specs, quarter, len(arrays)...  3.8 us
    pallas_call x3, Pallas kernels, place(): pl.pallas_call(functools.partial(place_kernel, specs, quarter, job, len(m...  3.73 us
  transfers between devices with their start and end apart: 15, of which 7 were waited for; matrix products, arithmetic and copies ran while one was open for 1% of the time, Pallas kernels for 16%

profile of v4, /device:TPU:1, one launch (start us, length us, event | category | flops | bytes accessed | tf_op | source)
XLA Modules:
  0.0 75.8 jit_solution(11473152907313044752)
XLA Ops:
  0.6 1.2 %shard_map.59 = (f32[2,24,2560]{2,1,0:T(8,128)S(1)}, f32[2,24,2560]{2,1,0:T(8,128)S(1)}) custom-call(f32[2,96,4096]{2,1,0:T(8,128)} %refs_0_.5), custom_call_target="tpu_custom_call" | custom-call | bytes 1966080 | tf_op jit(solution)/shard_map/pallas_call | solution.py:58
  1.8 4.5 %collective-permute-start.4 = (f32[2,24,2560]{2,1,0:T(8,128)S(1)}, f32[2,24,2560]{2,1,0:T(8,128)S(1)}, u32[]{:S(2)}, u32[]{:S(2)}) collective-permute-start(f32[2,24,2560]{2,1,0:T(8,128)S(1)} %get-tuple-element.24.refs_1_), channel_id=1, source_target_pairs={{0,64},{1,65},{2,66},{3,67},{4,68},{5,69},{6,70},{7,71},{8,72},{9,... | collective-permute-start | bytes 1474568 | tf_op jit(solution)/shard_map/ppermute | solution.py:28
  6.4 0.7 collective-permute-start.5
  7.0 1.1 %shard_map.60 = (f32[2,24,1536]{2,1,0:T(8,128)S(1)}, f32[2,24,1536]{2,1,0:T(8,128)S(1)}) custom-call(f32[2,96,4096]{2,1,0:T(8,128)} %refs_0_.5, f32[2,24,2560]{2,1,0:T(8,128)S(1)} %get-tuple-element.24.refs_1_, f32[2,24,2560]{2,1,0:T(8,128)S(1)} %get-tuple-element.25.refs_2_), custom_call_target="tpu_custom_call" | custom-call | bytes 1179648 | tf_op jit(solution)/shard_map/pallas_call | solution.py:58
  8.1 0.0 copy-start
  8.1 0.0 copy-start.1
  8.1 1.5 %shard_map.61 = (f32[1,24,4096]{2,1,0:T(8,128)S(1)}, f32[1,24,4096]{2,1,0:T(8,128)S(1)}, f32[2,24,4096]{2,1,0:T(8,128)S(1)}, f32[24,4096]{1,0:T(8,128)S(1)}) custom-call(f32[2,96,4096]{2,1,0:T(8,128)} %refs_0_.5, f32[96,4096]{1,0:T(8,128)} %refs_1_.1, f32[2,24,1536]{2,1,0:T(8,128)S(1)} %get-tuple-element.26.refs_2_, f32[2,24,1536]{2,1,0:T(8,128)S(1)} %get-tuple-element.27.refs_3_), custom_call_target="tpu_custom_call" | custom-call | bytes 3932160 | tf_op jit(solution)/shard_map/pallas_call | solution.py:58
  9.6 0.4 collective-permute-start
  10.0 0.2 collective-permute-start.1
  10.2 3.2 %collective-permute-start.2 = (f32[2,24,1536]{2,1,0:T(8,128)S(1)}, f32[2,24,1536]{2,1,0:T(8,128)S(1)}, u32[]{:S(2)}, u32[]{:S(2)}) collective-permute-start(f32[2,24,1536]{2,1,0:T(8,128)S(1)} %get-tuple-element.26.refs_2_), channel_id=1, source_target_pairs={{0,64},{1,65},{2,66},{3,67},{4,68},{5,69},{6,70},{7,71},{8,72},{9,... | collective-permute-start | bytes 884744 | tf_op jit(solution)/shard_map/ppermute | solution.py:28
  13.4 0.0 collective-permute-done.near_0
  13.4 1.2 %collective-permute-start.3 = (f32[2,24,1536]{2,1,0:T(8,128)S(1)}, f32[2,24,1536]{2,1,0:T(8,128)S(1)}, u32[]{:S(2)}, u32[]{:S(2)}) collective-permute-start(f32[2,24,1536]{2,1,0:T(8,128)S(1)} %get-tuple-element.27.refs_3_), channel_id=1, source_target_pairs={{0,96},{1,97},{2,98},{3,99},{4,100},{5,101},{6,102},{7,103},{8,104... | collective-permute-start | bytes 884744 | tf_op jit(solution)/shard_map/ppermute | solution.py:28
  14.6 0.0 collective-permute-done.1.near_1
  14.6 2.7 %collective-permute-done.4.far = f32[2,24,2560]{2,1,0:T(8,128)S(1)} collective-permute-done((f32[2,24,2560]{2,1,0:T(8,128)S(1)}, f32[2,24,2560]{2,1,0:T(8,128)S(1)}, u32[]{:S(2)}, u32[]{:S(2)}) %collective-permute-start.4) | collective-permute-done | bytes 491552 | tf_op jit(solution)/shard_map/ppermute | solution.py:28
  17.3 11.9 %collective-permute-done.5.cross = f32[2,24,2560]{2,1,0:T(8,128)S(1)} collective-permute-done((f32[2,24,2560]{2,1,0:T(8,128)S(1)}, f32[2,24,2560]{2,1,0:T(8,128)S(1)}, u32[]{:S(2)}, u32[]{:S(2)}) %collective-permute-start.5) | collective-permute-done | bytes 491552 | tf_op jit(solution)/shard_map/ppermute | solution.py:28
  29.2 0.0 copy-done
  29.2 0.1 broadcast_in_dim.22.pen
  29.3 0.0 copy-done.1
  29.3 3.7 %shard_map.62 = (f32[2,24,2560]{2,1,0:T(8,128)}, f32[2,24,2560]{2,1,0:T(8,128)S(1)}, f32[2,24,4096]{2,1,0:T(8,128)S(1)}, f32[24,128]{1,0:T(8,128)S(1)}, f32[2,96,4096]{2,1,0:T(8,128)}, /*index=5*/f32[1,128]{1,0:T(1,128)}) custom-call(f32[2,24,4096]{2,1,0:T(8,128)S(1)} %get-tuple-element.28.own, f32[1,24,4096]{2,1,0:T(8,128)S(1)} %collective-permute-done.near_0, ...), custom_call_target="tpu_custom_call" | custom-call | flops 24576000000 | bytes 4915200 | tf_op jit(solution)/shard_map/pallas_call | solution.py:162
  33.0 3.4 %collective-permute-start.9 = (f32[2,24,2560]{2,1,0:T(8,128)}, f32[2,24,2560]{2,1,0:T(8,128)S(1)}, u32[]{:S(2)}, u32[]{:S(2)}) collective-permute-start(f32[2,24,2560]{2,1,0:T(8,128)} %get-tuple-element.38), channel_id=1, source_target_pairs={{0,64},{1,65},{2,66},{3,67},{4,68},{5,69},{6,70},{7,71},{8,72},{9,... | collective-permute-start | bytes 1474568 | tf_op jit(solution)/shard_map/ppermute | solution.py:28
  36.3 0.1 collective-permute-start.10
  36.5 0.0 collective-permute-done.2.far
  36.5 5.4 %collective-permute-done.3.cross = f32[2,24,1536]{2,1,0:T(8,128)S(1)} collective-permute-done((f32[2,24,1536]{2,1,0:T(8,128)S(1)}, f32[2,24,1536]{2,1,0:T(8,128)S(1)}, u32[]{:S(2)}, u32[]{:S(2)}) %collective-permute-start.3) | collective-permute-done | bytes 294944 | tf_op jit(solution)/shard_map/ppermute | solution.py:28
  41.8 2.7 %shard_map.63 = (f32[2,24,1536]{2,1,0:T(8,128)}, f32[2,24,1536]{2,1,0:T(8,128)S(1)}, f32[2,24,4096]{2,1,0:T(8,128)S(1)}, f32[24,128]{1,0:T(8,128)S(1)}, f32[2,96,4096]{2,1,0:T(8,128)}, /*index=5*/f32[1,128]{1,0:T(1,128)S(1)}) custom-call(f32[2,24,4096]{2,1,0:T(8,128)S(1)} %get-tuple-element.28.own, ...), custom_call_target="tpu_custom_call", output_to_operand_aliasing={{2}: (8, {}), {3}: (9, {}), {4}: (10, {})} | custom-call | flops 14745600000 | bytes 2949120 | tf_op jit(solution)/shard_map/pallas_call | solution.py:162
  44.6 0.6 broadcast_in_dim.24
  45.2 8.1 %all-to-all-start = ((f32[32,1,128]{2,1,0:T(1,128)}), f32[32,1,128]{2,1,0:T(1,128)S(1)}, u32[]{:S(2)}, u32[]{:S(2)}) async-start(f32[32,1,128]{2,1,0:T(1,128)} %broadcast_in_dim.24), calls=%async_computation | async-start | bytes 32768 | tf_op jit(solution)/shard_map/all_to_all | solution.py:205
  53.3 3.4 %collective-permute-start.6 = (f32[2,24,1536]{2,1,0:T(8,128)}, f32[2,24,1536]{2,1,0:T(8,128)S(1)}, u32[]{:S(2)}, u32[]{:S(2)}) collective-permute-start(f32[2,24,1536]{2,1,0:T(8,128)} %get-tuple-element.35), channel_id=1, source_target_pairs={{0,64},{1,65},{2,66},{3,67},{4,68},{5,69},{6,70},{7,71},{8,72},{9,... | collective-permute-start | bytes 884744 | tf_op jit(solution)/shard_map/ppermute | solution.py:28
  56.6 0.0 collective-permute-start.7
  56.7 0.5 collective-permute-start.8
  57.1 4.7 %all-to-all-done.refs_3_ = f32[32,1,128]{2,1,0:T(1,128)S(1)} async-done(((f32[32,1,128]{2,1,0:T(1,128)}), f32[32,1,128]{2,1,0:T(1,128)S(1)}, u32[]{:S(2)}, u32[]{:S(2)}) %all-to-all-start) | async-done | bytes 16416 | tf_op jit(solution)/shard_map/all_to_all | solution.py:205
  61.8 0.0 collective-permute-done.9.refs_0_
  61.8 1.4 %collective-permute-done.10.refs_1_ = f32[2,24,2560]{2,1,0:T(8,128)} collective-permute-done((f32[2,24,2560]{2,1,0:T(8,128)S(1)}, f32[2,24,2560]{2,1,0:T(8,128)}, u32[]{:S(2)}, u32[]{:S(2)}) %collective-permute-start.10) | collective-permute-done | bytes 491552 | tf_op jit(solution)/shard_map/ppermute | solution.py:28
  63.2 2.0 %shard_map.64 = (f32[2,96,4096]{2,1,0:T(8,128)}, f32[1,128]{1,0:T(1,128)S(1)}) custom-call(f32[2,24,2560]{2,1,0:T(8,128)S(1)} %collective-permute-done.9.refs_0_, f32[2,24,2560]{2,1,0:T(8,128)} %collective-permute-done.10.refs_1_, f32[2,96,4096]{2,1,0:T(8,128)} %get-tuple-element.40.refs_2_, ...), custom_call_target="tpu_custom_call", output_to_operand_aliasing={{0}: (2, {})} | custom-call | flops 40000000000 | bytes 1966080 | tf_op jit(solution)/shard_map/pallas_call | solution.py:87
  65.2 1.7 %collective-permute-start.13 = (f32[1,128]{1,0:T(1,128)S(1)}, f32[1,128]{1,0:T(1,128)S(1)}, u32[]{:S(2)}, u32[]{:S(2)}) collective-permute-start(f32[1,128]{1,0:T(1,128)S(1)} %get-tuple-element.43.refs_4_), channel_id=1, source_target_pairs={{0,32},{1,33},{2,34},{3,35},{4,36},{5,37},{6,38},{7,39},{8,40},{9,... | collective-permute-start | bytes 1544 | tf_op jit(solution)/shard_map/ppermute | solution.py:28
  66.9 2.1 %collective-permute-start.12 = (f32[1,128]{1,0:T(1,128)S(1)}, f32[1,128]{1,0:T(1,128)S(1)}, u32[]{:S(2)}, u32[]{:S(2)}) collective-permute-start(f32[1,128]{1,0:T(1,128)S(1)} %get-tuple-element.43.refs_4_), channel_id=1, source_target_pairs={{0,96},{1,97},{2,98},{3,99},{4,100},{5,101},{6,102},{7,103},{8,104... | collective-permute-start | bytes 1544 | tf_op jit(solution)/shard_map/ppermute | solution.py:28
  68.9 0.0 collective-permute-done.8.refs_0_
  68.9 0.9 %collective-permute-start.11 = (f32[1,128]{1,0:T(1,128)S(1)}, f32[1,128]{1,0:T(1,128)S(1)}, u32[]{:S(2)}, u32[]{:S(2)}) collective-permute-start(f32[1,128]{1,0:T(1,128)S(1)} %get-tuple-element.43.refs_4_), channel_id=1, source_target_pairs={{0,64},{1,65},{2,66},{3,67},{4,68},{5,69},{6,70},{7,71},{8,72},{9,... | collective-permute-start | bytes 1544 | tf_op jit(solution)/shard_map/ppermute | solution.py:28
  69.8 0.9 %shard_map.65.refs_2_ = f32[2,96,4096]{2,1,0:T(8,128)} custom-call(f32[2,24,4096]{2,1,0:T(8,128)S(1)} %collective-permute-done.8.refs_0_, f32[2,96,4096]{2,1,0:T(8,128)} %get-tuple-element.42.refs_1_), custom_call_target="tpu_custom_call", output_to_operand_aliasing={{}: (1, {})} | custom-call | bytes 1572864 | tf_op jit(solution)/shard_map/pallas_call | solution.py:87
  70.7 0.0 collective-permute-done.6.refs_0_
  70.8 4.1 %collective-permute-done.7.refs_1_ = f32[2,24,1536]{2,1,0:T(8,128)S(1)} collective-permute-done((f32[2,24,1536]{2,1,0:T(8,128)S(1)}, f32[2,24,1536]{2,1,0:T(8,128)S(1)}, u32[]{:S(2)}, u32[]{:S(2)}) %collective-permute-start.7) | collective-permute-done | bytes 294944 | tf_op jit(solution)/shard_map/ppermute | solution.py:28
  74.9 0.0 collective-permute-done.13.refs_7_
  74.9 0.1 collective-permute-done.12.refs_6_
  75.0 0.0 collective-permute-done.11.refs_5_
  75.0 0.8 %shard_map.66 = (f32[2,96,4096]{2,1,0:T(8,128)}, f32[1,96]{1,0:T(1,128)}) custom-call(f32[2,24,1536]{2,1,0:T(8,128)S(1)} %collective-permute-done.6.refs_0_, f32[2,24,1536]{2,1,0:T(8,128)S(1)} %collective-permute-done.7.refs_1_, f32[2,96,4096]{2,1,0:T(8,128)} %shard_map.65.refs_2_, f32[1,96]{1,0:T(1,128)S(1)} %bitcast.4, ...), custom_call_target="tpu_custom_call", output_to_operand_aliasing={{0}: (2, {})} | custom-call | bytes 1179648 | tf_op jit(solution)/shard_map/pallas_call | solution.py:87
Async XLA Ops:
  1.8 15.5 %collective-permute-start.4 = (f32[2,24,2560]{2,1,0:T(8,128)S(1)}, f32[2,24,2560]{2,1,0:T(8,128)S(1)}, u32[]{:S(2)}, u32[]{:S(2)}) collective-permute-start(f32[2,24,2560]{2,1,0:T(8,128)S(1)} %get-tuple-element.24.refs_1_), channel_id=1, source_target_pairs={{0,64},{1,65},{2,66},{3,67},{4,68},{5,69},{6,70},{7,71},{8,72},{9,... | collective-permute-start | bytes 1474568 | tf_op jit(solution)/shard_map/ppermute | solution.py:28
  6.4 22.8 %collective-permute-start.5 = (f32[2,24,2560]{2,1,0:T(8,128)S(1)}, f32[2,24,2560]{2,1,0:T(8,128)S(1)}, u32[]{:S(2)}, u32[]{:S(2)}) collective-permute-start(f32[2,24,2560]{2,1,0:T(8,128)S(1)} %get-tuple-element.25.refs_2_), channel_id=1, source_target_pairs={{0,96},{1,97},{2,98},{3,99},{4,100},{5,101},{6,102},{7,103},{8,104... | collective-permute-start | bytes 1474568 | tf_op jit(solution)/shard_map/ppermute | solution.py:28
  8.1 21.1 %copy-start = (f32[96]{0:T(128)S(1)}, f32[96]{0:T(128)}, u32[]{:S(2)}) copy-start(f32[96]{0:T(128)} %param.7) | copy-start | bytes 1156
  8.1 21.2 %copy-start.1 = (f32[4096]{0:T(1024)S(1)}, f32[4096]{0:T(1024)}, u32[]{:S(2)}) copy-start(f32[4096]{0:T(1024)} %param.6) | copy-start | bytes 49156
  9.6 3.8 %collective-permute-start = (f32[1,24,4096]{2,1,0:T(8,128)S(1)}, f32[1,24,4096]{2,1,0:T(8,128)S(1)}, u32[]{:S(2)}, u32[]{:S(2)}) collective-permute-start(f32[1,24,4096]{2,1,0:T(8,128)S(1)} %get-tuple-element.29), channel_id=1, source_target_pairs={{0,32},{1,33},{2,34},{3,35},{4,36},{5,37},{6,38},{7,39},{8,40},{9,... | collective-permute-start | bytes 1179656 | tf_op jit(solution)/shard_map/ppermute | solution.py:28
  10.0 4.6 %collective-permute-start.1 = (f32[1,24,4096]{2,1,0:T(8,128)S(1)}, f32[1,24,4096]{2,1,0:T(8,128)S(1)}, u32[]{:S(2)}, u32[]{:S(2)}) collective-permute-start(f32[1,24,4096]{2,1,0:T(8,128)S(1)} %get-tuple-element.30), channel_id=1, source_target_pairs={{0,32},{1,33},{2,34},{3,35},{4,36},{5,37},{6,38},{7,39},{8,40},{9,... | collective-permute-start | bytes 1179656 | tf_op jit(solution)/shard_map/ppermute | solution.py:28
  10.2 26.2 %collective-permute-start.2 = (f32[2,24,1536]{2,1,0:T(8,128)S(1)}, f32[2,24,1536]{2,1,0:T(8,128)S(1)}, u32[]{:S(2)}, u32[]{:S(2)}) collective-permute-start(f32[2,24,1536]{2,1,0:T(8,128)S(1)} %get-tuple-element.26.refs_2_), channel_id=1, source_target_pairs={{0,64},{1,65},{2,66},{3,67},{4,68},{5,69},{6,70},{7,71},{8,72},{9,... | collective-permute-start | bytes 884744 | tf_op jit(solution)/shard_map/ppermute | solution.py:28
  13.4 28.4 %collective-permute-start.3 = (f32[2,24,1536]{2,1,0:T(8,128)S(1)}, f32[2,24,1536]{2,1,0:T(8,128)S(1)}, u32[]{:S(2)}, u32[]{:S(2)}) collective-permute-start(f32[2,24,1536]{2,1,0:T(8,128)S(1)} %get-tuple-element.27.refs_3_), channel_id=1, source_target_pairs={{0,96},{1,97},{2,98},{3,99},{4,100},{5,101},{6,102},{7,103},{8,104... | collective-permute-start | bytes 884744 | tf_op jit(solution)/shard_map/ppermute | solution.py:28
  33.0 28.8 %collective-permute-start.9 = (f32[2,24,2560]{2,1,0:T(8,128)}, f32[2,24,2560]{2,1,0:T(8,128)S(1)}, u32[]{:S(2)}, u32[]{:S(2)}) collective-permute-start(f32[2,24,2560]{2,1,0:T(8,128)} %get-tuple-element.38), channel_id=1, source_target_pairs={{0,64},{1,65},{2,66},{3,67},{4,68},{5,69},{6,70},{7,71},{8,72},{9,... | collective-permute-start | bytes 1474568 | tf_op jit(solution)/shard_map/ppermute | solution.py:28
  36.3 26.8 %collective-permute-start.10 = (f32[2,24,2560]{2,1,0:T(8,128)S(1)}, f32[2,24,2560]{2,1,0:T(8,128)}, u32[]{:S(2)}, u32[]{:S(2)}) collective-permute-start(f32[2,24,2560]{2,1,0:T(8,128)S(1)} %get-tuple-element.39), channel_id=1, source_target_pairs={{0,96},{1,97},{2,98},{3,99},{4,100},{5,101},{6,102},{7,103},{8,104... | collective-permute-start | bytes 1474568 | tf_op jit(solution)/shard_map/ppermute | solution.py:28
  45.2 16.6 %all-to-all-start = ((f32[32,1,128]{2,1,0:T(1,128)}), f32[32,1,128]{2,1,0:T(1,128)S(1)}, u32[]{:S(2)}, u32[]{:S(2)}) async-start(f32[32,1,128]{2,1,0:T(1,128)} %broadcast_in_dim.24), calls=%async_computation | async-start | bytes 32768 | tf_op jit(solution)/shard_map/all_to_all | solution.py:205
  53.3 17.5 %collective-permute-start.6 = (f32[2,24,1536]{2,1,0:T(8,128)}, f32[2,24,1536]{2,1,0:T(8,128)S(1)}, u32[]{:S(2)}, u32[]{:S(2)}) collective-permute-start(f32[2,24,1536]{2,1,0:T(8,128)} %get-tuple-element.35), channel_id=1, source_target_pairs={{0,64},{1,65},{2,66},{3,67},{4,68},{5,69},{6,70},{7,71},{8,72},{9,... | collective-permute-start | bytes 884744 | tf_op jit(solution)/shard_map/ppermute | solution.py:28
  56.6 18.3 %collective-permute-start.7 = (f32[2,24,1536]{2,1,0:T(8,128)S(1)}, f32[2,24,1536]{2,1,0:T(8,128)S(1)}, u32[]{:S(2)}, u32[]{:S(2)}) collective-permute-start(f32[2,24,1536]{2,1,0:T(8,128)S(1)} %get-tuple-element.36), channel_id=1, source_target_pairs={{0,96},{1,97},{2,98},{3,99},{4,100},{5,101},{6,102},{7,103},{8,104... | collective-permute-start | bytes 884744 | tf_op jit(solution)/shard_map/ppermute | solution.py:28
  56.7 12.3 %collective-permute-start.8 = (f32[2,24,4096]{2,1,0:T(8,128)S(1)}, f32[2,24,4096]{2,1,0:T(8,128)S(1)}, u32[]{:S(2)}, u32[]{:S(2)}) collective-permute-start(f32[2,24,4096]{2,1,0:T(8,128)S(1)} %get-tuple-element.37), channel_id=1, source_target_pairs={{0,32},{1,33},{2,34},{3,35},{4,36},{5,37},{6,38},{7,39},{8,40},{9,... | collective-permute-start | bytes 2359304 | tf_op jit(solution)/shard_map/ppermute | solution.py:28
  65.2 9.7 %collective-permute-start.13 = (f32[1,128]{1,0:T(1,128)S(1)}, f32[1,128]{1,0:T(1,128)S(1)}, u32[]{:S(2)}, u32[]{:S(2)}) collective-permute-start(f32[1,128]{1,0:T(1,128)S(1)} %get-tuple-element.43.refs_4_), channel_id=1, source_target_pairs={{0,32},{1,33},{2,34},{3,35},{4,36},{5,37},{6,38},{7,39},{8,40},{9,... | collective-permute-start | bytes 1544 | tf_op jit(solution)/shard_map/ppermute | solution.py:28
  66.9 8.1 %collective-permute-start.12 = (f32[1,128]{1,0:T(1,128)S(1)}, f32[1,128]{1,0:T(1,128)S(1)}, u32[]{:S(2)}, u32[]{:S(2)}) collective-permute-start(f32[1,128]{1,0:T(1,128)S(1)} %get-tuple-element.43.refs_4_), channel_id=1, source_target_pairs={{0,96},{1,97},{2,98},{3,99},{4,100},{5,101},{6,102},{7,103},{8,104... | collective-permute-start | bytes 1544 | tf_op jit(solution)/shard_map/ppermute | solution.py:28
  68.9 6.0 %collective-permute-start.11 = (f32[1,128]{1,0:T(1,128)S(1)}, f32[1,128]{1,0:T(1,128)S(1)}, u32[]{:S(2)}, u32[]{:S(2)}) collective-permute-start(f32[1,128]{1,0:T(1,128)S(1)} %get-tuple-element.43.refs_4_), channel_id=1, source_target_pairs={{0,64},{1,65},{2,66},{3,67},{4,68},{5,69},{6,70},{7,71},{8,72},{9,... | collective-permute-start | bytes 1544 | tf_op jit(solution)/shard_map/ppermute | solution.py:28

commit v5 on v4

--- a/solution.py
+++ b/solution.py
@@ -100,8 +100,8 @@
     total[...] = jnp.sum(rows[:, 0, :], axis=0, keepdims=True)
 
 
-def weigh(count, pen, own, far, cross, near, loss):
-    total = own[...] + far[...] + cross[...] + near[...]
+def weigh(count, pen, own, near, loss):
+    total = own[...] + near[...]
     loss[...] = pen[...] * total[:, :pen.shape[1]] / count
 
 
@@ -199,20 +199,22 @@
         d_far, d_cross, *before, sums = score(
             scale, 1.0 / samples, start, width, x.shape, own, near, far[c], cross[c], truth, lat[None, :], pen_lanes, *before
         )
-        back.append([(FAR, start, width, exchange(d_far, FAR)), (CROSS, start, width, exchange(d_cross, CROSS))])
+        back.append([(CROSS, start, width, exchange(d_cross, CROSS)), (FAR, start, width, exchange(d_far, FAR))])
     d_near, loss, out = before
     back.insert(1, [(NEAR, 0, points, exchange(d_near, NEAR))])
-    everyone = lax.all_to_all(jnp.broadcast_to(sums[None], (spaces,) + sums.shape), "space", 0, 0)
+    cores = [[m * spaces + s for m in range(core, members, 2) for s in range(spaces)] for core in range(2)]
+    copies = jnp.broadcast_to(sums[None], (len(cores[0]),) + sums.shape)
+    everyone = lax.all_to_all(copies, AXES, 0, 0, axis_index_groups=cores)
 
     def put(group, *job):
         return place([g[:3] for g in group], quarter, [g[3] for g in group], out, *job)
 
     out, sums = put(back[0], PLACING, add_rows, (everyone,), sums.shape)
-    rows = [exchange(sums, f) for f in (FAR, CROSS, NEAR)]
+    near_sums = exchange(sums, NEAR)
     out, = put(back[1])
     pen_row = pen[None, :]
     out, field_loss = put(
-        back[2], 0, functools.partial(weigh, points * spaces), (pen_row, sums, *rows), pen_row.shape
+        back[2], 0, functools.partial(weigh, points * spaces), (pen_row, sums, near_sums), pen_row.shape
     )
     return out, field_loss[0]
 

time: 76.1 us -> 75.6 us (level)
  starting transfers between devices: 30.3 us -> 28.4 us
  waiting for transfers between devices: 30.2 us -> 31.6 us
    ppermute x14 -> x12, starting transfers between devices: 22.2 us -> 17.6 us  [exchange(): return lax.ppermute(block, AXES, pairs)]
    all_to_all x1, starting transfers between devices: 8.08 us -> 10.8 us  [shards(): everyone = lax.all_to_all(copies, AXES, 0, 0, axis_index_groups=cores)]
    ppermute x14 -> x12, waiting for transfers between devices: 25.5 us -> 26.9 us  [exchange(): return lax.ppermute(block, AXES, pairs)]
  transfers between devices with their start and end apart: 15 -> 13, of which waited for: 7 -> 6; matrix products, arithmetic and copies ran while one was open for 1% -> 1% of each run, Pallas kernels for 16% -> 16%
where the time goes in v5:
time: 75.6 us; the launch traced here: 75.4 us
  waiting for transfers between devices  31.6 us (42%)
  starting transfers between devices  28.4 us (38%)
  Pallas kernels  13.9 us (18%)
    ppermute x12, waiting for transfers between devices, exchange(): return lax.ppermute(block, AXES, pairs)  26.9 us
    ppermute x12, starting transfers between devices, exchange(): return lax.ppermute(block, AXES, pairs)  17.6 us
    all_to_all x1, starting transfers between devices, shards(): everyone = lax.all_to_all(copies, AXES, 0, 0, axis_index_groups=cores)  10.8 us
    pallas_call x2, Pallas kernels, score(): pl.pallas_call(functools.partial(score_kernel, scale, weight, start, len(...  6.4 us
    all_to_all x1, waiting for transfers between devices, shards(): everyone = lax.all_to_all(copies, AXES, 0, 0, axis_index_groups=cores)  4.72 us
    pallas_call x3, Pallas kernels, take(): pl.pallas_call(functools.partial(take_kernel, specs, quarter, len(arrays)...  3.8 us
    pallas_call x3, Pallas kernels, place(): pl.pallas_call(functools.partial(place_kernel, specs, quarter, job, len(m...  3.74 us
  transfers between devices with their start and end apart: 13, of which 6 were waited for; matrix products, arithmetic and copies ran while one was open for 1% of the time, Pallas kernels for 16%

profile of v5, /device:TPU:1, one launch (start us, length us, event | category | flops | bytes accessed | tf_op | source)
XLA Modules:
  0.0 75.4 jit_solution(8403251845597804611)
XLA Ops:
  0.6 1.2 %shard_map.59 = (f32[2,24,2560]{2,1,0:T(8,128)S(1)}, f32[2,24,2560]{2,1,0:T(8,128)S(1)}) custom-call(f32[2,96,4096]{2,1,0:T(8,128)} %refs_0_.5), custom_call_target="tpu_custom_call" | custom-call | bytes 1966080 | tf_op jit(solution)/shard_map/pallas_call | solution.py:58
  1.8 4.5 %collective-permute-start.4 = (f32[2,24,2560]{2,1,0:T(8,128)S(1)}, f32[2,24,2560]{2,1,0:T(8,128)S(1)}, u32[]{:S(2)}, u32[]{:S(2)}) collective-permute-start(f32[2,24,2560]{2,1,0:T(8,128)S(1)} %get-tuple-element.24.refs_1_), channel_id=1, source_target_pairs={{0,64},{1,65},{2,66},{3,67},{4,68},{5,69},{6,70},{7,71},{8,72},{9,... | collective-permute-start | bytes 1474568 | tf_op jit(solution)/shard_map/ppermute | solution.py:28
  6.4 0.7 collective-permute-start.5
  7.0 1.1 %shard_map.60 = (f32[2,24,1536]{2,1,0:T(8,128)S(1)}, f32[2,24,1536]{2,1,0:T(8,128)S(1)}) custom-call(f32[2,96,4096]{2,1,0:T(8,128)} %refs_0_.5, f32[2,24,2560]{2,1,0:T(8,128)S(1)} %get-tuple-element.24.refs_1_, f32[2,24,2560]{2,1,0:T(8,128)S(1)} %get-tuple-element.25.refs_2_), custom_call_target="tpu_custom_call" | custom-call | bytes 1179648 | tf_op jit(solution)/shard_map/pallas_call | solution.py:58
  8.1 0.0 copy-start
  8.1 0.0 copy-start.1
  8.1 1.5 %shard_map.61 = (f32[1,24,4096]{2,1,0:T(8,128)S(1)}, f32[1,24,4096]{2,1,0:T(8,128)S(1)}, f32[2,24,4096]{2,1,0:T(8,128)S(1)}, f32[24,4096]{1,0:T(8,128)S(1)}) custom-call(f32[2,96,4096]{2,1,0:T(8,128)} %refs_0_.5, f32[96,4096]{1,0:T(8,128)} %refs_1_.1, f32[2,24,1536]{2,1,0:T(8,128)S(1)} %get-tuple-element.26.refs_2_, f32[2,24,1536]{2,1,0:T(8,128)S(1)} %get-tuple-element.27.refs_3_), custom_call_target="tpu_custom_call" | custom-call | bytes 3932160 | tf_op jit(solution)/shard_map/pallas_call | solution.py:58
  9.6 0.4 collective-permute-start
  10.0 0.2 collective-permute-start.1
  10.2 3.2 %collective-permute-start.2 = (f32[2,24,1536]{2,1,0:T(8,128)S(1)}, f32[2,24,1536]{2,1,0:T(8,128)S(1)}, u32[]{:S(2)}, u32[]{:S(2)}) collective-permute-start(f32[2,24,1536]{2,1,0:T(8,128)S(1)} %get-tuple-element.26.refs_2_), channel_id=1, source_target_pairs={{0,64},{1,65},{2,66},{3,67},{4,68},{5,69},{6,70},{7,71},{8,72},{9,... | collective-permute-start | bytes 884744 | tf_op jit(solution)/shard_map/ppermute | solution.py:28
  13.4 0.0 collective-permute-done.near_0
  13.4 1.2 %collective-permute-start.3 = (f32[2,24,1536]{2,1,0:T(8,128)S(1)}, f32[2,24,1536]{2,1,0:T(8,128)S(1)}, u32[]{:S(2)}, u32[]{:S(2)}) collective-permute-start(f32[2,24,1536]{2,1,0:T(8,128)S(1)} %get-tuple-element.27.refs_3_), channel_id=1, source_target_pairs={{0,96},{1,97},{2,98},{3,99},{4,100},{5,101},{6,102},{7,103},{8,104... | collective-permute-start | bytes 884744 | tf_op jit(solution)/shard_map/ppermute | solution.py:28
  14.6 0.0 collective-permute-done.1.near_1
  14.6 2.7 %collective-permute-done.4.far = f32[2,24,2560]{2,1,0:T(8,128)S(1)} collective-permute-done((f32[2,24,2560]{2,1,0:T(8,128)S(1)}, f32[2,24,2560]{2,1,0:T(8,128)S(1)}, u32[]{:S(2)}, u32[]{:S(2)}) %collective-permute-start.4) | collective-permute-done | bytes 491552 | tf_op jit(solution)/shard_map/ppermute | solution.py:28
  17.3 11.9 %collective-permute-done.5.cross = f32[2,24,2560]{2,1,0:T(8,128)S(1)} collective-permute-done((f32[2,24,2560]{2,1,0:T(8,128)S(1)}, f32[2,24,2560]{2,1,0:T(8,128)S(1)}, u32[]{:S(2)}, u32[]{:S(2)}) %collective-permute-start.5) | collective-permute-done | bytes 491552 | tf_op jit(solution)/shard_map/ppermute | solution.py:28
  29.2 0.0 copy-done
  29.2 0.1 broadcast_in_dim.22.pen
  29.3 0.0 copy-done.1
  29.3 3.7 %shard_map.62 = (f32[2,24,2560]{2,1,0:T(8,128)S(1)}, f32[2,24,2560]{2,1,0:T(8,128)}, f32[2,24,4096]{2,1,0:T(8,128)S(1)}, f32[24,128]{1,0:T(8,128)S(1)}, f32[2,96,4096]{2,1,0:T(8,128)}, /*index=5*/f32[1,128]{1,0:T(1,128)}) custom-call(f32[2,24,4096]{2,1,0:T(8,128)S(1)} %get-tuple-element.28.own, f32[1,24,4096]{2,1,0:T(8,128)S(1)} %collective-permute-done.near_0, ...), custom_call_target="tpu_custom_call" | custom-call | flops 24576000000 | bytes 4915200 | tf_op jit(solution)/shard_map/pallas_call | solution.py:162
  33.0 1.6 %collective-permute-start.9 = (f32[2,24,2560]{2,1,0:T(8,128)}, f32[2,24,2560]{2,1,0:T(8,128)S(1)}, u32[]{:S(2)}, u32[]{:S(2)}) collective-permute-start(f32[2,24,2560]{2,1,0:T(8,128)} %get-tuple-element.38), channel_id=1, source_target_pairs={{0,96},{1,97},{2,98},{3,99},{4,100},{5,101},{6,102},{7,103},{8,104... | collective-permute-start | bytes 1474568 | tf_op jit(solution)/shard_map/ppermute | solution.py:28
  34.6 1.8 %collective-permute-start.10 = (f32[2,24,2560]{2,1,0:T(8,128)S(1)}, f32[2,24,2560]{2,1,0:T(8,128)}, u32[]{:S(2)}, u32[]{:S(2)}) collective-permute-start(f32[2,24,2560]{2,1,0:T(8,128)S(1)} %get-tuple-element.39), channel_id=1, source_target_pairs={{0,64},{1,65},{2,66},{3,67},{4,68},{5,69},{6,70},{7,71},{8,72},{9,... | collective-permute-start | bytes 1474568 | tf_op jit(solution)/shard_map/ppermute | solution.py:28
  36.4 0.0 collective-permute-done.2.far
  36.4 5.7 %collective-permute-done.3.cross = f32[2,24,1536]{2,1,0:T(8,128)S(1)} collective-permute-done((f32[2,24,1536]{2,1,0:T(8,128)S(1)}, f32[2,24,1536]{2,1,0:T(8,128)S(1)}, u32[]{:S(2)}, u32[]{:S(2)}) %collective-permute-start.3) | collective-permute-done | bytes 294944 | tf_op jit(solution)/shard_map/ppermute | solution.py:28
  42.1 2.7 %shard_map.63 = (f32[2,24,1536]{2,1,0:T(8,128)S(1)}, f32[2,24,1536]{2,1,0:T(8,128)}, f32[2,24,4096]{2,1,0:T(8,128)S(1)}, f32[24,128]{1,0:T(8,128)S(1)}, f32[2,96,4096]{2,1,0:T(8,128)}, /*index=5*/f32[1,128]{1,0:T(1,128)S(1)}) custom-call(f32[2,24,4096]{2,1,0:T(8,128)S(1)} %get-tuple-element.28.own, ...), custom_call_target="tpu_custom_call", output_to_operand_aliasing={{2}: (8, {}), {3}: (9, {}), {4}: (10, {})} | custom-call | flops 14745600000 | bytes 2949120 | tf_op jit(solution)/shard_map/pallas_call | solution.py:162
  44.9 0.6 broadcast_in_dim.24
  45.5 10.8 %all-to-all-start = ((f32[64,1,128]{2,1,0:T(1,128)}), f32[64,1,128]{2,1,0:T(1,128)S(1)}, u32[]{:S(2)}, u32[]{:S(2)}) async-start(f32[64,1,128]{2,1,0:T(1,128)} %broadcast_in_dim.24), calls=%async_computation | async-start | bytes 65536 | tf_op jit(solution)/shard_map/all_to_all | solution.py:207
  56.3 1.2 %collective-permute-start.6 = (f32[2,24,1536]{2,1,0:T(8,128)}, f32[2,24,1536]{2,1,0:T(8,128)S(1)}, u32[]{:S(2)}, u32[]{:S(2)}) collective-permute-start(f32[2,24,1536]{2,1,0:T(8,128)} %get-tuple-element.35), channel_id=1, source_target_pairs={{0,96},{1,97},{2,98},{3,99},{4,100},{5,101},{6,102},{7,103},{8,104... | collective-permute-start | bytes 884744 | tf_op jit(solution)/shard_map/ppermute | solution.py:28
  57.6 1.6 %collective-permute-start.7 = (f32[2,24,1536]{2,1,0:T(8,128)S(1)}, f32[2,24,1536]{2,1,0:T(8,128)S(1)}, u32[]{:S(2)}, u32[]{:S(2)}) collective-permute-start(f32[2,24,1536]{2,1,0:T(8,128)S(1)} %get-tuple-element.36), channel_id=1, source_target_pairs={{0,64},{1,65},{2,66},{3,67},{4,68},{5,69},{6,70},{7,71},{8,72},{9,... | collective-permute-start | bytes 884744 | tf_op jit(solution)/shard_map/ppermute | solution.py:28
  59.1 0.9 %collective-permute-start.8 = (f32[2,24,4096]{2,1,0:T(8,128)S(1)}, f32[2,24,4096]{2,1,0:T(8,128)S(1)}, u32[]{:S(2)}, u32[]{:S(2)}) collective-permute-start(f32[2,24,4096]{2,1,0:T(8,128)S(1)} %get-tuple-element.37), channel_id=1, source_target_pairs={{0,32},{1,33},{2,34},{3,35},{4,36},{5,37},{6,38},{7,39},{8,40},{9,... | collective-permute-start | bytes 2359304 | tf_op jit(solution)/shard_map/ppermute | solution.py:28
  60.1 4.7 %all-to-all-done.refs_3_ = f32[64,1,128]{2,1,0:T(1,128)S(1)} async-done(((f32[64,1,128]{2,1,0:T(1,128)}), f32[64,1,128]{2,1,0:T(1,128)S(1)}, u32[]{:S(2)}, u32[]{:S(2)}) %all-to-all-start) | async-done | bytes 32800 | tf_op jit(solution)/shard_map/all_to_all | solution.py:207
  64.8 0.0 collective-permute-done.9.refs_0_
  64.8 0.0 collective-permute-done.10.refs_1_
  64.8 2.0 %shard_map.64 = (f32[2,96,4096]{2,1,0:T(8,128)}, f32[1,128]{1,0:T(1,128)S(1)}) custom-call(f32[2,24,2560]{2,1,0:T(8,128)S(1)} %collective-permute-done.9.refs_0_, f32[2,24,2560]{2,1,0:T(8,128)} %collective-permute-done.10.refs_1_, f32[2,96,4096]{2,1,0:T(8,128)} %get-tuple-element.40.refs_2_, ...), custom_call_target="tpu_custom_call", output_to_operand_aliasing={{0}: (2, {})} | custom-call | flops 40000000000 | bytes 1966080 | tf_op jit(solution)/shard_map/pallas_call | solution.py:87
  66.8 0.3 collective-permute-start.11
  67.1 0.0 collective-permute-done.8.refs_0_
  67.1 0.9 %shard_map.65.refs_2_ = f32[2,96,4096]{2,1,0:T(8,128)} custom-call(f32[2,24,4096]{2,1,0:T(8,128)S(1)} %collective-permute-done.8.refs_0_, f32[2,96,4096]{2,1,0:T(8,128)} %get-tuple-element.42.refs_1_), custom_call_target="tpu_custom_call", output_to_operand_aliasing={{}: (1, {})} | custom-call | bytes 1572864 | tf_op jit(solution)/shard_map/pallas_call | solution.py:87
  68.0 1.6 %collective-permute-done.6.refs_0_ = f32[2,24,1536]{2,1,0:T(8,128)S(1)} collective-permute-done((f32[2,24,1536]{2,1,0:T(8,128)}, f32[2,24,1536]{2,1,0:T(8,128)S(1)}, u32[]{:S(2)}, u32[]{:S(2)}) %collective-permute-start.6) | collective-permute-done | bytes 294944 | tf_op jit(solution)/shard_map/ppermute | solution.py:28
  69.6 5.0 %collective-permute-done.7.refs_1_ = f32[2,24,1536]{2,1,0:T(8,128)S(1)} collective-permute-done((f32[2,24,1536]{2,1,0:T(8,128)S(1)}, f32[2,24,1536]{2,1,0:T(8,128)S(1)}, u32[]{:S(2)}, u32[]{:S(2)}) %collective-permute-start.7) | collective-permute-done | bytes 294944 | tf_op jit(solution)/shard_map/ppermute | solution.py:28
  74.5 0.0 collective-permute-done.11.refs_5_
  74.5 0.8 %shard_map.66 = (f32[2,96,4096]{2,1,0:T(8,128)}, f32[1,96]{1,0:T(1,128)}) custom-call(f32[2,24,1536]{2,1,0:T(8,128)S(1)} %collective-permute-done.6.refs_0_, f32[2,24,1536]{2,1,0:T(8,128)S(1)} %collective-permute-done.7.refs_1_, f32[2,96,4096]{2,1,0:T(8,128)} %shard_map.65.refs_2_, f32[1,96]{1,0:T(1,128)S(1)} %bitcast.4, ...), custom_call_target="tpu_custom_call", output_to_operand_aliasing={{0}: (2, {})} | custom-call | bytes 1179648 | tf_op jit(solution)/shard_map/pallas_call | solution.py:87
Async XLA Ops:
  1.8 15.5 %collective-permute-start.4 = (f32[2,24,2560]{2,1,0:T(8,128)S(1)}, f32[2,24,2560]{2,1,0:T(8,128)S(1)}, u32[]{:S(2)}, u32[]{:S(2)}) collective-permute-start(f32[2,24,2560]{2,1,0:T(8,128)S(1)} %get-tuple-element.24.refs_1_), channel_id=1, source_target_pairs={{0,64},{1,65},{2,66},{3,67},{4,68},{5,69},{6,70},{7,71},{8,72},{9,... | collective-permute-start | bytes 1474568 | tf_op jit(solution)/shard_map/ppermute | solution.py:28
  6.4 22.8 %collective-permute-start.5 = (f32[2,24,2560]{2,1,0:T(8,128)S(1)}, f32[2,24,2560]{2,1,0:T(8,128)S(1)}, u32[]{:S(2)}, u32[]{:S(2)}) collective-permute-start(f32[2,24,2560]{2,1,0:T(8,128)S(1)} %get-tuple-element.25.refs_2_), channel_id=1, source_target_pairs={{0,96},{1,97},{2,98},{3,99},{4,100},{5,101},{6,102},{7,103},{8,104... | collective-permute-start | bytes 1474568 | tf_op jit(solution)/shard_map/ppermute | solution.py:28
  8.1 21.1 %copy-start = (f32[96]{0:T(128)S(1)}, f32[96]{0:T(128)}, u32[]{:S(2)}) copy-start(f32[96]{0:T(128)} %param.7) | copy-start | bytes 1156
  8.1 21.2 %copy-start.1 = (f32[4096]{0:T(1024)S(1)}, f32[4096]{0:T(1024)}, u32[]{:S(2)}) copy-start(f32[4096]{0:T(1024)} %param.6) | copy-start | bytes 49156
  9.6 3.8 %collective-permute-start = (f32[1,24,4096]{2,1,0:T(8,128)S(1)}, f32[1,24,4096]{2,1,0:T(8,128)S(1)}, u32[]{:S(2)}, u32[]{:S(2)}) collective-permute-start(f32[1,24,4096]{2,1,0:T(8,128)S(1)} %get-tuple-element.29), channel_id=1, source_target_pairs={{0,32},{1,33},{2,34},{3,35},{4,36},{5,37},{6,38},{7,39},{8,40},{9,... | collective-permute-start | bytes 1179656 | tf_op jit(solution)/shard_map/ppermute | solution.py:28
  10.0 4.6 %collective-permute-start.1 = (f32[1,24,4096]{2,1,0:T(8,128)S(1)}, f32[1,24,4096]{2,1,0:T(8,128)S(1)}, u32[]{:S(2)}, u32[]{:S(2)}) collective-permute-start(f32[1,24,4096]{2,1,0:T(8,128)S(1)} %get-tuple-element.30), channel_id=1, source_target_pairs={{0,32},{1,33},{2,34},{3,35},{4,36},{5,37},{6,38},{7,39},{8,40},{9,... | collective-permute-start | bytes 1179656 | tf_op jit(solution)/shard_map/ppermute | solution.py:28
  10.2 26.2 %collective-permute-start.2 = (f32[2,24,1536]{2,1,0:T(8,128)S(1)}, f32[2,24,1536]{2,1,0:T(8,128)S(1)}, u32[]{:S(2)}, u32[]{:S(2)}) collective-permute-start(f32[2,24,1536]{2,1,0:T(8,128)S(1)} %get-tuple-element.26.refs_2_), channel_id=1, source_target_pairs={{0,64},{1,65},{2,66},{3,67},{4,68},{5,69},{6,70},{7,71},{8,72},{9,... | collective-permute-start | bytes 884744 | tf_op jit(solution)/shard_map/ppermute | solution.py:28
  13.4 28.7 %collective-permute-start.3 = (f32[2,24,1536]{2,1,0:T(8,128)S(1)}, f32[2,24,1536]{2,1,0:T(8,128)S(1)}, u32[]{:S(2)}, u32[]{:S(2)}) collective-permute-start(f32[2,24,1536]{2,1,0:T(8,128)S(1)} %get-tuple-element.27.refs_3_), channel_id=1, source_target_pairs={{0,96},{1,97},{2,98},{3,99},{4,100},{5,101},{6,102},{7,103},{8,104... | collective-permute-start | bytes 884744 | tf_op jit(solution)/shard_map/ppermute | solution.py:28
  33.0 31.8 %collective-permute-start.9 = (f32[2,24,2560]{2,1,0:T(8,128)}, f32[2,24,2560]{2,1,0:T(8,128)S(1)}, u32[]{:S(2)}, u32[]{:S(2)}) collective-permute-start(f32[2,24,2560]{2,1,0:T(8,128)} %get-tuple-element.38), channel_id=1, source_target_pairs={{0,96},{1,97},{2,98},{3,99},{4,100},{5,101},{6,102},{7,103},{8,104... | collective-permute-start | bytes 1474568 | tf_op jit(solution)/shard_map/ppermute | solution.py:28
  34.6 30.2 %collective-permute-start.10 = (f32[2,24,2560]{2,1,0:T(8,128)S(1)}, f32[2,24,2560]{2,1,0:T(8,128)}, u32[]{:S(2)}, u32[]{:S(2)}) collective-permute-start(f32[2,24,2560]{2,1,0:T(8,128)S(1)} %get-tuple-element.39), channel_id=1, source_target_pairs={{0,64},{1,65},{2,66},{3,67},{4,68},{5,69},{6,70},{7,71},{8,72},{9,... | collective-permute-start | bytes 1474568 | tf_op jit(solution)/shard_map/ppermute | solution.py:28
  45.5 19.3 %all-to-all-start = ((f32[64,1,128]{2,1,0:T(1,128)}), f32[64,1,128]{2,1,0:T(1,128)S(1)}, u32[]{:S(2)}, u32[]{:S(2)}) async-start(f32[64,1,128]{2,1,0:T(1,128)} %broadcast_in_dim.24), calls=%async_computation | async-start | bytes 65536 | tf_op jit(solution)/shard_map/all_to_all | solution.py:207
  56.3 13.2 %collective-permute-start.6 = (f32[2,24,1536]{2,1,0:T(8,128)}, f32[2,24,1536]{2,1,0:T(8,128)S(1)}, u32[]{:S(2)}, u32[]{:S(2)}) collective-permute-start(f32[2,24,1536]{2,1,0:T(8,128)} %get-tuple-element.35), channel_id=1, source_target_pairs={{0,96},{1,97},{2,98},{3,99},{4,100},{5,101},{6,102},{7,103},{8,104... | collective-permute-start | bytes 884744 | tf_op jit(solution)/shard_map/ppermute | solution.py:28
  57.6 17.0 %collective-permute-start.7 = (f32[2,24,1536]{2,1,0:T(8,128)S(1)}, f32[2,24,1536]{2,1,0:T(8,128)S(1)}, u32[]{:S(2)}, u32[]{:S(2)}) collective-permute-start(f32[2,24,1536]{2,1,0:T(8,128)S(1)} %get-tuple-element.36), channel_id=1, source_target_pairs={{0,64},{1,65},{2,66},{3,67},{4,68},{5,69},{6,70},{7,71},{8,72},{9,... | collective-permute-start | bytes 884744 | tf_op jit(solution)/shard_map/ppermute | solution.py:28
  59.1 7.9 %collective-permute-start.8 = (f32[2,24,4096]{2,1,0:T(8,128)S(1)}, f32[2,24,4096]{2,1,0:T(8,128)S(1)}, u32[]{:S(2)}, u32[]{:S(2)}) collective-permute-start(f32[2,24,4096]{2,1,0:T(8,128)S(1)} %get-tuple-element.37), channel_id=1, source_target_pairs={{0,32},{1,33},{2,34},{3,35},{4,36},{5,37},{6,38},{7,39},{8,40},{9,... | collective-permute-start | bytes 2359304 | tf_op jit(solution)/shard_map/ppermute | solution.py:28
  66.8 7.7 %collective-permute-start.11 = (f32[1,128]{1,0:T(1,128)S(1)}, f32[1,128]{1,0:T(1,128)S(1)}, u32[]{:S(2)}, u32[]{:S(2)}) collective-permute-start(f32[1,128]{1,0:T(1,128)S(1)} %get-tuple-element.43.refs_4_), channel_id=1, source_target_pairs={{0,32},{1,33},{2,34},{3,35},{4,36},{5,37},{6,38},{7,39},{8,40},{9,... | collective-permute-start | bytes 1544 | tf_op jit(solution)/shard_map/ppermute | solution.py:28

commit v6 on v5

--- a/solution.py
+++ b/solution.py
@@ -9,7 +9,6 @@
 from jax.sharding import PartitionSpec as P
 
 AXES = ("member", "space")
-SPLIT = 0.625
 LANES = 128
 SUBLANES = 8
 NEAR, FAR, CROSS = 1, 2, 3
@@ -28,9 +27,9 @@
     return lax.ppermute(block, AXES, pairs)
 
 
-def window(ref, flip, quarter, start, width):
-    row = pl.multiple_of((lax.axis_index("member") ^ flip) * quarter, SUBLANES)
-    index = (pl.ds(row, quarter), pl.ds(start, width))
+def window(ref, flip, quarter, first, rows):
+    row = pl.multiple_of((lax.axis_index("member") ^ flip) * quarter + first, SUBLANES)
+    index = (pl.ds(row, rows), slice(None))
     return ref.at[(slice(None),) + index if len(ref.shape) == 3 else index]
 
 
@@ -42,8 +41,8 @@
 def take_kernel(specs, quarter, n_arrays, n_deps, *refs):
     arrays, outs, sems = refs[:n_arrays], refs[n_arrays + n_deps:-1], refs[-1]
     copies = []
-    for i, (which, flip, start, width, *member) in enumerate(specs):
-        source = window(arrays[which], flip, quarter, start, width)
+    for i, (which, flip, first, rows, *member) in enumerate(specs):
+        source = window(arrays[which], flip, quarter, first, rows)
         if member:
             source = source.at[pl.ds(member[0], 1)]
         copies.append(pltpu.make_async_copy(source, outs[i], sems.at[i]))
@@ -54,7 +53,7 @@
 
 
 def take(specs, quarter, arrays, deps=()):
-    shapes = [((1,) if member else arrays[w].shape[:-2]) + (quarter, width) for w, _, _, width, *member in specs]
+    shapes = [((1,) if member else arrays[w].shape[:-2]) + (rows, arrays[w].shape[-1]) for w, _, _, rows, *member in specs]
     return pl.pallas_call(
         functools.partial(take_kernel, specs, quarter, len(arrays), len(deps)),
         out_shape=[jax.ShapeDtypeStruct(s, jnp.float32) for s in shapes],
@@ -69,8 +68,8 @@
 def place_kernel(specs, quarter, job, n_more, *refs):
     pieces, more, outs, sems = refs[:len(specs)], refs[len(specs) + 1:][:n_more], refs[len(specs) + 1 + n_more:-1], refs[-1]
     copies = []
-    for i, (flip, start, width) in enumerate(specs):
-        copies.append(pltpu.make_async_copy(pieces[i], window(outs[0], flip, quarter, start, width), sems.at[i]))
+    for i, (flip, first, rows) in enumerate(specs):
+        copies.append(pltpu.make_async_copy(pieces[i], window(outs[0], flip, quarter, first, rows), sems.at[i]))
     for copy in copies:
         copy.start()
     if job is not None:
@@ -105,26 +104,31 @@
     loss[...] = pen[...] * total[:, :pen.shape[1]] / count
 
 
-def score_kernel(scale, weight, start, n_before, own, near_0, near_1, far, cross, truth, lat, pen, *refs):
+def score_kernel(scale, weight, first, n_before, own, near_0, near_1, far, cross, truth, lat, pen, *refs):
     before, refs = refs[:n_before], refs[n_before:]
     d_far, d_cross, d_near, loss, out, row_sums, d_own, sems = refs
+    quarter = d_near.shape[1]
     rows, cols = d_far.shape[1:]
-    sources = ((own, 0, start), (own, 1, start), (near_0, 0, start), (near_1, 0, start), (far, 0, 0), (far, 1, 0), (cross, 0, 0), (cross, 1, 0))
-    targets = ((d_own, 0), (d_near, start), (d_far, 0), (d_cross, 0))
-    homes = ((d_own, window(out, 0, rows, start, cols)),)
+    sources = ((own, 0, first), (own, 1, first), (near_0, 0, first), (near_1, 0, first), (far, 0, 0), (far, 1, 0), (cross, 0, 0), (cross, 1, 0))
+    targets = ((d_own, 0), (d_near, first), (d_far, 0), (d_cross, 0))
+    homes = ((d_own, window(out, 0, quarter, first, rows)),)
+    if before:
+        d_near[:, :first, :] = before[0][:, :first, :]
+        loss[:first, :] = before[1][:first, :]
+    else:
+        loss[...] = jnp.zeros_like(loss)
     copies = []
     for row in range(0, rows, SUBLANES):
-        r = pl.ds(row, SUBLANES)
-        penalty = pen[pl.ds(pl.multiple_of(lax.axis_index("member") * rows + row, SUBLANES), SUBLANES), :]
+        r, q = pl.ds(row, SUBLANES), pl.ds(first + row, SUBLANES)
+        field = lax.axis_index("member") * quarter + first + row
+        penalty = pen[pl.ds(pl.multiple_of(field, SUBLANES), SUBLANES), :]
 
         def step(i, total):
-            def at(shift):
-                return pl.ds(pl.multiple_of(i * LANES + shift, LANES), LANES)
-
-            x = [ref[k, r, at(shift)] for ref, k, shift in sources]
+            c = pl.ds(pl.multiple_of(i * LANES, LANES), LANES)
+            x = [ref[k, pl.ds(shift + row, SUBLANES), c] for ref, k, shift in sources]
             n = len(x)
-            y = truth[r, at(start)]
-            area = jnp.broadcast_to(lat[:, at(start)], (SUBLANES, LANES))
+            y = truth[q, c]
+            area = jnp.broadcast_to(lat[:, c], (SUBLANES, LANES))
             signs = [None] * n
             for a in range(n):
                 for b in range(a + 1, n):
@@ -138,29 +142,27 @@
                 g = jnp.where(e > 0.0, weight, jnp.where(e < 0.0, -weight, 0.0)) - scale * signs[j]
                 score = score + e * g
                 target, shift = targets[j // 2]
-                target[j % 2, r, at(shift)] = factor * g
+                target[j % 2, pl.ds(shift + row, SUBLANES), c] = factor * g
             return total + area * score
 
-        total = before[1][r, :] if before else jnp.zeros((SUBLANES, LANES), jnp.float32)
-        total = lax.fori_loop(0, cols // LANES, step, total, unroll=2)
-        loss[r, :] = total
+        loss[q, :] = lax.fori_loop(0, cols // LANES, step, jnp.zeros((SUBLANES, LANES), jnp.float32), unroll=2)
         for i, (source, home) in enumerate(homes):
             copies.append(pltpu.make_async_copy(source.at[:, r], home.at[:, r], sems.at[i, row // SUBLANES]))
             copies[-1].start()
     sums = jnp.sum(loss[...], axis=1, keepdims=True)
-    field = lax.axis_index("member") * rows + lax.broadcasted_iota(jnp.int32, loss.shape, 0)
+    field = lax.axis_index("member") * quarter + lax.broadcasted_iota(jnp.int32, loss.shape, 0)
     here = lax.broadcasted_iota(jnp.int32, loss.shape, 1) == field
     row_sums[...] = jnp.sum(jnp.where(here, sums, 0.0), axis=0, keepdims=True)
     for copy in copies:
         copy.wait()
 
 
-def score(scale, weight, start, width, shape, own, near, far, cross, truth, lat, pen, *before):
+def score(scale, weight, first, rows, shape, own, near, far, cross, truth, lat, pen, *before):
     members, quarter = own.shape[:2]
-    block = (members, quarter, width)
+    block = (members, rows, own.shape[2])
     shapes = (own.shape, (quarter, LANES), shape, (1, LANES))
     return pl.pallas_call(
-        functools.partial(score_kernel, scale, weight, start, len(before)),
+        functools.partial(score_kernel, scale, weight, first, len(before)),
         out_shape=[jax.ShapeDtypeStruct(s, jnp.float32) for s in (block, block) + shapes],
         in_specs=[VMEM] * 8 + [VMEM, VMEM, HBM][:len(before)],
         out_specs=[VMEM, VMEM, VMEM, VMEM, HBM, VMEM],
@@ -168,7 +170,7 @@
         input_output_aliases={8: 2, 9: 3, 10: 4} if before else {},
         compiler_params=pltpu.CompilerParams(vmem_limit_bytes=LARGE),
         cost_estimate=pl.CostEstimate(
-            flops=WORK * quarter * width, bytes_accessed=20 * quarter * width * 4, transcendentals=0
+            flops=WORK * math.prod(block[1:]), bytes_accessed=80 * math.prod(block[1:]), transcendentals=0
         ),
     )(own, *near, far, cross, truth, lat, pen, *before)
 
@@ -180,14 +182,14 @@
     fields, points = y.shape
     scale = (1.0 - 0.05 / samples) / (samples * (samples - 1))
     quarter = fields // members
-    first = int(points * SPLIT)
-    chunks = ((0, first), (first, points - first))
-
-    far_cross = [[(0, FAR, start, width), (0, CROSS, start, width)] for start, width in chunks]
+    split = quarter * 2 // 3 // SUBLANES * SUBLANES
+    chunks = ((0, split), (split, quarter - split))
+
+    far_cross = [[(0, FAR, *chunk), (0, CROSS, *chunk)] for chunk in chunks]
     first_sent = take(far_cross[0], quarter, [x])
     second_sent = take(far_cross[1], quarter, [x], first_sent)
     *to_near, own, truth = take(
-        [(0, NEAR, 0, points, 0), (0, NEAR, 0, points, 1), (0, 0, 0, points), (1, 0, 0, points)], quarter, [x, y], second_sent
+        [(0, NEAR, 0, quarter, 0), (0, NEAR, 0, quarter, 1), (0, 0, 0, quarter), (1, 0, 0, quarter)], quarter, [x, y], second_sent
     )
     sent = (first_sent, second_sent)
     far = [exchange(pair[0], FAR) for pair in sent]
@@ -195,13 +197,13 @@
     near = [exchange(piece, NEAR) for piece in to_near]
     pen_lanes = jnp.broadcast_to(pen[:, None], (fields, LANES))
     back, before = [], ()
-    for c, (start, width) in enumerate(chunks):
+    for c, chunk in enumerate(chunks):
         d_far, d_cross, *before, sums = score(
-            scale, 1.0 / samples, start, width, x.shape, own, near, far[c], cross[c], truth, lat[None, :], pen_lanes, *before
+            scale, 1.0 / samples, *chunk, x.shape, own, near, far[c], cross[c], truth, lat[None, :], pen_lanes, *before
         )
-        back.append([(CROSS, start, width, exchange(d_cross, CROSS)), (FAR, start, width, exchange(d_far, FAR))])
+        back.append([(CROSS, *chunk, exchange(d_cross, CROSS)), (FAR, *chunk, exchange(d_far, FAR))])
     d_near, loss, out = before
-    back.insert(1, [(NEAR, 0, points, exchange(d_near, NEAR))])
+    back.insert(1, [(NEAR, 0, quarter, exchange(d_near, NEAR))])
     cores = [[m * spaces + s for m in range(core, members, 2) for s in range(spaces)] for core in range(2)]
     copies = jnp.broadcast_to(sums[None], (len(cores[0]),) + sums.shape)
     everyone = lax.all_to_all(copies, AXES, 0, 0, axis_index_groups=cores)

time: 75.6 us -> 75.7 us (level)
  waiting for transfers between devices: 31.6 us -> 30 us
  starting transfers between devices: 28.4 us -> 29.9 us
    ppermute x12, waiting for transfers between devices: 26.9 us -> 25.2 us  [exchange(): return lax.ppermute(block, AXES, pairs)]
    ppermute x12, starting transfers between devices: 17.6 us -> 19.1 us  [exchange(): return lax.ppermute(block, AXES, pairs)]
where the time goes in v6:
time: 75.7 us; the launch traced here: 75.4 us
  waiting for transfers between devices  30 us (40%)
  starting transfers between devices  29.9 us (39%)
  Pallas kernels  14.1 us (19%)
    ppermute x12, waiting for transfers between devices, exchange(): return lax.ppermute(block, AXES, pairs)  25.2 us
    ppermute x12, starting transfers between devices, exchange(): return lax.ppermute(block, AXES, pairs)  19.1 us
    all_to_all x1, starting transfers between devices, shards(): everyone = lax.all_to_all(copies, AXES, 0, 0, axis_index_groups=cores)  10.8 us
    pallas_call x2, Pallas kernels, score(): pl.pallas_call(functools.partial(score_kernel, scale, weight, first, len(...  6.54 us
    all_to_all x1, waiting for transfers between devices, shards(): everyone = lax.all_to_all(copies, AXES, 0, 0, axis_index_groups=cores)  4.72 us
    pallas_call x3, Pallas kernels, take(): pl.pallas_call(functools.partial(take_kernel, specs, quarter, len(arrays)...  3.79 us
    pallas_call x3, Pallas kernels, place(): pl.pallas_call(functools.partial(place_kernel, specs, quarter, job, len(m...  3.77 us
  transfers between devices with their start and end apart: 13, of which 6 were waited for; matrix products, arithmetic and copies ran while one was open for 1% of the time, Pallas kernels for 16%

profile of v6, /device:TPU:1, one launch (start us, length us, event | category | flops | bytes accessed | tf_op | source)
XLA Modules:
  0.0 75.4 jit_solution(12132960179413608321)
XLA Ops:
  0.6 1.2 %shard_map.59 = (f32[2,16,4096]{2,1,0:T(8,128)S(1)}, f32[2,16,4096]{2,1,0:T(8,128)S(1)}) custom-call(f32[2,96,4096]{2,1,0:T(8,128)} %refs_0_.5), custom_call_target="tpu_custom_call" | custom-call | bytes 2097152 | tf_op jit(solution)/shard_map/pallas_call | solution.py:57
  1.9 4.5 %collective-permute-start.4 = (f32[2,16,4096]{2,1,0:T(8,128)S(1)}, f32[2,16,4096]{2,1,0:T(8,128)S(1)}, u32[]{:S(2)}, u32[]{:S(2)}) collective-permute-start(f32[2,16,4096]{2,1,0:T(8,128)S(1)} %get-tuple-element.24.refs_1_), channel_id=1, source_target_pairs={{0,64},{1,65},{2,66},{3,67},{4,68},{5,69},{6,70},{7,71},{8,72},{9,... | collective-permute-start | bytes 1572872 | tf_op jit(solution)/shard_map/ppermute | solution.py:27
  6.4 0.7 collective-permute-start.5
  7.0 1.0 %shard_map.60 = (f32[2,8,4096]{2,1,0:T(8,128)S(1)}, f32[2,8,4096]{2,1,0:T(8,128)S(1)}) custom-call(f32[2,96,4096]{2,1,0:T(8,128)} %refs_0_.5, f32[2,16,4096]{2,1,0:T(8,128)S(1)} %get-tuple-element.24.refs_1_, f32[2,16,4096]{2,1,0:T(8,128)S(1)} %get-tuple-element.25.refs_2_), custom_call_target="tpu_custom_call" | custom-call | bytes 1048576 | tf_op jit(solution)/shard_map/pallas_call | solution.py:57
  8.1 0.0 copy-start
  8.1 0.0 copy-start.1
  8.1 1.5 %shard_map.61 = (f32[1,24,4096]{2,1,0:T(8,128)S(1)}, f32[1,24,4096]{2,1,0:T(8,128)S(1)}, f32[2,24,4096]{2,1,0:T(8,128)S(1)}, f32[24,4096]{1,0:T(8,128)S(1)}) custom-call(f32[2,96,4096]{2,1,0:T(8,128)} %refs_0_.5, f32[96,4096]{1,0:T(8,128)} %refs_1_.1, f32[2,8,4096]{2,1,0:T(8,128)S(1)} %get-tuple-element.26.refs_2_, f32[2,8,4096]{2,1,0:T(8,128)S(1)} %get-tuple-element.27.refs_3_), custom_call_target="tpu_custom_call" | custom-call | bytes 3932160 | tf_op jit(solution)/shard_map/pallas_call | solution.py:57
  9.6 0.4 collective-permute-start
  10.0 0.2 collective-permute-start.1
  10.2 3.2 %collective-permute-start.2 = (f32[2,8,4096]{2,1,0:T(8,128)S(1)}, f32[2,8,4096]{2,1,0:T(8,128)S(1)}, u32[]{:S(2)}, u32[]{:S(2)}) collective-permute-start(f32[2,8,4096]{2,1,0:T(8,128)S(1)} %get-tuple-element.26.refs_2_), channel_id=1, source_target_pairs={{0,64},{1,65},{2,66},{3,67},{4,68},{5,69},{6,70},{7,71},{8,72},{9,... | collective-permute-start | bytes 786440 | tf_op jit(solution)/shard_map/ppermute | solution.py:27
  13.4 0.0 collective-permute-done.near_0
  13.4 1.2 %collective-permute-start.3 = (f32[2,8,4096]{2,1,0:T(8,128)S(1)}, f32[2,8,4096]{2,1,0:T(8,128)S(1)}, u32[]{:S(2)}, u32[]{:S(2)}) collective-permute-start(f32[2,8,4096]{2,1,0:T(8,128)S(1)} %get-tuple-element.27.refs_3_), channel_id=1, source_target_pairs={{0,96},{1,97},{2,98},{3,99},{4,100},{5,101},{6,102},{7,103},{8,104... | collective-permute-start | bytes 786440 | tf_op jit(solution)/shard_map/ppermute | solution.py:27
  14.6 0.0 collective-permute-done.1.near_1
  14.6 3.4 %collective-permute-done.4.far = f32[2,16,4096]{2,1,0:T(8,128)S(1)} collective-permute-done((f32[2,16,4096]{2,1,0:T(8,128)S(1)}, f32[2,16,4096]{2,1,0:T(8,128)S(1)}, u32[]{:S(2)}, u32[]{:S(2)}) %collective-permute-start.4) | collective-permute-done | bytes 524320 | tf_op jit(solution)/shard_map/ppermute | solution.py:27
  18.0 12.6 %collective-permute-done.5.cross = f32[2,16,4096]{2,1,0:T(8,128)S(1)} collective-permute-done((f32[2,16,4096]{2,1,0:T(8,128)S(1)}, f32[2,16,4096]{2,1,0:T(8,128)S(1)}, u32[]{:S(2)}, u32[]{:S(2)}) %collective-permute-start.5) | collective-permute-done | bytes 524320 | tf_op jit(solution)/shard_map/ppermute | solution.py:27
  30.6 0.0 copy-done
  30.6 0.1 broadcast_in_dim.22.pen
  30.7 0.0 copy-done.1
  30.7 3.9 %shard_map.62 = (f32[2,16,4096]{2,1,0:T(8,128)S(1)}, f32[2,16,4096]{2,1,0:T(8,128)}, f32[2,24,4096]{2,1,0:T(8,128)S(1)}, f32[24,128]{1,0:T(8,128)S(1)}, f32[2,96,4096]{2,1,0:T(8,128)}, /*index=5*/f32[1,128]{1,0:T(1,128)}) custom-call(f32[2,24,4096]{2,1,0:T(8,128)S(1)} %get-tuple-element.28.own, f32[1,24,4096]{2,1,0:T(8,128)S(1)} %collective-permute-done.near_0, ...), custom_call_target="tpu_custom_call" | custom-call | flops 26214400000 | bytes 5242880 | tf_op jit(solution)/shard_map/pallas_call | solution.py:164
  34.6 1.6 %collective-permute-start.9 = (f32[2,16,4096]{2,1,0:T(8,128)}, f32[2,16,4096]{2,1,0:T(8,128)S(1)}, u32[]{:S(2)}, u32[]{:S(2)}) collective-permute-start(f32[2,16,4096]{2,1,0:T(8,128)} %get-tuple-element.38), channel_id=1, source_target_pairs={{0,96},{1,97},{2,98},{3,99},{4,100},{5,101},{6,102},{7,103},{8,104... | collective-permute-start | bytes 1572872 | tf_op jit(solution)/shard_map/ppermute | solution.py:27
  36.2 1.8 %collective-permute-start.10 = (f32[2,16,4096]{2,1,0:T(8,128)S(1)}, f32[2,16,4096]{2,1,0:T(8,128)}, u32[]{:S(2)}, u32[]{:S(2)}) collective-permute-start(f32[2,16,4096]{2,1,0:T(8,128)S(1)} %get-tuple-element.39), channel_id=1, source_target_pairs={{0,64},{1,65},{2,66},{3,67},{4,68},{5,69},{6,70},{7,71},{8,72},{9,... | collective-permute-start | bytes 1572872 | tf_op jit(solution)/shard_map/ppermute | solution.py:27
  38.0 0.0 collective-permute-done.2.far
  38.0 4.1 %collective-permute-done.3.cross = f32[2,8,4096]{2,1,0:T(8,128)S(1)} collective-permute-done((f32[2,8,4096]{2,1,0:T(8,128)S(1)}, f32[2,8,4096]{2,1,0:T(8,128)S(1)}, u32[]{:S(2)}, u32[]{:S(2)}) %collective-permute-start.3) | collective-permute-done | bytes 262176 | tf_op jit(solution)/shard_map/ppermute | solution.py:27
  42.2 2.7 %shard_map.63 = (f32[2,8,4096]{2,1,0:T(8,128)S(1)}, f32[2,8,4096]{2,1,0:T(8,128)}, f32[2,24,4096]{2,1,0:T(8,128)S(1)}, f32[24,128]{1,0:T(8,128)S(1)}, f32[2,96,4096]{2,1,0:T(8,128)}, /*index=5*/f32[1,128]{1,0:T(1,128)S(1)}) custom-call(f32[2,24,4096]{2,1,0:T(8,128)S(1)} %get-tuple-element.28.own, ...), custom_call_target="tpu_custom_call", output_to_operand_aliasing={{2}: (8, {}), {3}: (9, {}), {4}: (10, {})} | custom-call | flops 13107200000 | bytes 2621440 | tf_op jit(solution)/shard_map/pallas_call | solution.py:164
  44.8 0.6 broadcast_in_dim.24
  45.5 10.8 %all-to-all-start = ((f32[64,1,128]{2,1,0:T(1,128)}), f32[64,1,128]{2,1,0:T(1,128)S(1)}, u32[]{:S(2)}, u32[]{:S(2)}) async-start(f32[64,1,128]{2,1,0:T(1,128)} %broadcast_in_dim.24), calls=%async_computation | async-start | bytes 65536 | tf_op jit(solution)/shard_map/all_to_all | solution.py:209
  56.3 1.2 %collective-permute-start.6 = (f32[2,8,4096]{2,1,0:T(8,128)}, f32[2,8,4096]{2,1,0:T(8,128)S(1)}, u32[]{:S(2)}, u32[]{:S(2)}) collective-permute-start(f32[2,8,4096]{2,1,0:T(8,128)} %get-tuple-element.35), channel_id=1, source_target_pairs={{0,96},{1,97},{2,98},{3,99},{4,100},{5,101},{6,102},{7,103},{8,104... | collective-permute-start | bytes 786440 | tf_op jit(solution)/shard_map/ppermute | solution.py:27
  57.5 1.6 %collective-permute-start.7 = (f32[2,8,4096]{2,1,0:T(8,128)S(1)}, f32[2,8,4096]{2,1,0:T(8,128)S(1)}, u32[]{:S(2)}, u32[]{:S(2)}) collective-permute-start(f32[2,8,4096]{2,1,0:T(8,128)S(1)} %get-tuple-element.36), channel_id=1, source_target_pairs={{0,64},{1,65},{2,66},{3,67},{4,68},{5,69},{6,70},{7,71},{8,72},{9,... | collective-permute-start | bytes 786440 | tf_op jit(solution)/shard_map/ppermute | solution.py:27
  59.1 0.9 %collective-permute-start.8 = (f32[2,24,4096]{2,1,0:T(8,128)S(1)}, f32[2,24,4096]{2,1,0:T(8,128)S(1)}, u32[]{:S(2)}, u32[]{:S(2)}) collective-permute-start(f32[2,24,4096]{2,1,0:T(8,128)S(1)} %get-tuple-element.37), channel_id=1, source_target_pairs={{0,32},{1,33},{2,34},{3,35},{4,36},{5,37},{6,38},{7,39},{8,40},{9,... | collective-permute-start | bytes 2359304 | tf_op jit(solution)/shard_map/ppermute | solution.py:27
  60.0 4.7 %all-to-all-done.refs_3_ = f32[64,1,128]{2,1,0:T(1,128)S(1)} async-done(((f32[64,1,128]{2,1,0:T(1,128)}), f32[64,1,128]{2,1,0:T(1,128)S(1)}, u32[]{:S(2)}, u32[]{:S(2)}) %all-to-all-start) | async-done | bytes 32800 | tf_op jit(solution)/shard_map/all_to_all | solution.py:209
  64.7 0.0 collective-permute-done.9.refs_0_
  64.7 0.0 collective-permute-done.10.refs_1_
  64.7 2.0 %shard_map.64 = (f32[2,96,4096]{2,1,0:T(8,128)}, f32[1,128]{1,0:T(1,128)S(1)}) custom-call(f32[2,16,4096]{2,1,0:T(8,128)S(1)} %collective-permute-done.9.refs_0_, f32[2,16,4096]{2,1,0:T(8,128)} %collective-permute-done.10.refs_1_, f32[2,96,4096]{2,1,0:T(8,128)} %get-tuple-element.40.refs_2_, ...), custom_call_target="tpu_custom_call", output_to_operand_aliasing={{0}: (2, {})} | custom-call | flops 40000000000 | bytes 2097152 | tf_op jit(solution)/shard_map/pallas_call | solution.py:86
  66.8 1.7 %collective-permute-start.11 = (f32[1,128]{1,0:T(1,128)S(1)}, f32[1,128]{1,0:T(1,128)S(1)}, u32[]{:S(2)}, u32[]{:S(2)}) collective-permute-start(f32[1,128]{1,0:T(1,128)S(1)} %get-tuple-element.43.refs_4_), channel_id=1, source_target_pairs={{0,32},{1,33},{2,34},{3,35},{4,36},{5,37},{6,38},{7,39},{8,40},{9,... | collective-permute-start | bytes 1544 | tf_op jit(solution)/shard_map/ppermute | solution.py:27
  68.5 0.0 collective-permute-done.8.refs_0_
  68.5 0.9 %shard_map.65.refs_2_ = f32[2,96,4096]{2,1,0:T(8,128)} custom-call(f32[2,24,4096]{2,1,0:T(8,128)S(1)} %collective-permute-done.8.refs_0_, f32[2,96,4096]{2,1,0:T(8,128)} %get-tuple-element.42.refs_1_), custom_call_target="tpu_custom_call", output_to_operand_aliasing={{}: (1, {})} | custom-call | bytes 1572864 | tf_op jit(solution)/shard_map/pallas_call | solution.py:86
  69.4 0.9 %collective-permute-done.6.refs_0_ = f32[2,8,4096]{2,1,0:T(8,128)S(1)} collective-permute-done((f32[2,8,4096]{2,1,0:T(8,128)}, f32[2,8,4096]{2,1,0:T(8,128)S(1)}, u32[]{:S(2)}, u32[]{:S(2)}) %collective-permute-start.6) | collective-permute-done | bytes 262176 | tf_op jit(solution)/shard_map/ppermute | solution.py:27
  70.3 4.2 %collective-permute-done.7.refs_1_ = f32[2,8,4096]{2,1,0:T(8,128)S(1)} collective-permute-done((f32[2,8,4096]{2,1,0:T(8,128)S(1)}, f32[2,8,4096]{2,1,0:T(8,128)S(1)}, u32[]{:S(2)}, u32[]{:S(2)}) %collective-permute-start.7) | collective-permute-done | bytes 262176 | tf_op jit(solution)/shard_map/ppermute | solution.py:27
  74.5 0.0 collective-permute-done.11.refs_5_
  74.6 0.8 %shard_map.66 = (f32[2,96,4096]{2,1,0:T(8,128)}, f32[1,96]{1,0:T(1,128)}) custom-call(f32[2,8,4096]{2,1,0:T(8,128)S(1)} %collective-permute-done.6.refs_0_, f32[2,8,4096]{2,1,0:T(8,128)S(1)} %collective-permute-done.7.refs_1_, f32[2,96,4096]{2,1,0:T(8,128)} %shard_map.65.refs_2_, f32[1,96]{1,0:T(1,128)S(1)} %bitcast.4, ...), custom_call_target="tpu_custom_call", output_to_operand_aliasing={{0}: (2, {})} | custom-call | bytes 1048576 | tf_op jit(solution)/shard_map/pallas_call | solution.py:86
Async XLA Ops:
  1.9 16.2 %collective-permute-start.4 = (f32[2,16,4096]{2,1,0:T(8,128)S(1)}, f32[2,16,4096]{2,1,0:T(8,128)S(1)}, u32[]{:S(2)}, u32[]{:S(2)}) collective-permute-start(f32[2,16,4096]{2,1,0:T(8,128)S(1)} %get-tuple-element.24.refs_1_), channel_id=1, source_target_pairs={{0,64},{1,65},{2,66},{3,67},{4,68},{5,69},{6,70},{7,71},{8,72},{9,... | collective-permute-start | bytes 1572872 | tf_op jit(solution)/shard_map/ppermute | solution.py:27
  6.4 24.3 %collective-permute-start.5 = (f32[2,16,4096]{2,1,0:T(8,128)S(1)}, f32[2,16,4096]{2,1,0:T(8,128)S(1)}, u32[]{:S(2)}, u32[]{:S(2)}) collective-permute-start(f32[2,16,4096]{2,1,0:T(8,128)S(1)} %get-tuple-element.25.refs_2_), channel_id=1, source_target_pairs={{0,96},{1,97},{2,98},{3,99},{4,100},{5,101},{6,102},{7,103},{8,104... | collective-permute-start | bytes 1572872 | tf_op jit(solution)/shard_map/ppermute | solution.py:27
  8.1 22.5 %copy-start = (f32[96]{0:T(128)S(1)}, f32[96]{0:T(128)}, u32[]{:S(2)}) copy-start(f32[96]{0:T(128)} %param.7) | copy-start | bytes 1156
  8.1 22.6 %copy-start.1 = (f32[4096]{0:T(1024)S(1)}, f32[4096]{0:T(1024)}, u32[]{:S(2)}) copy-start(f32[4096]{0:T(1024)} %param.6) | copy-start | bytes 49156
  9.6 3.8 %collective-permute-start = (f32[1,24,4096]{2,1,0:T(8,128)S(1)}, f32[1,24,4096]{2,1,0:T(8,128)S(1)}, u32[]{:S(2)}, u32[]{:S(2)}) collective-permute-start(f32[1,24,4096]{2,1,0:T(8,128)S(1)} %get-tuple-element.29), channel_id=1, source_target_pairs={{0,32},{1,33},{2,34},{3,35},{4,36},{5,37},{6,38},{7,39},{8,40},{9,... | collective-permute-start | bytes 1179656 | tf_op jit(solution)/shard_map/ppermute | solution.py:27
  10.0 4.6 %collective-permute-start.1 = (f32[1,24,4096]{2,1,0:T(8,128)S(1)}, f32[1,24,4096]{2,1,0:T(8,128)S(1)}, u32[]{:S(2)}, u32[]{:S(2)}) collective-permute-start(f32[1,24,4096]{2,1,0:T(8,128)S(1)} %get-tuple-element.30), channel_id=1, source_target_pairs={{0,32},{1,33},{2,34},{3,35},{4,36},{5,37},{6,38},{7,39},{8,40},{9,... | collective-permute-start | bytes 1179656 | tf_op jit(solution)/shard_map/ppermute | solution.py:27
  10.2 27.8 %collective-permute-start.2 = (f32[2,8,4096]{2,1,0:T(8,128)S(1)}, f32[2,8,4096]{2,1,0:T(8,128)S(1)}, u32[]{:S(2)}, u32[]{:S(2)}) collective-permute-start(f32[2,8,4096]{2,1,0:T(8,128)S(1)} %get-tuple-element.26.refs_2_), channel_id=1, source_target_pairs={{0,64},{1,65},{2,66},{3,67},{4,68},{5,69},{6,70},{7,71},{8,72},{9,... | collective-permute-start | bytes 786440 | tf_op jit(solution)/shard_map/ppermute | solution.py:27
  13.4 28.8 %collective-permute-start.3 = (f32[2,8,4096]{2,1,0:T(8,128)S(1)}, f32[2,8,4096]{2,1,0:T(8,128)S(1)}, u32[]{:S(2)}, u32[]{:S(2)}) collective-permute-start(f32[2,8,4096]{2,1,0:T(8,128)S(1)} %get-tuple-element.27.refs_3_), channel_id=1, source_target_pairs={{0,96},{1,97},{2,98},{3,99},{4,100},{5,101},{6,102},{7,103},{8,104... | collective-permute-start | bytes 786440 | tf_op jit(solution)/shard_map/ppermute | solution.py:27
  34.6 30.1 %collective-permute-start.9 = (f32[2,16,4096]{2,1,0:T(8,128)}, f32[2,16,4096]{2,1,0:T(8,128)S(1)}, u32[]{:S(2)}, u32[]{:S(2)}) collective-permute-start(f32[2,16,4096]{2,1,0:T(8,128)} %get-tuple-element.38), channel_id=1, source_target_pairs={{0,96},{1,97},{2,98},{3,99},{4,100},{5,101},{6,102},{7,103},{8,104... | collective-permute-start | bytes 1572872 | tf_op jit(solution)/shard_map/ppermute | solution.py:27
  36.2 28.5 %collective-permute-start.10 = (f32[2,16,4096]{2,1,0:T(8,128)S(1)}, f32[2,16,4096]{2,1,0:T(8,128)}, u32[]{:S(2)}, u32[]{:S(2)}) collective-permute-start(f32[2,16,4096]{2,1,0:T(8,128)S(1)} %get-tuple-element.39), channel_id=1, source_target_pairs={{0,64},{1,65},{2,66},{3,67},{4,68},{5,69},{6,70},{7,71},{8,72},{9,... | collective-permute-start | bytes 1572872 | tf_op jit(solution)/shard_map/ppermute | solution.py:27
  45.5 19.3 %all-to-all-start = ((f32[64,1,128]{2,1,0:T(1,128)}), f32[64,1,128]{2,1,0:T(1,128)S(1)}, u32[]{:S(2)}, u32[]{:S(2)}) async-start(f32[64,1,128]{2,1,0:T(1,128)} %broadcast_in_dim.24), calls=%async_computation | async-start | bytes 65536 | tf_op jit(solution)/shard_map/all_to_all | solution.py:209
  56.3 14.0 %collective-permute-start.6 = (f32[2,8,4096]{2,1,0:T(8,128)}, f32[2,8,4096]{2,1,0:T(8,128)S(1)}, u32[]{:S(2)}, u32[]{:S(2)}) collective-permute-start(f32[2,8,4096]{2,1,0:T(8,128)} %get-tuple-element.35), channel_id=1, source_target_pairs={{0,96},{1,97},{2,98},{3,99},{4,100},{5,101},{6,102},{7,103},{8,104... | collective-permute-start | bytes 786440 | tf_op jit(solution)/shard_map/ppermute | solution.py:27
  57.5 17.0 %collective-permute-start.7 = (f32[2,8,4096]{2,1,0:T(8,128)S(1)}, f32[2,8,4096]{2,1,0:T(8,128)S(1)}, u32[]{:S(2)}, u32[]{:S(2)}) collective-permute-start(f32[2,8,4096]{2,1,0:T(8,128)S(1)} %get-tuple-element.36), channel_id=1, source_target_pairs={{0,64},{1,65},{2,66},{3,67},{4,68},{5,69},{6,70},{7,71},{8,72},{9,... | collective-permute-start | bytes 786440 | tf_op jit(solution)/shard_map/ppermute | solution.py:27
  59.1 9.5 %collective-permute-start.8 = (f32[2,24,4096]{2,1,0:T(8,128)S(1)}, f32[2,24,4096]{2,1,0:T(8,128)S(1)}, u32[]{:S(2)}, u32[]{:S(2)}) collective-permute-start(f32[2,24,4096]{2,1,0:T(8,128)S(1)} %get-tuple-element.37), channel_id=1, source_target_pairs={{0,32},{1,33},{2,34},{3,35},{4,36},{5,37},{6,38},{7,39},{8,40},{9,... | collective-permute-start | bytes 2359304 | tf_op jit(solution)/shard_map/ppermute | solution.py:27
  66.8 7.8 %collective-permute-start.11 = (f32[1,128]{1,0:T(1,128)S(1)}, f32[1,128]{1,0:T(1,128)S(1)}, u32[]{:S(2)}, u32[]{:S(2)}) collective-permute-start(f32[1,128]{1,0:T(1,128)S(1)} %get-tuple-element.43.refs_4_), channel_id=1, source_target_pairs={{0,32},{1,33},{2,34},{3,35},{4,36},{5,37},{6,38},{7,39},{8,40},{9,... | collective-permute-start | bytes 1544 | tf_op jit(solution)/shard_map/ppermute | solution.py:27

commit v7 on v6

--- a/solution.py
+++ b/solution.py
@@ -145,7 +145,7 @@
                 target[j % 2, pl.ds(shift + row, SUBLANES), c] = factor * g
             return total + area * score
 
-        loss[q, :] = lax.fori_loop(0, cols // LANES, step, jnp.zeros((SUBLANES, LANES), jnp.float32), unroll=2)
+        loss[q, :] = lax.fori_loop(0, cols // LANES, step, jnp.zeros((SUBLANES, LANES), jnp.float32), unroll=4)
         for i, (source, home) in enumerate(homes):
             copies.append(pltpu.make_async_copy(source.at[:, r], home.at[:, r], sems.at[i, row // SUBLANES]))
             copies[-1].start()

time: 75.7 us -> 75.7 us (level)
  no operation moved by 1% of the time
where the time goes in v7:
time: 75.7 us; the launch traced here: 75.4 us
  waiting for transfers between devices  30.1 us (40%)
  starting transfers between devices  29.9 us (39%)
  Pallas kernels  13.9 us (18%)
    ppermute x12, waiting for transfers between devices, exchange(): return lax.ppermute(block, AXES, pairs)  25.4 us
    ppermute x12, starting transfers between devices, exchange(): return lax.ppermute(block, AXES, pairs)  19.1 us
    all_to_all x1, starting transfers between devices, shards(): everyone = lax.all_to_all(copies, AXES, 0, 0, axis_index_groups=cores)  10.8 us
    pallas_call x2, Pallas kernels, score(): pl.pallas_call(functools.partial(score_kernel, scale, weight, first, len(...  6.36 us
    all_to_all x1, waiting for transfers between devices, shards(): everyone = lax.all_to_all(copies, AXES, 0, 0, axis_index_groups=cores)  4.72 us
    pallas_call x3, Pallas kernels, take(): pl.pallas_call(functools.partial(take_kernel, specs, quarter, len(arrays)...  3.79 us
    pallas_call x3, Pallas kernels, place(): pl.pallas_call(functools.partial(place_kernel, specs, quarter, job, len(m...  3.77 us
  transfers between devices with their start and end apart: 13, of which 6 were waited for; matrix products, arithmetic and copies ran while one was open for 1% of the time, Pallas kernels for 16%

profile of v7, /device:TPU:1, one launch (start us, length us, event | category | flops | bytes accessed | tf_op | source)
XLA Modules:
  0.0 75.4 jit_solution(9159913117541787199)
XLA Ops:
  0.6 1.2 %shard_map.59 = (f32[2,16,4096]{2,1,0:T(8,128)S(1)}, f32[2,16,4096]{2,1,0:T(8,128)S(1)}) custom-call(f32[2,96,4096]{2,1,0:T(8,128)} %refs_0_.5), custom_call_target="tpu_custom_call" | custom-call | bytes 2097152 | tf_op jit(solution)/shard_map/pallas_call | solution.py:57
  1.9 4.5 %collective-permute-start.4 = (f32[2,16,4096]{2,1,0:T(8,128)S(1)}, f32[2,16,4096]{2,1,0:T(8,128)S(1)}, u32[]{:S(2)}, u32[]{:S(2)}) collective-permute-start(f32[2,16,4096]{2,1,0:T(8,128)S(1)} %get-tuple-element.24.refs_1_), channel_id=1, source_target_pairs={{0,64},{1,65},{2,66},{3,67},{4,68},{5,69},{6,70},{7,71},{8,72},{9,... | collective-permute-start | bytes 1572872 | tf_op jit(solution)/shard_map/ppermute | solution.py:27
  6.4 0.7 collective-permute-start.5
  7.0 1.0 %shard_map.60 = (f32[2,8,4096]{2,1,0:T(8,128)S(1)}, f32[2,8,4096]{2,1,0:T(8,128)S(1)}) custom-call(f32[2,96,4096]{2,1,0:T(8,128)} %refs_0_.5, f32[2,16,4096]{2,1,0:T(8,128)S(1)} %get-tuple-element.24.refs_1_, f32[2,16,4096]{2,1,0:T(8,128)S(1)} %get-tuple-element.25.refs_2_), custom_call_target="tpu_custom_call" | custom-call | bytes 1048576 | tf_op jit(solution)/shard_map/pallas_call | solution.py:57
  8.1 0.0 copy-start
  8.1 0.0 copy-start.1
  8.1 1.5 %shard_map.61 = (f32[1,24,4096]{2,1,0:T(8,128)S(1)}, f32[1,24,4096]{2,1,0:T(8,128)S(1)}, f32[2,24,4096]{2,1,0:T(8,128)S(1)}, f32[24,4096]{1,0:T(8,128)S(1)}) custom-call(f32[2,96,4096]{2,1,0:T(8,128)} %refs_0_.5, f32[96,4096]{1,0:T(8,128)} %refs_1_.1, f32[2,8,4096]{2,1,0:T(8,128)S(1)} %get-tuple-element.26.refs_2_, f32[2,8,4096]{2,1,0:T(8,128)S(1)} %get-tuple-element.27.refs_3_), custom_call_target="tpu_custom_call" | custom-call | bytes 3932160 | tf_op jit(solution)/shard_map/pallas_call | solution.py:57
  9.6 0.4 collective-permute-start
  10.0 0.2 collective-permute-start.1
  10.2 3.2 %collective-permute-start.2 = (f32[2,8,4096]{2,1,0:T(8,128)S(1)}, f32[2,8,4096]{2,1,0:T(8,128)S(1)}, u32[]{:S(2)}, u32[]{:S(2)}) collective-permute-start(f32[2,8,4096]{2,1,0:T(8,128)S(1)} %get-tuple-element.26.refs_2_), channel_id=1, source_target_pairs={{0,64},{1,65},{2,66},{3,67},{4,68},{5,69},{6,70},{7,71},{8,72},{9,... | collective-permute-start | bytes 786440 | tf_op jit(solution)/shard_map/ppermute | solution.py:27
  13.4 0.0 collective-permute-done.near_0
  13.4 1.2 %collective-permute-start.3 = (f32[2,8,4096]{2,1,0:T(8,128)S(1)}, f32[2,8,4096]{2,1,0:T(8,128)S(1)}, u32[]{:S(2)}, u32[]{:S(2)}) collective-permute-start(f32[2,8,4096]{2,1,0:T(8,128)S(1)} %get-tuple-element.27.refs_3_), channel_id=1, source_target_pairs={{0,96},{1,97},{2,98},{3,99},{4,100},{5,101},{6,102},{7,103},{8,104... | collective-permute-start | bytes 786440 | tf_op jit(solution)/shard_map/ppermute | solution.py:27
  14.6 0.0 collective-permute-done.1.near_1
  14.6 3.4 %collective-permute-done.4.far = f32[2,16,4096]{2,1,0:T(8,128)S(1)} collective-permute-done((f32[2,16,4096]{2,1,0:T(8,128)S(1)}, f32[2,16,4096]{2,1,0:T(8,128)S(1)}, u32[]{:S(2)}, u32[]{:S(2)}) %collective-permute-start.4) | collective-permute-done | bytes 524320 | tf_op jit(solution)/shard_map/ppermute | solution.py:27
  18.0 12.6 %collective-permute-done.5.cross = f32[2,16,4096]{2,1,0:T(8,128)S(1)} collective-permute-done((f32[2,16,4096]{2,1,0:T(8,128)S(1)}, f32[2,16,4096]{2,1,0:T(8,128)S(1)}, u32[]{:S(2)}, u32[]{:S(2)}) %collective-permute-start.5) | collective-permute-done | bytes 524320 | tf_op jit(solution)/shard_map/ppermute | solution.py:27
  30.6 0.0 copy-done
  30.6 0.1 broadcast_in_dim.22.pen
  30.7 0.0 copy-done.1
  30.7 3.8 %shard_map.62 = (f32[2,16,4096]{2,1,0:T(8,128)S(1)}, f32[2,16,4096]{2,1,0:T(8,128)}, f32[2,24,4096]{2,1,0:T(8,128)S(1)}, f32[24,128]{1,0:T(8,128)S(1)}, f32[2,96,4096]{2,1,0:T(8,128)}, /*index=5*/f32[1,128]{1,0:T(1,128)}) custom-call(f32[2,24,4096]{2,1,0:T(8,128)S(1)} %get-tuple-element.28.own, f32[1,24,4096]{2,1,0:T(8,128)S(1)} %collective-permute-done.near_0, ...), custom_call_target="tpu_custom_call" | custom-call | flops 26214400000 | bytes 5242880 | tf_op jit(solution)/shard_map/pallas_call | solution.py:164
  34.5 1.6 %collective-permute-start.9 = (f32[2,16,4096]{2,1,0:T(8,128)}, f32[2,16,4096]{2,1,0:T(8,128)S(1)}, u32[]{:S(2)}, u32[]{:S(2)}) collective-permute-start(f32[2,16,4096]{2,1,0:T(8,128)} %get-tuple-element.38), channel_id=1, source_target_pairs={{0,96},{1,97},{2,98},{3,99},{4,100},{5,101},{6,102},{7,103},{8,104... | collective-permute-start | bytes 1572872 | tf_op jit(solution)/shard_map/ppermute | solution.py:27
  36.1 1.8 %collective-permute-start.10 = (f32[2,16,4096]{2,1,0:T(8,128)S(1)}, f32[2,16,4096]{2,1,0:T(8,128)}, u32[]{:S(2)}, u32[]{:S(2)}) collective-permute-start(f32[2,16,4096]{2,1,0:T(8,128)S(1)} %get-tuple-element.39), channel_id=1, source_target_pairs={{0,64},{1,65},{2,66},{3,67},{4,68},{5,69},{6,70},{7,71},{8,72},{9,... | collective-permute-start | bytes 1572872 | tf_op jit(solution)/shard_map/ppermute | solution.py:27
  37.9 0.0 collective-permute-done.2.far
  37.9 4.2 %collective-permute-done.3.cross = f32[2,8,4096]{2,1,0:T(8,128)S(1)} collective-permute-done((f32[2,8,4096]{2,1,0:T(8,128)S(1)}, f32[2,8,4096]{2,1,0:T(8,128)S(1)}, u32[]{:S(2)}, u32[]{:S(2)}) %collective-permute-start.3) | collective-permute-done | bytes 262176 | tf_op jit(solution)/shard_map/ppermute | solution.py:27
  42.2 2.6 %shard_map.63 = (f32[2,8,4096]{2,1,0:T(8,128)S(1)}, f32[2,8,4096]{2,1,0:T(8,128)}, f32[2,24,4096]{2,1,0:T(8,128)S(1)}, f32[24,128]{1,0:T(8,128)S(1)}, f32[2,96,4096]{2,1,0:T(8,128)}, /*index=5*/f32[1,128]{1,0:T(1,128)S(1)}) custom-call(f32[2,24,4096]{2,1,0:T(8,128)S(1)} %get-tuple-element.28.own, ...), custom_call_target="tpu_custom_call", output_to_operand_aliasing={{2}: (8, {}), {3}: (9, {}), {4}: (10, {})} | custom-call | flops 13107200000 | bytes 2621440 | tf_op jit(solution)/shard_map/pallas_call | solution.py:164
  44.8 0.6 broadcast_in_dim.24
  45.4 10.8 %all-to-all-start = ((f32[64,1,128]{2,1,0:T(1,128)}), f32[64,1,128]{2,1,0:T(1,128)S(1)}, u32[]{:S(2)}, u32[]{:S(2)}) async-start(f32[64,1,128]{2,1,0:T(1,128)} %broadcast_in_dim.24), calls=%async_computation | async-start | bytes 65536 | tf_op jit(solution)/shard_map/all_to_all | solution.py:209
  56.2 1.2 %collective-permute-start.6 = (f32[2,8,4096]{2,1,0:T(8,128)}, f32[2,8,4096]{2,1,0:T(8,128)S(1)}, u32[]{:S(2)}, u32[]{:S(2)}) collective-permute-start(f32[2,8,4096]{2,1,0:T(8,128)} %get-tuple-element.35), channel_id=1, source_target_pairs={{0,96},{1,97},{2,98},{3,99},{4,100},{5,101},{6,102},{7,103},{8,104... | collective-permute-start | bytes 786440 | tf_op jit(solution)/shard_map/ppermute | solution.py:27
  57.5 1.6 %collective-permute-start.7 = (f32[2,8,4096]{2,1,0:T(8,128)S(1)}, f32[2,8,4096]{2,1,0:T(8,128)S(1)}, u32[]{:S(2)}, u32[]{:S(2)}) collective-permute-start(f32[2,8,4096]{2,1,0:T(8,128)S(1)} %get-tuple-element.36), channel_id=1, source_target_pairs={{0,64},{1,65},{2,66},{3,67},{4,68},{5,69},{6,70},{7,71},{8,72},{9,... | collective-permute-start | bytes 786440 | tf_op jit(solution)/shard_map/ppermute | solution.py:27
  59.0 0.9 %collective-permute-start.8 = (f32[2,24,4096]{2,1,0:T(8,128)S(1)}, f32[2,24,4096]{2,1,0:T(8,128)S(1)}, u32[]{:S(2)}, u32[]{:S(2)}) collective-permute-start(f32[2,24,4096]{2,1,0:T(8,128)S(1)} %get-tuple-element.37), channel_id=1, source_target_pairs={{0,32},{1,33},{2,34},{3,35},{4,36},{5,37},{6,38},{7,39},{8,40},{9,... | collective-permute-start | bytes 2359304 | tf_op jit(solution)/shard_map/ppermute | solution.py:27
  59.9 4.7 %all-to-all-done.refs_3_ = f32[64,1,128]{2,1,0:T(1,128)S(1)} async-done(((f32[64,1,128]{2,1,0:T(1,128)}), f32[64,1,128]{2,1,0:T(1,128)S(1)}, u32[]{:S(2)}, u32[]{:S(2)}) %all-to-all-start) | async-done | bytes 32800 | tf_op jit(solution)/shard_map/all_to_all | solution.py:209
  64.7 0.0 collective-permute-done.9.refs_0_
  64.7 0.0 collective-permute-done.10.refs_1_
  64.7 2.0 %shard_map.64 = (f32[2,96,4096]{2,1,0:T(8,128)}, f32[1,128]{1,0:T(1,128)S(1)}) custom-call(f32[2,16,4096]{2,1,0:T(8,128)S(1)} %collective-permute-done.9.refs_0_, f32[2,16,4096]{2,1,0:T(8,128)} %collective-permute-done.10.refs_1_, f32[2,96,4096]{2,1,0:T(8,128)} %get-tuple-element.40.refs_2_, ...), custom_call_target="tpu_custom_call", output_to_operand_aliasing={{0}: (2, {})} | custom-call | flops 40000000000 | bytes 2097152 | tf_op jit(solution)/shard_map/pallas_call | solution.py:86
  66.7 1.8 %collective-permute-start.11 = (f32[1,128]{1,0:T(1,128)S(1)}, f32[1,128]{1,0:T(1,128)S(1)}, u32[]{:S(2)}, u32[]{:S(2)}) collective-permute-start(f32[1,128]{1,0:T(1,128)S(1)} %get-tuple-element.43.refs_4_), channel_id=1, source_target_pairs={{0,32},{1,33},{2,34},{3,35},{4,36},{5,37},{6,38},{7,39},{8,40},{9,... | collective-permute-start | bytes 1544 | tf_op jit(solution)/shard_map/ppermute | solution.py:27
  68.5 0.0 collective-permute-done.8.refs_0_
  68.5 0.9 %shard_map.65.refs_2_ = f32[2,96,4096]{2,1,0:T(8,128)} custom-call(f32[2,24,4096]{2,1,0:T(8,128)S(1)} %collective-permute-done.8.refs_0_, f32[2,96,4096]{2,1,0:T(8,128)} %get-tuple-element.42.refs_1_), custom_call_target="tpu_custom_call", output_to_operand_aliasing={{}: (1, {})} | custom-call | bytes 1572864 | tf_op jit(solution)/shard_map/pallas_call | solution.py:86
  69.4 0.9 %collective-permute-done.6.refs_0_ = f32[2,8,4096]{2,1,0:T(8,128)S(1)} collective-permute-done((f32[2,8,4096]{2,1,0:T(8,128)}, f32[2,8,4096]{2,1,0:T(8,128)S(1)}, u32[]{:S(2)}, u32[]{:S(2)}) %collective-permute-start.6) | collective-permute-done | bytes 262176 | tf_op jit(solution)/shard_map/ppermute | solution.py:27
  70.3 4.2 %collective-permute-done.7.refs_1_ = f32[2,8,4096]{2,1,0:T(8,128)S(1)} collective-permute-done((f32[2,8,4096]{2,1,0:T(8,128)S(1)}, f32[2,8,4096]{2,1,0:T(8,128)S(1)}, u32[]{:S(2)}, u32[]{:S(2)}) %collective-permute-start.7) | collective-permute-done | bytes 262176 | tf_op jit(solution)/shard_map/ppermute | solution.py:27
  74.5 0.0 collective-permute-done.11.refs_5_
  74.6 0.8 %shard_map.66 = (f32[2,96,4096]{2,1,0:T(8,128)}, f32[1,96]{1,0:T(1,128)}) custom-call(f32[2,8,4096]{2,1,0:T(8,128)S(1)} %collective-permute-done.6.refs_0_, f32[2,8,4096]{2,1,0:T(8,128)S(1)} %collective-permute-done.7.refs_1_, f32[2,96,4096]{2,1,0:T(8,128)} %shard_map.65.refs_2_, f32[1,96]{1,0:T(1,128)S(1)} %bitcast.4, ...), custom_call_target="tpu_custom_call", output_to_operand_aliasing={{0}: (2, {})} | custom-call | bytes 1048576 | tf_op jit(solution)/shard_map/pallas_call | solution.py:86
Async XLA Ops:
  1.9 16.2 %collective-permute-start.4 = (f32[2,16,4096]{2,1,0:T(8,128)S(1)}, f32[2,16,4096]{2,1,0:T(8,128)S(1)}, u32[]{:S(2)}, u32[]{:S(2)}) collective-permute-start(f32[2,16,4096]{2,1,0:T(8,128)S(1)} %get-tuple-element.24.refs_1_), channel_id=1, source_target_pairs={{0,64},{1,65},{2,66},{3,67},{4,68},{5,69},{6,70},{7,71},{8,72},{9,... | collective-permute-start | bytes 1572872 | tf_op jit(solution)/shard_map/ppermute | solution.py:27
  6.4 24.3 %collective-permute-start.5 = (f32[2,16,4096]{2,1,0:T(8,128)S(1)}, f32[2,16,4096]{2,1,0:T(8,128)S(1)}, u32[]{:S(2)}, u32[]{:S(2)}) collective-permute-start(f32[2,16,4096]{2,1,0:T(8,128)S(1)} %get-tuple-element.25.refs_2_), channel_id=1, source_target_pairs={{0,96},{1,97},{2,98},{3,99},{4,100},{5,101},{6,102},{7,103},{8,104... | collective-permute-start | bytes 1572872 | tf_op jit(solution)/shard_map/ppermute | solution.py:27
  8.1 22.5 %copy-start = (f32[96]{0:T(128)S(1)}, f32[96]{0:T(128)}, u32[]{:S(2)}) copy-start(f32[96]{0:T(128)} %param.7) | copy-start | bytes 1156
  8.1 22.6 %copy-start.1 = (f32[4096]{0:T(1024)S(1)}, f32[4096]{0:T(1024)}, u32[]{:S(2)}) copy-start(f32[4096]{0:T(1024)} %param.6) | copy-start | bytes 49156
  9.6 3.8 %collective-permute-start = (f32[1,24,4096]{2,1,0:T(8,128)S(1)}, f32[1,24,4096]{2,1,0:T(8,128)S(1)}, u32[]{:S(2)}, u32[]{:S(2)}) collective-permute-start(f32[1,24,4096]{2,1,0:T(8,128)S(1)} %get-tuple-element.29), channel_id=1, source_target_pairs={{0,32},{1,33},{2,34},{3,35},{4,36},{5,37},{6,38},{7,39},{8,40},{9,... | collective-permute-start | bytes 1179656 | tf_op jit(solution)/shard_map/ppermute | solution.py:27
  10.0 4.6 %collective-permute-start.1 = (f32[1,24,4096]{2,1,0:T(8,128)S(1)}, f32[1,24,4096]{2,1,0:T(8,128)S(1)}, u32[]{:S(2)}, u32[]{:S(2)}) collective-permute-start(f32[1,24,4096]{2,1,0:T(8,128)S(1)} %get-tuple-element.30), channel_id=1, source_target_pairs={{0,32},{1,33},{2,34},{3,35},{4,36},{5,37},{6,38},{7,39},{8,40},{9,... | collective-permute-start | bytes 1179656 | tf_op jit(solution)/shard_map/ppermute | solution.py:27
  10.2 27.7 %collective-permute-start.2 = (f32[2,8,4096]{2,1,0:T(8,128)S(1)}, f32[2,8,4096]{2,1,0:T(8,128)S(1)}, u32[]{:S(2)}, u32[]{:S(2)}) collective-permute-start(f32[2,8,4096]{2,1,0:T(8,128)S(1)} %get-tuple-element.26.refs_2_), channel_id=1, source_target_pairs={{0,64},{1,65},{2,66},{3,67},{4,68},{5,69},{6,70},{7,71},{8,72},{9,... | collective-permute-start | bytes 786440 | tf_op jit(solution)/shard_map/ppermute | solution.py:27
  13.4 28.8 %collective-permute-start.3 = (f32[2,8,4096]{2,1,0:T(8,128)S(1)}, f32[2,8,4096]{2,1,0:T(8,128)S(1)}, u32[]{:S(2)}, u32[]{:S(2)}) collective-permute-start(f32[2,8,4096]{2,1,0:T(8,128)S(1)} %get-tuple-element.27.refs_3_), channel_id=1, source_target_pairs={{0,96},{1,97},{2,98},{3,99},{4,100},{5,101},{6,102},{7,103},{8,104... | collective-permute-start | bytes 786440 | tf_op jit(solution)/shard_map/ppermute | solution.py:27
  34.5 30.2 %collective-permute-start.9 = (f32[2,16,4096]{2,1,0:T(8,128)}, f32[2,16,4096]{2,1,0:T(8,128)S(1)}, u32[]{:S(2)}, u32[]{:S(2)}) collective-permute-start(f32[2,16,4096]{2,1,0:T(8,128)} %get-tuple-element.38), channel_id=1, source_target_pairs={{0,96},{1,97},{2,98},{3,99},{4,100},{5,101},{6,102},{7,103},{8,104... | collective-permute-start | bytes 1572872 | tf_op jit(solution)/shard_map/ppermute | solution.py:27
  36.1 28.6 %collective-permute-start.10 = (f32[2,16,4096]{2,1,0:T(8,128)S(1)}, f32[2,16,4096]{2,1,0:T(8,128)}, u32[]{:S(2)}, u32[]{:S(2)}) collective-permute-start(f32[2,16,4096]{2,1,0:T(8,128)S(1)} %get-tuple-element.39), channel_id=1, source_target_pairs={{0,64},{1,65},{2,66},{3,67},{4,68},{5,69},{6,70},{7,71},{8,72},{9,... | collective-permute-start | bytes 1572872 | tf_op jit(solution)/shard_map/ppermute | solution.py:27
  45.4 19.3 %all-to-all-start = ((f32[64,1,128]{2,1,0:T(1,128)}), f32[64,1,128]{2,1,0:T(1,128)S(1)}, u32[]{:S(2)}, u32[]{:S(2)}) async-start(f32[64,1,128]{2,1,0:T(1,128)} %broadcast_in_dim.24), calls=%async_computation | async-start | bytes 65536 | tf_op jit(solution)/shard_map/all_to_all | solution.py:209
  56.2 14.1 %collective-permute-start.6 = (f32[2,8,4096]{2,1,0:T(8,128)}, f32[2,8,4096]{2,1,0:T(8,128)S(1)}, u32[]{:S(2)}, u32[]{:S(2)}) collective-permute-start(f32[2,8,4096]{2,1,0:T(8,128)} %get-tuple-element.35), channel_id=1, source_target_pairs={{0,96},{1,97},{2,98},{3,99},{4,100},{5,101},{6,102},{7,103},{8,104... | collective-permute-start | bytes 786440 | tf_op jit(solution)/shard_map/ppermute | solution.py:27
  57.5 17.1 %collective-permute-start.7 = (f32[2,8,4096]{2,1,0:T(8,128)S(1)}, f32[2,8,4096]{2,1,0:T(8,128)S(1)}, u32[]{:S(2)}, u32[]{:S(2)}) collective-permute-start(f32[2,8,4096]{2,1,0:T(8,128)S(1)} %get-tuple-element.36), channel_id=1, source_target_pairs={{0,64},{1,65},{2,66},{3,67},{4,68},{5,69},{6,70},{7,71},{8,72},{9,... | collective-permute-start | bytes 786440 | tf_op jit(solution)/shard_map/ppermute | solution.py:27
  59.0 9.5 %collective-permute-start.8 = (f32[2,24,4096]{2,1,0:T(8,128)S(1)}, f32[2,24,4096]{2,1,0:T(8,128)S(1)}, u32[]{:S(2)}, u32[]{:S(2)}) collective-permute-start(f32[2,24,4096]{2,1,0:T(8,128)S(1)} %get-tuple-element.37), channel_id=1, source_target_pairs={{0,32},{1,33},{2,34},{3,35},{4,36},{5,37},{6,38},{7,39},{8,40},{9,... | collective-permute-start | bytes 2359304 | tf_op jit(solution)/shard_map/ppermute | solution.py:27
  66.7 7.8 %collective-permute-start.11 = (f32[1,128]{1,0:T(1,128)S(1)}, f32[1,128]{1,0:T(1,128)S(1)}, u32[]{:S(2)}, u32[]{:S(2)}) collective-permute-start(f32[1,128]{1,0:T(1,128)S(1)} %get-tuple-element.43.refs_4_), channel_id=1, source_target_pairs={{0,32},{1,33},{2,34},{3,35},{4,36},{5,37},{6,38},{7,39},{8,40},{9,... | collective-permute-start | bytes 1544 | tf_op jit(solution)/shard_map/ppermute | solution.py:27
